TPU v7x, 32 devices: a whole 2x2x4 slice. The times are simulated.
32 devices in a mesh: pb: 4 (over z), ka: 4 (over y, core), ha: 2 (over x).
Axes of the slice: x: 2, y: 2, z: 4, core: 2. Of those that a mesh axis runs over, the one named last changes fastest.
Arguments:
- queries: bfloat16 [4096, 4096], P('pb', 'ha'), may hold values from -512 to 512
- keys: bfloat16 [8, 4, 128, 512], P('pb', 'ka', None, 'ha'), may hold values from -6 to 6
- values: bfloat16 [8, 4, 128, 512], P('pb', 'ka', None, 'ha'), may hold values from -6 to 6
- q_order: int32 [32], P('pb'), may hold values from 0 to 31, as said below
- block_mask: int32 [32, 32], P('pb'), may hold values from 0 to 1, as said below
Outputs:
- attended: bfloat16 [4096, 4096], P(('pb', 'ka'), 'ha')
Inputs may be any that keep to these rules, and one draw needn't show every extreme that they name: `q_order`: slots 2m and 2m+1 hold query blocks i and 31 - i for some i, in either order; every block sits in exactly one slot. block_mask[s, b] is 1 only where b <= q_order[s], and block_mask[s, q_order[s]] is 1. For every m and every r below 4, slots 2m and 2m+1 together list at most 4 key blocks b with b % 4 == r, and exactly 4 for some m and r in every draw.
All inputs are finite; a program needn't handle non-finite values.
Results may differ from a plain program's by a relative error of at most 0.0042.
Values may be sent and summed in bfloat16 or wider, within the bound.
No kernel may reach another device: no remote copies, remote signals or barrier semaphores. Data moves between devices by JAX's collectives and lax.ppermute only.
A program may use at most 128 MiB of HBM per device.

v0:
```python
import functools
import math

import jax
import jax.numpy as jnp
from jax import lax
from jax.sharding import PartitionSpec as P

HEAD_DIM = 128


masked_score = -1e30


def compact(listed, entry_count):
    running = jnp.cumsum(listed, axis=1)
    span_size = listed.shape[1]
    ranks = jnp.arange(entry_count, dtype=jnp.int32)
    picked = (listed[:, None, :] == 1) & (running[:, None, :] == ranks[None, :, None] + 1)
    places = jnp.arange(span_size, dtype=jnp.int32)
    position = jnp.sum(jnp.where(picked, places[None, None, :], 0), axis=2)
    living = jnp.any(picked, axis=2)
    return (position, living)


def unit_scores(key_pool, query_unit, pool_index, owners, living, global_block, query_blocks):
    head_width = query_unit.shape[-1]
    block_rows = query_unit.shape[1]
    query_rows = jnp.take(query_unit, owners, axis=0)
    key_rows = jnp.take(key_pool, pool_index, axis=0)
    scores = jnp.einsum(
        "eigxd,ejgd->egxij", query_rows, key_rows, preferred_element_type=jnp.float32
    )
    scores = scores * (1.0 / math.sqrt(head_width))
    diagonal = global_block == jnp.take(query_blocks, owners, axis=0)
    causal = jnp.arange(block_rows)[:, None] >= jnp.arange(block_rows)[None, :]
    allowed = living[:, None, None, None, None] & (
        jnp.logical_not(diagonal)[:, None, None, None, None] | causal[None, None, None]
    )
    return (jnp.where(allowed, scores, masked_score), allowed)


def unit_peak(key_pool, unit_args):
    query_unit, pool_index, owners, living, global_block, query_blocks = unit_args
    scores, allowed = unit_scores(
        key_pool, query_unit, pool_index, owners, living, global_block, query_blocks
    )
    row_peak = jnp.max(scores, axis=4)
    belongs = owners[:, None] == jnp.arange(query_unit.shape[0])[None, :]
    return jnp.max(
        jnp.where(belongs[:, :, None, None, None], row_peak[:, None], masked_score), axis=0
    )


def unit_sums(key_pool, value_pool, unit_args):
    query_unit, pool_index, owners, living, global_block, query_blocks, row_tops = unit_args
    scores, allowed = unit_scores(
        key_pool, query_unit, pool_index, owners, living, global_block, query_blocks
    )
    top_rows = jnp.take(row_tops, owners, axis=0)
    weights = jnp.where(allowed, jnp.exp(scores - top_rows[..., None]), 0.0)
    value_rows = jnp.take(value_pool, pool_index, axis=0)
    partial_sum = jnp.einsum(
        "egxij,ejgd->eigxd",
        weights.astype(jnp.bfloat16),
        value_rows,
        preferred_element_type=jnp.float32,
    )
    belongs = (owners[:, None] == jnp.arange(query_unit.shape[0])[None, :]).astype(jnp.float32)
    numerator = jnp.einsum("es,eigxd->sigxd", belongs, partial_sum, precision=lax.Precision.HIGHEST)
    denominator = jnp.einsum("es,egxij->sigx", belongs, weights, precision=lax.Precision.HIGHEST)
    return (numerator, denominator)


def on_device(queries, keys, values, q_order, block_mask):
    head_width = HEAD_DIM
    block_rows = keys.shape[2]
    kv_local = keys.shape[3] // head_width
    q_local = queries.shape[1] // head_width
    group_size = q_local // kv_local
    slot_count = queries.shape[0] // block_rows
    residues = lax.axis_size("ka")
    key_index = lax.axis_index("ka")
    near_keys, near_values = (
        lax.all_gather(keys, "pb", axis=0, tiled=True),
        lax.all_gather(values, "pb", axis=0, tiled=True),
    )
    class_blocks = near_keys.shape[0]
    pair_cap = class_blocks // 2
    queried = queries.reshape(slot_count, block_rows, kv_local, group_size, head_width)
    whole_keys, whole_values = (
        lax.all_gather(near_keys, "ka", axis=1, tiled=True),
        lax.all_gather(near_values, "ka", axis=1, tiled=True),
    )
    block_total = class_blocks * residues
    key_pool = whole_keys.reshape(block_total, block_rows, kv_local, head_width)
    value_pool = whole_values.reshape(block_total, block_rows, kv_local, head_width)
    own_slots = slot_count // residues
    first_slot = key_index * own_slots
    own_queries = lax.dynamic_slice_in_dim(queried, first_slot, own_slots, 0)
    own_listed = lax.dynamic_slice_in_dim(block_mask, first_slot, own_slots, 0)
    own_blocks = lax.dynamic_slice_in_dim(q_order, first_slot, own_slots, 0)
    position, living = compact(own_listed, pair_cap * residues)
    unit_total = own_slots * residues
    pool_index = position.reshape(unit_total, pair_cap)
    living = living.reshape(unit_total, pair_cap)
    owners = jnp.zeros((unit_total, pair_cap), jnp.int32)
    query_units = jnp.repeat(own_queries[:, None], residues, axis=1).reshape(
        unit_total, 1, block_rows, kv_local, group_size, head_width
    )
    query_blocks = jnp.repeat(own_blocks, residues).reshape(unit_total, 1)
    unit_args = (query_units, pool_index, owners, living, pool_index, query_blocks)
    row_tops = lax.map(functools.partial(unit_peak, key_pool), unit_args)
    row_tops = jnp.max(
        row_tops.reshape(own_slots, residues, kv_local, group_size, block_rows), axis=1
    )
    row_tops = jnp.repeat(row_tops, residues, axis=0).reshape(
        unit_total, 1, kv_local, group_size, block_rows
    )
    numerator, denominator = lax.map(
        functools.partial(unit_sums, key_pool, value_pool), unit_args + (row_tops,)
    )
    numerator = jnp.sum(
        numerator.reshape(own_slots, residues, block_rows, kv_local, group_size, head_width), axis=1
    )
    numerator = numerator.reshape(own_slots * block_rows, q_local * head_width)
    denominator = jnp.sum(
        denominator.reshape(own_slots, residues, block_rows, kv_local, group_size), axis=1
    )
    denominator = denominator.reshape(own_slots * block_rows, q_local)
    attended = numerator.reshape(-1, q_local, head_width) / denominator[:, :, None]
    return attended.astype(jnp.bfloat16).reshape(-1, q_local * head_width)


def solution(mesh):
    in_specs = (
        P("pb", "ha"),
        P("pb", "ka", None, "ha"),
        P("pb", "ka", None, "ha"),
        P("pb"),
        P("pb", None),
    )
    out_specs = P(("pb", "ka"), "ha")
    return jax.shard_map(
        on_device, mesh=mesh, in_specs=in_specs, out_specs=out_specs, check_vma=False
    )
```

profile of v0, /device:TPU:27, one launch (start us, length us, event | category | flops | bytes accessed | tf_op | source)
XLA Modules:
  0.0 306.3 jit_solution(17527718883726945055)
XLA Ops:
  6.5 13.7 %all_gather.14 = bf16[8,1,128,256]{3,2,1,0:T(8,128)(2,1)} all-gather(bf16[2,1,128,256]{3,2,1,0:T(8,128)(2,1)} %param.16), channel_id=1, replica_groups=mesh['pb'=4,'ka'=4,'ha'=2] {'pb'}, dimensions={0}, use_global_device_ids=true | all-gather | bytes 655360 | tf_op jit(solution)/shard_map/all_gather | solution.py:85
  20.3 14.4 %all_gather.12 = bf16[8,1,128,256]{3,2,1,0:T(8,128)(2,1)} all-gather(bf16[2,1,128,256]{3,2,1,0:T(8,128)(2,1)} %param.17), channel_id=1, replica_groups=mesh['pb'=4,'ka'=4,'ha'=2] {'pb'}, dimensions={0}, use_global_device_ids=true | all-gather | bytes 655360 | tf_op jit(solution)/shard_map/all_gather | solution.py:86
  37.2 3.6 %copy.43 = bf16[128,8,16,128]{3,2,1,0:T(8,128)(2,1)S(1)} copy(bf16[128,8,16,128]{3,1,2,0:T(8,128)(2,1)} %bitcast.148) | data formatting | bytes 8388608
  41.3 6.0 %all-gather.5.cloned.1.call-done = bf16[8,4,128,256]{3,2,1,0:T(8,128)(2,1)} async-done(((bf16[8,1,128,256]{3,2,1,0:T(8,128)(2,1)}), bf16[8,4,128,256]{3,2,1,0:T(8,128)(2,1)}) %all-gather.5.cloned.1.call-update) | async-done | bytes 2097168 | tf_op jit(solution)/shard_map/all_gather | solution.py:92
  47.3 2.5 reshape.123
  49.8 3.0 broadcast_in_dim.130
  52.8 37.9 %while.22 = (s32[]{:T(128)}, f32[8,1,2,8,128]{4,3,2,1,0:T(8,128)S(1)}, pred[8,4]{1,0:T(8,128)(4,1)S(1)}, s32[8,4]{1,0:T(8,128)S(1)}, s32[8,1]{0,1:T(1,128)S(1)},...) while((s32[]{:T(128)}, ...), condition=%wide.region_5.9_spmd, body=%wide.region_3.8_spmd.sunk | while | flops 271858720 | bytes 3076313 | solution.py:113
  90.8 4.0 %reshape.121 = bf16[32,128,2,128]{3,2,1,0:T(2,128)(2,1)} reshape(bf16[8,4,128,256]{3,2,1,0:T(8,128)(2,1)} %all-gather.3.cloned.1.call-done) | data formatting | bytes 4194304 | tf_op jit(solution)/shard_map/reshape | solution.py:97
  94.8 194.8 %while.23 = (s32[]{:T(128)}, f32[8,1,128,2,8,128]{5,4,3,2,1,0:T(8,128)}, f32[8,1,128,2,8]{2,4,3,1,0:T(8,128)S(1)}, s32[8,4]{1,0:T(8,128)S(1)}, bf16[32,128,2,128...) while((s32[]{:T(128)}, ...), condition=%wide.region_9.13_spmd, body=%wide.region_7.12_spmd.sunk | while | flops 560440320 | bytes 32862472 | solution.py:120
  97.3 2.7 gather_fusion.1
  101.6 1.4 fusion.61
  103.0 3.2 %convolution_bitcast_fusion.2 = f32[4,128,2,8,128]{1,4,3,2,0:T(8,128)} fusion(f32[4,2,128,128,8]{3,2,4,1,0:T(8,128)S(1)} %get-tuple-element.268, f32[2,8,128]{2,1,0:T(8,128)S(1)} %dynamic-slice_bitcast_fusion.12, pred[4,128,128]{1,2,0:T(8,128)(4,1)S(1)} %or_and_fusion.5, bf16[4,128,2,128,1]{3,2,1,0,4:T(2,128)(2,1)S(1)} %get-tuple-element.269), kind=kOutput, calls=%fused_computation.27.clone.1 | convolution fusion | flops 273678336 | bytes 8724480 | tf_op jit(solution)/shard_map/while/body/eval_jaxpr/egxij,ejgd->eigxd/dot_general | solution.py:63
  106.2 5.5 %copy.70 = f32[4,128,2,8,128]{4,0,3,2,1:T(4,128)} copy(f32[4,128,2,8,128]{1,4,3,2,0:T(8,128)} %convolution_bitcast_fusion.2) | data formatting | bytes 8388608 | tf_op jit(solution)/shard_map/while/body/eval_jaxpr/egxij,ejgd->eigxd/transpose | solution.py:63
  111.7 6.3 %fusion.62 = f32[1,128,2,8,128]{4,0,3,2,1:T(1,128)S(1)} fusion(f32[4,128,2,8,128]{4,0,3,2,1:T(4,128)} %copy.70), kind=kOutput, calls=%fused_computation.57.clone.1 | convolution fusion | flops 12582912 | bytes 5242880 | tf_op jit(solution)/shard_map/while/body/eval_jaxpr/es,eigxd->sigxd/dot_general | solution.py:70
  121.7 2.7 gather_fusion.1
  126.0 1.4 fusion.61
  127.4 3.2 %convolution_bitcast_fusion.2 = f32[4,128,2,8,128]{1,4,3,2,0:T(8,128)} fusion(f32[4,2,128,128,8]{3,2,4,1,0:T(8,128)S(1)} %get-tuple-element.268, f32[2,8,128]{2,1,0:T(8,128)S(1)} %dynamic-slice_bitcast_fusion.12, pred[4,128,128]{1,2,0:T(8,128)(4,1)S(1)} %or_and_fusion.5, bf16[4,128,2,128,1]{3,2,1,0,4:T(2,128)(2,1)S(1)} %get-tuple-element.269), kind=kOutput, calls=%fused_computation.27.clone.1 | convolution fusion | flops 273678336 | bytes 8724480 | tf_op jit(solution)/shard_map/while/body/eval_jaxpr/egxij,ejgd->eigxd/dot_general | solution.py:63
  130.5 5.5 %copy.70 = f32[4,128,2,8,128]{4,0,3,2,1:T(4,128)} copy(f32[4,128,2,8,128]{1,4,3,2,0:T(8,128)} %convolution_bitcast_fusion.2) | data formatting | bytes 8388608 | tf_op jit(solution)/shard_map/while/body/eval_jaxpr/egxij,ejgd->eigxd/transpose | solution.py:63
  136.0 6.3 %fusion.62 = f32[1,128,2,8,128]{4,0,3,2,1:T(1,128)S(1)} fusion(f32[4,128,2,8,128]{4,0,3,2,1:T(4,128)} %copy.70), kind=kOutput, calls=%fused_computation.57.clone.1 | convolution fusion | flops 12582912 | bytes 5242880 | tf_op jit(solution)/shard_map/while/body/eval_jaxpr/es,eigxd->sigxd/dot_general | solution.py:70
  146.1 2.7 gather_fusion.1
  150.4 1.3 fusion.61
  151.7 3.2 %convolution_bitcast_fusion.2 = f32[4,128,2,8,128]{1,4,3,2,0:T(8,128)} fusion(f32[4,2,128,128,8]{3,2,4,1,0:T(8,128)S(1)} %get-tuple-element.268, f32[2,8,128]{2,1,0:T(8,128)S(1)} %dynamic-slice_bitcast_fusion.12, pred[4,128,128]{1,2,0:T(8,128)(4,1)S(1)} %or_and_fusion.5, bf16[4,128,2,128,1]{3,2,1,0,4:T(2,128)(2,1)S(1)} %get-tuple-element.269), kind=kOutput, calls=%fused_computation.27.clone.1 | convolution fusion | flops 273678336 | bytes 8724480 | tf_op jit(solution)/shard_map/while/body/eval_jaxpr/egxij,ejgd->eigxd/dot_general | solution.py:63
  154.9 5.5 %copy.70 = f32[4,128,2,8,128]{4,0,3,2,1:T(4,128)} copy(f32[4,128,2,8,128]{1,4,3,2,0:T(8,128)} %convolution_bitcast_fusion.2) | data formatting | bytes 8388608 | tf_op jit(solution)/shard_map/while/body/eval_jaxpr/egxij,ejgd->eigxd/transpose | solution.py:63
  160.4 6.3 %fusion.62 = f32[1,128,2,8,128]{4,0,3,2,1:T(1,128)S(1)} fusion(f32[4,128,2,8,128]{4,0,3,2,1:T(4,128)} %copy.70), kind=kOutput, calls=%fused_computation.57.clone.1 | convolution fusion | flops 12582912 | bytes 5242880 | tf_op jit(solution)/shard_map/while/body/eval_jaxpr/es,eigxd->sigxd/dot_general | solution.py:70
  170.4 2.7 gather_fusion.1
  176.1 3.2 %convolution_bitcast_fusion.2 = f32[4,128,2,8,128]{1,4,3,2,0:T(8,128)} fusion(f32[4,2,128,128,8]{3,2,4,1,0:T(8,128)S(1)} %get-tuple-element.268, f32[2,8,128]{2,1,0:T(8,128)S(1)} %dynamic-slice_bitcast_fusion.12, pred[4,128,128]{1,2,0:T(8,128)(4,1)S(1)} %or_and_fusion.5, bf16[4,128,2,128,1]{3,2,1,0,4:T(2,128)(2,1)S(1)} %get-tuple-element.269), kind=kOutput, calls=%fused_computation.27.clone.1 | convolution fusion | flops 273678336 | bytes 8724480 | tf_op jit(solution)/shard_map/while/body/eval_jaxpr/egxij,ejgd->eigxd/dot_general | solution.py:63
  179.3 5.5 %copy.70 = f32[4,128,2,8,128]{4,0,3,2,1:T(4,128)} copy(f32[4,128,2,8,128]{1,4,3,2,0:T(8,128)} %convolution_bitcast_fusion.2) | data formatting | bytes 8388608 | tf_op jit(solution)/shard_map/while/body/eval_jaxpr/egxij,ejgd->eigxd/transpose | solution.py:63
  184.7 6.3 %fusion.62 = f32[1,128,2,8,128]{4,0,3,2,1:T(1,128)S(1)} fusion(f32[4,128,2,8,128]{4,0,3,2,1:T(4,128)} %copy.70), kind=kOutput, calls=%fused_computation.57.clone.1 | convolution fusion | flops 12582912 | bytes 5242880 | tf_op jit(solution)/shard_map/while/body/eval_jaxpr/es,eigxd->sigxd/dot_general | solution.py:70
  194.8 2.7 gather_fusion.1
  199.0 1.4 fusion.61
  200.4 3.2 %convolution_bitcast_fusion.2 = f32[4,128,2,8,128]{1,4,3,2,0:T(8,128)} fusion(f32[4,2,128,128,8]{3,2,4,1,0:T(8,128)S(1)} %get-tuple-element.268, f32[2,8,128]{2,1,0:T(8,128)S(1)} %dynamic-slice_bitcast_fusion.12, pred[4,128,128]{1,2,0:T(8,128)(4,1)S(1)} %or_and_fusion.5, bf16[4,128,2,128,1]{3,2,1,0,4:T(2,128)(2,1)S(1)} %get-tuple-element.269), kind=kOutput, calls=%fused_computation.27.clone.1 | convolution fusion | flops 273678336 | bytes 8724480 | tf_op jit(solution)/shard_map/while/body/eval_jaxpr/egxij,ejgd->eigxd/dot_general | solution.py:63
  203.6 5.5 %copy.70 = f32[4,128,2,8,128]{4,0,3,2,1:T(4,128)} copy(f32[4,128,2,8,128]{1,4,3,2,0:T(8,128)} %convolution_bitcast_fusion.2) | data formatting | bytes 8388608 | tf_op jit(solution)/shard_map/while/body/eval_jaxpr/egxij,ejgd->eigxd/transpose | solution.py:63
  209.1 6.3 %fusion.62 = f32[1,128,2,8,128]{4,0,3,2,1:T(1,128)S(1)} fusion(f32[4,128,2,8,128]{4,0,3,2,1:T(4,128)} %copy.70), kind=kOutput, calls=%fused_computation.57.clone.1 | convolution fusion | flops 12582912 | bytes 5242880 | tf_op jit(solution)/shard_map/while/body/eval_jaxpr/es,eigxd->sigxd/dot_general | solution.py:70
  219.1 2.7 gather_fusion.1
  224.7 3.2 %convolution_bitcast_fusion.2 = f32[4,128,2,8,128]{1,4,3,2,0:T(8,128)} fusion(f32[4,2,128,128,8]{3,2,4,1,0:T(8,128)S(1)} %get-tuple-element.268, f32[2,8,128]{2,1,0:T(8,128)S(1)} %dynamic-slice_bitcast_fusion.12, pred[4,128,128]{1,2,0:T(8,128)(4,1)S(1)} %or_and_fusion.5, bf16[4,128,2,128,1]{3,2,1,0,4:T(2,128)(2,1)S(1)} %get-tuple-element.269), kind=kOutput, calls=%fused_computation.27.clone.1 | convolution fusion | flops 273678336 | bytes 8724480 | tf_op jit(solution)/shard_map/while/body/eval_jaxpr/egxij,ejgd->eigxd/dot_general | solution.py:63
  227.9 5.5 %copy.70 = f32[4,128,2,8,128]{4,0,3,2,1:T(4,128)} copy(f32[4,128,2,8,128]{1,4,3,2,0:T(8,128)} %convolution_bitcast_fusion.2) | data formatting | bytes 8388608 | tf_op jit(solution)/shard_map/while/body/eval_jaxpr/egxij,ejgd->eigxd/transpose | solution.py:63
  233.4 6.3 %fusion.62 = f32[1,128,2,8,128]{4,0,3,2,1:T(1,128)S(1)} fusion(f32[4,128,2,8,128]{4,0,3,2,1:T(4,128)} %copy.70), kind=kOutput, calls=%fused_computation.57.clone.1 | convolution fusion | flops 12582912 | bytes 5242880 | tf_op jit(solution)/shard_map/while/body/eval_jaxpr/es,eigxd->sigxd/dot_general | solution.py:70
  243.4 2.7 gather_fusion.1
  249.1 3.2 %convolution_bitcast_fusion.2 = f32[4,128,2,8,128]{1,4,3,2,0:T(8,128)} fusion(f32[4,2,128,128,8]{3,2,4,1,0:T(8,128)S(1)} %get-tuple-element.268, f32[2,8,128]{2,1,0:T(8,128)S(1)} %dynamic-slice_bitcast_fusion.12, pred[4,128,128]{1,2,0:T(8,128)(4,1)S(1)} %or_and_fusion.5, bf16[4,128,2,128,1]{3,2,1,0,4:T(2,128)(2,1)S(1)} %get-tuple-element.269), kind=kOutput, calls=%fused_computation.27.clone.1 | convolution fusion | flops 273678336 | bytes 8724480 | tf_op jit(solution)/shard_map/while/body/eval_jaxpr/egxij,ejgd->eigxd/dot_general | solution.py:63
  252.3 5.5 %copy.70 = f32[4,128,2,8,128]{4,0,3,2,1:T(4,128)} copy(f32[4,128,2,8,128]{1,4,3,2,0:T(8,128)} %convolution_bitcast_fusion.2) | data formatting | bytes 8388608 | tf_op jit(solution)/shard_map/while/body/eval_jaxpr/egxij,ejgd->eigxd/transpose | solution.py:63
  257.8 6.3 %fusion.62 = f32[1,128,2,8,128]{4,0,3,2,1:T(1,128)S(1)} fusion(f32[4,128,2,8,128]{4,0,3,2,1:T(4,128)} %copy.70), kind=kOutput, calls=%fused_computation.57.clone.1 | convolution fusion | flops 12582912 | bytes 5242880 | tf_op jit(solution)/shard_map/while/body/eval_jaxpr/es,eigxd->sigxd/dot_general | solution.py:70
  267.8 2.7 gather_fusion.1
  273.5 3.2 %convolution_bitcast_fusion.2 = f32[4,128,2,8,128]{1,4,3,2,0:T(8,128)} fusion(f32[4,2,128,128,8]{3,2,4,1,0:T(8,128)S(1)} %get-tuple-element.268, f32[2,8,128]{2,1,0:T(8,128)S(1)} %dynamic-slice_bitcast_fusion.12, pred[4,128,128]{1,2,0:T(8,128)(4,1)S(1)} %or_and_fusion.5, bf16[4,128,2,128,1]{3,2,1,0,4:T(2,128)(2,1)S(1)} %get-tuple-element.269), kind=kOutput, calls=%fused_computation.27.clone.1 | convolution fusion | flops 273678336 | bytes 8724480 | tf_op jit(solution)/shard_map/while/body/eval_jaxpr/egxij,ejgd->eigxd/dot_general | solution.py:63
  276.6 5.5 %copy.70 = f32[4,128,2,8,128]{4,0,3,2,1:T(4,128)} copy(f32[4,128,2,8,128]{1,4,3,2,0:T(8,128)} %convolution_bitcast_fusion.2) | data formatting | bytes 8388608 | tf_op jit(solution)/shard_map/while/body/eval_jaxpr/egxij,ejgd->eigxd/transpose | solution.py:63
  282.1 6.3 %fusion.62 = f32[1,128,2,8,128]{4,0,3,2,1:T(1,128)S(1)} fusion(f32[4,128,2,8,128]{4,0,3,2,1:T(4,128)} %copy.70), kind=kOutput, calls=%fused_computation.57.clone.1 | convolution fusion | flops 12582912 | bytes 5242880 | tf_op jit(solution)/shard_map/while/body/eval_jaxpr/es,eigxd->sigxd/dot_general | solution.py:70
  289.7 4.2 %bitcast_reduce_fusion = f32[2,128,2,8,128]{4,3,2,1,0:T(8,128)S(1)} fusion(f32[2,4,128,2,8,128]{5,4,3,2,1,0:T(8,128)} %bitcast.145), kind=kLoop, calls=%fused_computation.65 | loop fusion | flops 1572864 | bytes 10485760 | tf_op jit(solution)/shard_map/reduce_sum | solution.py:123
  293.9 1.5 reshape_reshape.15
  296.1 3.4 %fusion.33 = bf16[256,2048]{1,0:T(8,128)(2,1)} fusion(f32[256,2048]{1,0:T(8,128)} %reshape_reshape.15, f32[32,8,16,128]{3,2,1,0:T(8,128)S(1)} %bitcast.146), kind=kLoop, calls=%fused_computation.67 | loop fusion | flops 1048576 | bytes 5242880 | tf_op jit(solution)/shard_map/convert_element_type | solution.py:132
  (223 shorter events, 88.6 us)
Async XLA Ops:
  6.5 40.7 %all-gather.5.cloned.1.call-start = ((), (), s32[]{:S(2)}) async-start(), calls=%async_computation.1 | async-start | bytes 2621440 | tf_op jit(solution)/shard_map/all_gather | solution.py:92
  20.3 70.5 %all-gather.3.cloned.1.call-start = ((), (), s32[]{:S(2)}) async-start(), calls=%async_computation | async-start | bytes 2621440 | tf_op jit(solution)/shard_map/all_gather | solution.py:93
Sparse Core Ops, SparseCore 0:
  20.4 26.8 all-gather.4
  48.8 22.5 all-gather.2
where the time goes:
time: 311 us; the launch traced here: 306 us
  local copies, waits for them, and re-layouts  136 us (44%)
  matrix products  93.6 us (30%)
  blocking collectives  28.2 us (9%)
  other arithmetic  27.9 us (9%)
  between operations  13.5 us (4%)
  waiting for transfers between devices  6.06 us (2%)
    dot_general x8, matrix products, unit_sums(): jnp.einsum('es,eigxd->sigxd', belongs, partial_sum, precision=lax.Precisi...  50.3 us
    transpose x8, local copies, waits for them, and re-layouts, unit_sums(): jnp.einsum('egxij,ejgd->eigxd', weights.astype(jnp.bfloat16), value_rows,...  43.9 us
    dot_general x8, matrix products, unit_sums(): jnp.einsum('egxij,ejgd->eigxd', weights.astype(jnp.bfloat16), value_rows,...  25.5 us
    gather x8, local copies, waits for them, and re-layouts, unit_sums(): value_rows = jnp.take(value_pool, pool_index, axis=0)  21.3 us
    gather x16, local copies, waits for them, and re-layouts, unit_scores(): query_rows = jnp.take(query_unit, owners, axis=0)  17.4 us
    gather x16, local copies, waits for them, and re-layouts, unit_scores(): key_rows = jnp.take(key_pool, pool_index, axis=0)  17.2 us
    dot_general x16, matrix products, unit_scores(): jnp.einsum('eigxd,ejgd->egxij', query_rows, key_rows, preferred_element_t...  16.6 us
    all_gather x1, blocking collectives, on_device(): lax.all_gather(values, 'pb', axis=0, tiled=True)  14.4 us
  transfers between devices with their start and end apart: 2, of which 1 were waited for; matrix products, arithmetic and copies ran while one was open for 16% of the time, Pallas kernels for 0%

commit v1 on v0

v1 whole, which is shorter than its diff:
```python
import functools
import math

import jax
import jax.numpy as jnp
from jax import lax
from jax.experimental import pallas as pl
from jax.experimental.pallas import tpu as pltpu
from jax.sharding import PartitionSpec as P

HEAD_DIM = 128
HEADS_AT_ONCE = 4
MASKED = -1e30


def shift(array, axis, size, step):
    return lax.ppermute(array, axis, [(i, (i + step) % size) for i in range(size)])


def swap_in_ring(array, axis, size, cores, step, core_step):
    rings = size // cores
    pairs = []
    for ring in range(rings):
        for core in range(cores):
            to = ((ring + step) % rings) * cores + (core + core_step) % cores
            pairs.append((ring * cores + core, to))
    return lax.ppermute(array, axis, pairs)


def attend(
    sizes, order_ref, mask_ref, queries_ref, *refs
):
    pb, ka, cores, sources = sizes
    pieces = refs[: 2 * sources]
    out_ref, q_buf, k_pool, v_pool, scores, listed, sems = refs[2 * sources :]
    blocks_total, block_rows, kv_width = k_pool.shape
    kv_local = kv_width // HEAD_DIM
    group = queries_ref.shape[1] // kv_width
    class_local = pieces[0].shape[0]
    own_slots = q_buf.shape[0] // block_rows
    rings = ka // cores
    p_at, k_at = lax.axis_index("pb"), lax.axis_index("ka")
    ring_at, core_at = k_at // cores, k_at % cores

    copies = []
    q_copy = pltpu.make_async_copy(
        queries_ref.at[pl.ds(pl.multiple_of(k_at * q_buf.shape[0], block_rows), q_buf.shape[0])],
        q_buf,
        sems.at[0],
    )
    q_copy.start()
    copies.append(q_copy)
    index = 0
    for z in range(pb):
        for y in range(rings):
            for c in range(cores):
                source_p = lax.rem(p_at + (pb - z), pb)
                source_ring = lax.rem(ring_at + (rings - y), rings)
                source_core = lax.rem(core_at + (cores - c), cores)
                residue = source_ring * cores + source_core
                for t in range(class_local):
                    block = (source_p * class_local + t) * ka + residue
                    for which, pool in ((0, k_pool), (1, v_pool)):
                        copy = pltpu.make_async_copy(
                            pieces[2 * index + which].at[t, 0],
                            pool.at[block],
                            sems.at[1 + (2 * index + which) * class_local + t],
                        )
                        copy.start()
                        copies.append(copy)
                index += 1

    counts = []
    for s in range(own_slots):
        row = k_at * own_slots + s
        own_block = order_ref[row]
        listed[s, 0] = own_block

        def place(b, count):
            listed[s, count] = b
            return count + jnp.where(b == own_block, 0, mask_ref[row, b])

        counts.append(lax.fori_loop(0, blocks_total, place, 1))

    for copy in copies:
        copy.wait()

    scale = math.log2(math.e) / math.sqrt(HEAD_DIM)
    heads = min(HEADS_AT_ONCE, group)
    rows = heads * block_rows
    row_id = lax.broadcasted_iota(jnp.int32, (block_rows, block_rows), 0)
    col_id = lax.broadcasted_iota(jnp.int32, (block_rows, block_rows), 1)
    causal = jnp.concatenate([col_id <= row_id] * heads, axis=0)

    def dot_t(a, b):
        return lax.dot_general(a, b, (((1,), (1,)), ((), ())), preferred_element_type=jnp.float32)

    for s in range(own_slots):
        count = counts[s]
        odd = lax.rem(count, 2)
        for g in range(kv_local):
            columns = slice(g * HEAD_DIM, (g + 1) * HEAD_DIM)
            for first in range(0, group, heads):
                q_rows = jnp.concatenate(
                    [
                        q_buf[
                            s * block_rows : (s + 1) * block_rows,
                            (g * group + x) * HEAD_DIM : (g * group + x + 1) * HEAD_DIM,
                        ]
                        for x in range(first, first + heads)
                    ],
                    axis=0,
                )

                own = dot_t(q_rows, k_pool[listed[s, 0], :, columns])
                own = jnp.where(causal, own, MASKED)
                scores[0] = own

                def score_pair(u, top):
                    e = 1 + 2 * u
                    keys = jnp.concatenate(
                        [k_pool[listed[s, e], :, columns], k_pool[listed[s, e + 1], :, columns]],
                        axis=0,
                    )
                    pair = dot_t(q_rows, keys)
                    one, two = pair[:, :block_rows], pair[:, block_rows:]
                    scores[e] = one
                    scores[e + 1] = two
                    return jnp.maximum(top, jnp.maximum(one, two))

                pairs = (count - 1) // 2
                top = lax.fori_loop(0, pairs, score_pair, own)

                def score_last(top):
                    last = dot_t(q_rows, k_pool[listed[s, count - 1], :, columns])
                    scores[count - 1] = last
                    return jnp.maximum(top, last)

                top = lax.cond(odd == 0, score_last, lambda top: top, top)
                peak = jnp.max(top, axis=1, keepdims=True)

                def weigh(e):
                    return jnp.exp2((scores[e] - peak) * scale)

                def sum_pair(u, carry):
                    total, numerator = carry
                    e = 2 * u + odd
                    one, two = weigh(e), weigh(e + 1)
                    weights = jnp.concatenate(
                        [one.astype(jnp.bfloat16), two.astype(jnp.bfloat16)], axis=1
                    )
                    rows_v = jnp.concatenate(
                        [v_pool[listed[s, e], :, columns], v_pool[listed[s, e + 1], :, columns]],
                        axis=0,
                    )
                    return (
                        total + (one + two),
                        numerator + jnp.dot(weights, rows_v, preferred_element_type=jnp.float32),
                    )

                def sum_first():
                    one = weigh(0)
                    return one, jnp.dot(
                        one.astype(jnp.bfloat16),
                        v_pool[listed[s, 0], :, columns],
                        preferred_element_type=jnp.float32,
                    )

                zero = jnp.zeros((rows, block_rows), jnp.float32)
                zero_n = jnp.zeros((rows, HEAD_DIM), jnp.float32)
                carry = lax.cond(odd == 1, sum_first, lambda: (zero, zero_n))
                total, numerator = lax.fori_loop(0, count // 2, sum_pair, carry)
                result = numerator / jnp.sum(total, axis=1, keepdims=True)
                result = result.astype(jnp.bfloat16)
                for x in range(heads):
                    head = g * group + first + x
                    out_ref[
                        s * block_rows : (s + 1) * block_rows,
                        head * HEAD_DIM : (head + 1) * HEAD_DIM,
                    ] = result[x * block_rows : (x + 1) * block_rows]


def on_device(queries, keys, values, q_order, block_mask):
    pb, ka = lax.axis_size("pb"), lax.axis_size("ka")
    cores = 2 if ka % 2 == 0 else 1
    rings = ka // cores
    class_local, _, block_rows, kv_width = keys.shape
    block_total = block_mask.shape[1]
    slots = queries.shape[0] // block_rows
    own_slots = slots // ka

    pieces = []
    near = (keys, values)
    for z in range(pb):
        if z:
            near = tuple(shift(array, "pb", pb, 1) for array in near)
        ring = near
        for y in range(rings):
            if y:
                ring = tuple(swap_in_ring(array, "ka", ka, cores, 1, 0) for array in ring)
            here = ring
            for c in range(cores):
                if c:
                    here = tuple(swap_in_ring(array, "ka", ka, cores, 0, 1) for array in here)
                pieces.extend(here)

    sources = pb * ka
    kernel = functools.partial(attend, (pb, ka, cores, sources))
    group = queries.shape[1] // kv_width
    rows = min(HEADS_AT_ONCE, group) * block_rows
    width = queries.shape[1]
    return pl.pallas_call(
        kernel,
        out_shape=jax.ShapeDtypeStruct((own_slots * block_rows, width), jnp.bfloat16),
        in_specs=[pl.BlockSpec(memory_space=pltpu.SMEM)] * 2
        + [pl.BlockSpec(memory_space=pl.ANY)] * (1 + 2 * sources),
        out_specs=pl.BlockSpec(memory_space=pltpu.VMEM),
        scratch_shapes=[
            pltpu.VMEM((own_slots * block_rows, width), jnp.bfloat16),
            pltpu.VMEM((block_total, block_rows, kv_width), jnp.bfloat16),
            pltpu.VMEM((block_total, block_rows, kv_width), jnp.bfloat16),
            pltpu.VMEM((block_total // 2, rows, block_rows), jnp.float32),
            pltpu.SMEM((own_slots, block_total + 1), jnp.int32),
            pltpu.SemaphoreType.DMA((1 + 2 * sources * class_local,)),
        ],
        compiler_params=pltpu.CompilerParams(vmem_limit_bytes=56 * 1024 * 1024),
    )(q_order, block_mask, queries, *pieces)


def solution(mesh):
    in_specs = (
        P("pb", "ha"),
        P("pb", "ka", None, "ha"),
        P("pb", "ka", None, "ha"),
        P("pb"),
        P("pb", None),
    )
    out_specs = P(("pb", "ka"), "ha")
    return jax.shard_map(
        on_device, mesh=mesh, in_specs=in_specs, out_specs=out_specs, check_vma=False
    )
```

time: 311 us -> 62 us (0.20)
  the two profiles are of different devices: /device:TPU:27 before, /device:TPU:0 now
where the time goes in v1:
time: 62 us; the launch traced here: 61.8 us
  waiting for transfers between devices  24.3 us (39%)
  Pallas kernels  21.7 us (35%)
  starting transfers between devices  14.6 us (24%)
  local copies, waits for them, and re-layouts  0.75 us (1%)
    pallas_call x1, Pallas kernels, on_device(): pl.pallas_call(kernel, out_shape=jax.ShapeDtypeStruct((own_slots * block_...  21.7 us
    ppermute x6, waiting for transfers between devices, shift(): lax.ppermute(array, axis, [(i, (i + step) % size) for i in range(size)])  15 us
    ppermute x24, starting transfers between devices, swap_in_ring(): return lax.ppermute(array, axis, pairs)  10.5 us
    ppermute x24, waiting for transfers between devices, swap_in_ring(): return lax.ppermute(array, axis, pairs)  9.3 us
    ppermute x6, starting transfers between devices, shift(): lax.ppermute(array, axis, [(i, (i + step) % size) for i in range(size)])  4.13 us
  transfers between devices with their start and end apart: 30, of which 12 were waited for; matrix products, arithmetic and copies ran while one was open for 0% of the time, Pallas kernels for 0%

profile of v1, /device:TPU:0, one launch (start us, length us, event | category | flops | bytes accessed | tf_op | source)
XLA Modules:
  0.0 61.8 jit_solution(17873507884368959095)
XLA Ops:
  0.0 3.0 %collective-permute-start.2 = (bf16[2,1,128,256]{3,2,1,0:T(8,128)(2,1)}, bf16[2,1,128,256]{3,2,1,0:T(8,128)(2,1)S(1)}, u32[]{:S(2)}, u32[]{:S(2)}) collective-permute-start(bf16[2,1,128,256]{3,2,1,0:T(8,128)(2,1)} %refs_0_.1), channel_id=1, source_target_pairs={{0,4},{2,6},{4,0},{6,2},{1,5},{3,7},{5,1},{7,3},{8,12},{10,14},{12... | collective-permute-start | bytes 393224 | tf_op jit(solution)/shard_map/ppermute | solution.py:27
  3.0 0.0 collective-permute-start
  3.0 1.6 %collective-permute-start.6 = (bf16[2,1,128,256]{3,2,1,0:T(8,128)(2,1)}, bf16[2,1,128,256]{3,2,1,0:T(8,128)(2,1)S(1)}, u32[]{:S(2)}, u32[]{:S(2)}) collective-permute-start(bf16[2,1,128,256]{3,2,1,0:T(8,128)(2,1)} %refs_0_.1), channel_id=1, source_target_pairs={{0,8},{8,16},{16,24},{24,0},{1,9},{9,17},{17,25},{25,1},{2,10},{10... | collective-permute-start | bytes 393224 | tf_op jit(solution)/shard_map/ppermute | solution.py:17
  4.5 0.5 collective-permute-start.3
  5.1 0.0 collective-permute-start.1
  5.1 1.6 %collective-permute-done.2.refs_4_ = bf16[2,1,128,256]{3,2,1,0:T(8,128)(2,1)S(1)} collective-permute-done((bf16[2,1,128,256]{3,2,1,0:T(8,128)(2,1)}, bf16[2,1,128,256]{3,2,1,0:T(8,128)(2,1)S(1)}, u32[]{:S(2)}, u32[]{:S(2)}) %collective-permute-start.2) | collective-permute-done | bytes 131104 | tf_op jit(solution)/shard_map/ppermute | solution.py:27
  6.7 1.8 %collective-permute-start.7 = (bf16[2,1,128,256]{3,2,1,0:T(8,128)(2,1)}, bf16[2,1,128,256]{3,2,1,0:T(8,128)(2,1)S(1)}, u32[]{:S(2)}, u32[]{:S(2)}) collective-permute-start(bf16[2,1,128,256]{3,2,1,0:T(8,128)(2,1)} %refs_1_.1), channel_id=1, source_target_pairs={{0,8},{8,16},{16,24},{24,0},{1,9},{9,17},{17,25},{25,1},{2,10},{10... | collective-permute-start | bytes 393224 | tf_op jit(solution)/shard_map/ppermute | solution.py:17
  8.5 0.0 collective-permute-start.4
  8.5 2.8 %collective-permute-done.6.refs_8_ = bf16[2,1,128,256]{3,2,1,0:T(8,128)(2,1)S(1)} collective-permute-done((bf16[2,1,128,256]{3,2,1,0:T(8,128)(2,1)}, bf16[2,1,128,256]{3,2,1,0:T(8,128)(2,1)S(1)}, u32[]{:S(2)}, u32[]{:S(2)}) %collective-permute-start.6) | collective-permute-done | bytes 131104 | tf_op jit(solution)/shard_map/ppermute | solution.py:17
  11.3 0.7 %collective-permute-start.10 = (bf16[2,1,128,256]{3,2,1,0:T(8,128)(2,1)S(1)}, bf16[2,1,128,256]{3,2,1,0:T(8,128)(2,1)S(1)}, u32[]{:S(2)}, u32[]{:S(2)}) collective-permute-start(bf16[2,1,128,256]{3,2,1,0:T(8,128)(2,1)S(1)} %collective-permute-done.6.refs_8_), channel_id=1, source_target_pairs={{0,4},{2,6},{4,0},{6,2},{1,5},{3,7},{5,1},{7,3},{8,12},{10,14},{12... | collective-permute-start | bytes 393224 | tf_op jit(solution)/shard_map/ppermute | solution.py:27
  11.9 0.0 collective-permute-done.1.refs_3_
  12.0 0.0 collective-permute-start.8
  12.0 2.3 %collective-permute-done.7.refs_9_ = bf16[2,1,128,256]{3,2,1,0:T(8,128)(2,1)S(1)} collective-permute-done((bf16[2,1,128,256]{3,2,1,0:T(8,128)(2,1)}, bf16[2,1,128,256]{3,2,1,0:T(8,128)(2,1)S(1)}, u32[]{:S(2)}, u32[]{:S(2)}) %collective-permute-start.7) | collective-permute-done | bytes 131104 | tf_op jit(solution)/shard_map/ppermute | solution.py:17
  14.3 0.6 %collective-permute-start.15 = (bf16[2,1,128,256]{3,2,1,0:T(8,128)(2,1)S(1)}, bf16[2,1,128,256]{3,2,1,0:T(8,128)(2,1)S(1)}, u32[]{:S(2)}, u32[]{:S(2)}) collective-permute-start(bf16[2,1,128,256]{3,2,1,0:T(8,128)(2,1)S(1)} %collective-permute-done.7.refs_9_), channel_id=1, source_target_pairs={{0,8},{8,16},{16,24},{24,0},{1,9},{9,17},{17,25},{25,1},{2,10},{10... | collective-permute-start | bytes 393224 | tf_op jit(solution)/shard_map/ppermute | solution.py:17
  14.9 3.1 %collective-permute-done.14.refs_16_ = bf16[2,1,128,256]{3,2,1,0:T(8,128)(2,1)S(1)} collective-permute-done((bf16[2,1,128,256]{3,2,1,0:T(8,128)(2,1)S(1)}, bf16[2,1,128,256]{3,2,1,0:T(8,128)(2,1)S(1)}, u32[]{:S(2)}, u32[]{:S(2)}) %collective-permute-start.14) | collective-permute-done | bytes 131104 | tf_op jit(solution)/shard_map/ppermute | solution.py:17
  18.0 1.1 %collective-permute-start.11 = (bf16[2,1,128,256]{3,2,1,0:T(8,128)(2,1)S(1)}, bf16[2,1,128,256]{3,2,1,0:T(8,128)(2,1)S(1)}, u32[]{:S(2)}, u32[]{:S(2)}) collective-permute-start(bf16[2,1,128,256]{3,2,1,0:T(8,128)(2,1)S(1)} %collective-permute-done.7.refs_9_), channel_id=1, source_target_pairs={{0,4},{2,6},{4,0},{6,2},{1,5},{3,7},{5,1},{7,3},{8,12},{10,14},{12... | collective-permute-start | bytes 393224 | tf_op jit(solution)/shard_map/ppermute | solution.py:27
  19.1 0.0 collective-permute-done.10.refs_12_
  19.1 0.0 collective-permute-start.9
  19.2 0.1 collective-permute-start.22
  19.3 1.0 %collective-permute-start.18 = (bf16[2,1,128,256]{3,2,1,0:T(8,128)(2,1)S(1)}, bf16[2,1,128,256]{3,2,1,0:T(8,128)(2,1)S(1)}, u32[]{:S(2)}, u32[]{:S(2)}) collective-permute-start(bf16[2,1,128,256]{3,2,1,0:T(8,128)(2,1)S(1)} %collective-permute-done.14.refs_16_), channel_id=1, source_target_pairs={{0,4},{2,6},{4,0},{6,2},{1,5},{3,7},{5,1},{7,3},{8,12},{10,14},{12... | collective-permute-start | bytes 393224 | tf_op jit(solution)/shard_map/ppermute | solution.py:27
  20.2 1.7 %collective-permute-done.15.refs_17_ = bf16[2,1,128,256]{3,2,1,0:T(8,128)(2,1)S(1)} collective-permute-done((bf16[2,1,128,256]{3,2,1,0:T(8,128)(2,1)S(1)}, bf16[2,1,128,256]{3,2,1,0:T(8,128)(2,1)S(1)}, u32[]{:S(2)}, u32[]{:S(2)}) %collective-permute-start.15) | collective-permute-done | bytes 131104 | tf_op jit(solution)/shard_map/ppermute | solution.py:17
  22.0 0.0 collective-permute-start.16
  22.0 1.7 %collective-permute-done.11.refs_13_ = bf16[2,1,128,256]{3,2,1,0:T(8,128)(2,1)S(1)} collective-permute-done((bf16[2,1,128,256]{3,2,1,0:T(8,128)(2,1)S(1)}, bf16[2,1,128,256]{3,2,1,0:T(8,128)(2,1)S(1)}, u32[]{:S(2)}, u32[]{:S(2)}) %collective-permute-start.11) | collective-permute-done | bytes 131104 | tf_op jit(solution)/shard_map/ppermute | solution.py:27
  23.7 0.0 collective-permute-start.12
  23.7 0.0 collective-permute-done.9.refs_11_
  23.7 0.1 collective-permute-start.23
  23.8 3.1 %collective-permute-done.22.refs_24_ = bf16[2,1,128,256]{3,2,1,0:T(8,128)(2,1)S(1)} collective-permute-done((bf16[2,1,128,256]{3,2,1,0:T(8,128)(2,1)S(1)}, bf16[2,1,128,256]{3,2,1,0:T(8,128)(2,1)S(1)}, u32[]{:S(2)}, u32[]{:S(2)}) %collective-permute-start.22) | collective-permute-done | bytes 131104 | tf_op jit(solution)/shard_map/ppermute | solution.py:17
  26.9 0.9 %collective-permute-start.19 = (bf16[2,1,128,256]{3,2,1,0:T(8,128)(2,1)S(1)}, bf16[2,1,128,256]{3,2,1,0:T(8,128)(2,1)S(1)}, u32[]{:S(2)}, u32[]{:S(2)}) collective-permute-start(bf16[2,1,128,256]{3,2,1,0:T(8,128)(2,1)S(1)} %collective-permute-done.15.refs_17_), channel_id=1, source_target_pairs={{0,4},{2,6},{4,0},{6,2},{1,5},{3,7},{5,1},{7,3},{8,12},{10,14},{12... | collective-permute-start | bytes 393224 | tf_op jit(solution)/shard_map/ppermute | solution.py:27
  27.8 0.0 collective-permute-start.17
  27.8 0.0 collective-permute-done.16.refs_18_
  27.8 0.5 collective-permute-start.13
  28.3 0.0 collective-permute-done.12.refs_14_
  28.3 1.1 %collective-permute-start.26 = (bf16[2,1,128,256]{3,2,1,0:T(8,128)(2,1)S(1)}, bf16[2,1,128,256]{3,2,1,0:T(8,128)(2,1)S(1)}, u32[]{:S(2)}, u32[]{:S(2)}) collective-permute-start(bf16[2,1,128,256]{3,2,1,0:T(8,128)(2,1)S(1)} %collective-permute-done.22.refs_24_), channel_id=1, source_target_pairs={{0,4},{2,6},{4,0},{6,2},{1,5},{3,7},{5,1},{7,3},{8,12},{10,14},{12... | collective-permute-start | bytes 393224 | tf_op jit(solution)/shard_map/ppermute | solution.py:27
  29.4 2.0 %collective-permute-done.23.refs_25_ = bf16[2,1,128,256]{3,2,1,0:T(8,128)(2,1)S(1)} collective-permute-done((bf16[2,1,128,256]{3,2,1,0:T(8,128)(2,1)S(1)}, bf16[2,1,128,256]{3,2,1,0:T(8,128)(2,1)S(1)}, u32[]{:S(2)}, u32[]{:S(2)}) %collective-permute-start.23) | collective-permute-done | bytes 131104 | tf_op jit(solution)/shard_map/ppermute | solution.py:17
  31.4 1.5 %collective-permute-done.19.refs_21_ = bf16[2,1,128,256]{3,2,1,0:T(8,128)(2,1)S(1)} collective-permute-done((bf16[2,1,128,256]{3,2,1,0:T(8,128)(2,1)S(1)}, bf16[2,1,128,256]{3,2,1,0:T(8,128)(2,1)S(1)}, u32[]{:S(2)}, u32[]{:S(2)}) %collective-permute-start.19) | collective-permute-done | bytes 131104 | tf_op jit(solution)/shard_map/ppermute | solution.py:27
  32.9 0.7 %collective-permute-start.27 = (bf16[2,1,128,256]{3,2,1,0:T(8,128)(2,1)S(1)}, bf16[2,1,128,256]{3,2,1,0:T(8,128)(2,1)S(1)}, u32[]{:S(2)}, u32[]{:S(2)}) collective-permute-start(bf16[2,1,128,256]{3,2,1,0:T(8,128)(2,1)S(1)} %collective-permute-done.23.refs_25_), channel_id=1, source_target_pairs={{0,4},{2,6},{4,0},{6,2},{1,5},{3,7},{5,1},{7,3},{8,12},{10,14},{12... | collective-permute-start | bytes 393224 | tf_op jit(solution)/shard_map/ppermute | solution.py:27
  33.6 0.0 collective-permute-done.17.refs_19_
  33.6 0.0 collective-permute-done.13.refs_15_
  33.6 0.5 collective-permute-start.20
  34.1 0.7 %collective-permute-done.26.refs_28_ = bf16[2,1,128,256]{3,2,1,0:T(8,128)(2,1)S(1)} collective-permute-done((bf16[2,1,128,256]{3,2,1,0:T(8,128)(2,1)S(1)}, bf16[2,1,128,256]{3,2,1,0:T(8,128)(2,1)S(1)}, u32[]{:S(2)}, u32[]{:S(2)}) %collective-permute-start.26) | collective-permute-done | bytes 131104 | tf_op jit(solution)/shard_map/ppermute | solution.py:27
  34.9 0.0 collective-permute-start.21
  34.9 0.5 collective-permute-start.28
  35.4 2.5 %collective-permute-done.27.refs_29_ = bf16[2,1,128,256]{3,2,1,0:T(8,128)(2,1)S(1)} collective-permute-done((bf16[2,1,128,256]{3,2,1,0:T(8,128)(2,1)S(1)}, bf16[2,1,128,256]{3,2,1,0:T(8,128)(2,1)S(1)}, u32[]{:S(2)}, u32[]{:S(2)}) %collective-permute-start.27) | collective-permute-done | bytes 131104 | tf_op jit(solution)/shard_map/ppermute | solution.py:27
  37.9 0.0 collective-permute-done.25.refs_27_
  37.9 0.0 collective-permute-done.21.refs_23_
  37.9 1.3 %collective-permute-done.29.refs_31_ = bf16[2,1,128,256]{3,2,1,0:T(8,128)(2,1)S(1)} collective-permute-done((bf16[2,1,128,256]{3,2,1,0:T(8,128)(2,1)S(1)}, bf16[2,1,128,256]{3,2,1,0:T(8,128)(2,1)S(1)}, u32[]{:S(2)}, u32[]{:S(2)}) %collective-permute-start.29) | collective-permute-done | bytes 131104 | tf_op jit(solution)/shard_map/ppermute | solution.py:27
  39.5 0.6 %copy-done.29 = bf16[2,1,128,256]{3,2,1,0:T(8,128)(2,1)} copy-done((bf16[2,1,128,256]{3,2,1,0:T(8,128)(2,1)}, bf16[2,1,128,256]{3,2,1,0:T(8,128)(2,1)S(1)}, u32[]{:S(2)}) %copy-start.29) | copy-done | bytes 131096
  40.1 21.7 %shard_map.55 = bf16[256,2048]{1,0:T(8,128)(2,1)} custom-call(s32[8]{0:T(128)} %order_ref.1, s32[8,32]{1,0:T(8,128)} %mask_ref.1, bf16[1024,2048]{1,0:T(8,128)(2,1)} %queries_ref.1, bf16[2,1,128,256]{3,2,1,0:T(8,128)(2,1)} %refs_0_.1, bf16[2,1,128,256]{3,2,1,0:T(8,128)(2,1)} %refs_1_.1, bf16[2,1,128,256]{3,2,1,0:T(8,128)(2,1)} %copy-done.1, ...), custom_call_target="tpu_custom_call" | custom-call | tf_op jit(solution)/shard_map/pallas_call | solution.py:212
  (73 shorter events, 0.2 us)
Async XLA Ops:
  0.0 6.7 %collective-permute-start.2 = (bf16[2,1,128,256]{3,2,1,0:T(8,128)(2,1)}, bf16[2,1,128,256]{3,2,1,0:T(8,128)(2,1)S(1)}, u32[]{:S(2)}, u32[]{:S(2)}) collective-permute-start(bf16[2,1,128,256]{3,2,1,0:T(8,128)(2,1)} %refs_0_.1), channel_id=1, source_target_pairs={{0,4},{2,6},{4,0},{6,2},{1,5},{3,7},{5,1},{7,3},{8,12},{10,14},{12... | collective-permute-start | bytes 393224 | tf_op jit(solution)/shard_map/ppermute | solution.py:27
  3.0 5.5 %collective-permute-start = (bf16[2,1,128,256]{3,2,1,0:T(8,128)(2,1)}, bf16[2,1,128,256]{3,2,1,0:T(8,128)(2,1)S(1)}, u32[]{:S(2)}, u32[]{:S(2)}) collective-permute-start(bf16[2,1,128,256]{3,2,1,0:T(8,128)(2,1)} %refs_0_.1), channel_id=1, source_target_pairs={{0,2},{2,0},{4,6},{6,4},{1,3},{3,1},{5,7},{7,5},{8,10},{10,8},{12,... | collective-permute-start | bytes 393224 | tf_op jit(solution)/shard_map/ppermute | solution.py:27
  3.0 8.3 %collective-permute-start.6 = (bf16[2,1,128,256]{3,2,1,0:T(8,128)(2,1)}, bf16[2,1,128,256]{3,2,1,0:T(8,128)(2,1)S(1)}, u32[]{:S(2)}, u32[]{:S(2)}) collective-permute-start(bf16[2,1,128,256]{3,2,1,0:T(8,128)(2,1)} %refs_0_.1), channel_id=1, source_target_pairs={{0,8},{8,16},{16,24},{24,0},{1,9},{9,17},{17,25},{25,1},{2,10},{10... | collective-permute-start | bytes 393224 | tf_op jit(solution)/shard_map/ppermute | solution.py:17
  4.5 6.7 %collective-permute-start.3 = (bf16[2,1,128,256]{3,2,1,0:T(8,128)(2,1)}, bf16[2,1,128,256]{3,2,1,0:T(8,128)(2,1)S(1)}, u32[]{:S(2)}, u32[]{:S(2)}) collective-permute-start(bf16[2,1,128,256]{3,2,1,0:T(8,128)(2,1)} %refs_1_.1), channel_id=1, source_target_pairs={{0,4},{2,6},{4,0},{6,2},{1,5},{3,7},{5,1},{7,3},{8,12},{10,14},{12... | collective-permute-start | bytes 393224 | tf_op jit(solution)/shard_map/ppermute | solution.py:27
  5.1 6.9 %collective-permute-start.1 = (bf16[2,1,128,256]{3,2,1,0:T(8,128)(2,1)}, bf16[2,1,128,256]{3,2,1,0:T(8,128)(2,1)S(1)}, u32[]{:S(2)}, u32[]{:S(2)}) collective-permute-start(bf16[2,1,128,256]{3,2,1,0:T(8,128)(2,1)} %refs_1_.1), channel_id=1, source_target_pairs={{0,2},{2,0},{4,6},{6,4},{1,3},{3,1},{5,7},{7,5},{8,10},{10,8},{12,... | collective-permute-start | bytes 393224 | tf_op jit(solution)/shard_map/ppermute | solution.py:27
  6.7 32.5 %copy-start = (bf16[2,1,128,256]{3,2,1,0:T(8,128)(2,1)}, bf16[2,1,128,256]{3,2,1,0:T(8,128)(2,1)S(1)}, u32[]{:S(2)}) copy-start(bf16[2,1,128,256]{3,2,1,0:T(8,128)(2,1)S(1)} %collective-permute-done.2.refs_4_) | copy-start | bytes 393220
  6.7 7.6 %collective-permute-start.7 = (bf16[2,1,128,256]{3,2,1,0:T(8,128)(2,1)}, bf16[2,1,128,256]{3,2,1,0:T(8,128)(2,1)S(1)}, u32[]{:S(2)}, u32[]{:S(2)}) collective-permute-start(bf16[2,1,128,256]{3,2,1,0:T(8,128)(2,1)} %refs_1_.1), channel_id=1, source_target_pairs={{0,8},{8,16},{16,24},{24,0},{1,9},{9,17},{17,25},{25,1},{2,10},{10... | collective-permute-start | bytes 393224 | tf_op jit(solution)/shard_map/ppermute | solution.py:17
  8.5 30.7 %copy-start.1 = (bf16[2,1,128,256]{3,2,1,0:T(8,128)(2,1)}, bf16[2,1,128,256]{3,2,1,0:T(8,128)(2,1)S(1)}, u32[]{:S(2)}) copy-start(bf16[2,1,128,256]{3,2,1,0:T(8,128)(2,1)S(1)} %collective-permute-done.refs_2_) | copy-start | bytes 393220
  8.5 5.8 %collective-permute-start.4 = (bf16[2,1,128,256]{3,2,1,0:T(8,128)(2,1)S(1)}, bf16[2,1,128,256]{3,2,1,0:T(8,128)(2,1)S(1)}, u32[]{:S(2)}, u32[]{:S(2)}) collective-permute-start(bf16[2,1,128,256]{3,2,1,0:T(8,128)(2,1)S(1)} %collective-permute-done.2.refs_4_), channel_id=1, source_target_pairs={{0,2},{2,0},{4,6},{6,4},{1,3},{3,1},{5,7},{7,5},{8,10},{10,8},{12,... | collective-permute-start | bytes 393224 | tf_op jit(solution)/shard_map/ppermute | solution.py:27
  11.3 28.0 %copy-start.2 = (bf16[2,1,128,256]{3,2,1,0:T(8,128)(2,1)}, bf16[2,1,128,256]{3,2,1,0:T(8,128)(2,1)S(1)}, u32[]{:S(2)}) copy-start(bf16[2,1,128,256]{3,2,1,0:T(8,128)(2,1)S(1)} %collective-permute-done.6.refs_8_) | copy-start | bytes 393220
  11.3 6.8 %collective-permute-start.14 = (bf16[2,1,128,256]{3,2,1,0:T(8,128)(2,1)S(1)}, bf16[2,1,128,256]{3,2,1,0:T(8,128)(2,1)S(1)}, u32[]{:S(2)}, u32[]{:S(2)}) collective-permute-start(bf16[2,1,128,256]{3,2,1,0:T(8,128)(2,1)S(1)} %collective-permute-done.6.refs_8_), channel_id=1, source_target_pairs={{0,8},{8,16},{16,24},{24,0},{1,9},{9,17},{17,25},{25,1},{2,10},{10... | collective-permute-start | bytes 393224 | tf_op jit(solution)/shard_map/ppermute | solution.py:17
  11.3 27.9 %copy-start.3 = (bf16[2,1,128,256]{3,2,1,0:T(8,128)(2,1)}, bf16[2,1,128,256]{3,2,1,0:T(8,128)(2,1)S(1)}, u32[]{:S(2)}) copy-start(bf16[2,1,128,256]{3,2,1,0:T(8,128)(2,1)S(1)} %collective-permute-done.3.refs_5_) | copy-start | bytes 393220
  11.3 7.9 %collective-permute-start.10 = (bf16[2,1,128,256]{3,2,1,0:T(8,128)(2,1)S(1)}, bf16[2,1,128,256]{3,2,1,0:T(8,128)(2,1)S(1)}, u32[]{:S(2)}, u32[]{:S(2)}) collective-permute-start(bf16[2,1,128,256]{3,2,1,0:T(8,128)(2,1)S(1)} %collective-permute-done.6.refs_8_), channel_id=1, source_target_pairs={{0,4},{2,6},{4,0},{6,2},{1,5},{3,7},{5,1},{7,3},{8,12},{10,14},{12... | collective-permute-start | bytes 393224 | tf_op jit(solution)/shard_map/ppermute | solution.py:27
  11.9 27.3 %copy-start.4 = (bf16[2,1,128,256]{3,2,1,0:T(8,128)(2,1)}, bf16[2,1,128,256]{3,2,1,0:T(8,128)(2,1)S(1)}, u32[]{:S(2)}) copy-start(bf16[2,1,128,256]{3,2,1,0:T(8,128)(2,1)S(1)} %collective-permute-done.1.refs_3_) | copy-start | bytes 393220
  12.0 7.2 %collective-permute-start.8 = (bf16[2,1,128,256]{3,2,1,0:T(8,128)(2,1)S(1)}, bf16[2,1,128,256]{3,2,1,0:T(8,128)(2,1)S(1)}, u32[]{:S(2)}, u32[]{:S(2)}) collective-permute-start(bf16[2,1,128,256]{3,2,1,0:T(8,128)(2,1)S(1)} %collective-permute-done.6.refs_8_), channel_id=1, source_target_pairs={{0,2},{2,0},{4,6},{6,4},{1,3},{3,1},{5,7},{7,5},{8,10},{10,8},{12,... | collective-permute-start | bytes 393224 | tf_op jit(solution)/shard_map/ppermute | solution.py:27
  14.3 25.0 %copy-start.5 = (bf16[2,1,128,256]{3,2,1,0:T(8,128)(2,1)}, bf16[2,1,128,256]{3,2,1,0:T(8,128)(2,1)S(1)}, u32[]{:S(2)}) copy-start(bf16[2,1,128,256]{3,2,1,0:T(8,128)(2,1)S(1)} %collective-permute-done.7.refs_9_) | copy-start | bytes 393220
  14.3 5.0 %collective-permute-start.5 = (bf16[2,1,128,256]{3,2,1,0:T(8,128)(2,1)S(1)}, bf16[2,1,128,256]{3,2,1,0:T(8,128)(2,1)S(1)}, u32[]{:S(2)}, u32[]{:S(2)}) collective-permute-start(bf16[2,1,128,256]{3,2,1,0:T(8,128)(2,1)S(1)} %collective-permute-done.3.refs_5_), channel_id=1, source_target_pairs={{0,2},{2,0},{4,6},{6,4},{1,3},{3,1},{5,7},{7,5},{8,10},{10,8},{12,... | collective-permute-start | bytes 393224 | tf_op jit(solution)/shard_map/ppermute | solution.py:27
  14.3 25.0 %copy-start.6 = (bf16[2,1,128,256]{3,2,1,0:T(8,128)(2,1)}, bf16[2,1,128,256]{3,2,1,0:T(8,128)(2,1)S(1)}, u32[]{:S(2)}) copy-start(bf16[2,1,128,256]{3,2,1,0:T(8,128)(2,1)S(1)} %collective-permute-done.4.refs_6_) | copy-start | bytes 393220
  14.3 7.7 %collective-permute-start.15 = (bf16[2,1,128,256]{3,2,1,0:T(8,128)(2,1)S(1)}, bf16[2,1,128,256]{3,2,1,0:T(8,128)(2,1)S(1)}, u32[]{:S(2)}, u32[]{:S(2)}) collective-permute-start(bf16[2,1,128,256]{3,2,1,0:T(8,128)(2,1)S(1)} %collective-permute-done.7.refs_9_), channel_id=1, source_target_pairs={{0,8},{8,16},{16,24},{24,0},{1,9},{9,17},{17,25},{25,1},{2,10},{10... | collective-permute-start | bytes 393224 | tf_op jit(solution)/shard_map/ppermute | solution.py:17
  18.0 21.2 %copy-start.7 = (bf16[2,1,128,256]{3,2,1,0:T(8,128)(2,1)}, bf16[2,1,128,256]{3,2,1,0:T(8,128)(2,1)S(1)}, u32[]{:S(2)}) copy-start(bf16[2,1,128,256]{3,2,1,0:T(8,128)(2,1)S(1)} %collective-permute-done.14.refs_16_) | copy-start | bytes 393220
  18.0 5.6 %collective-permute-start.11 = (bf16[2,1,128,256]{3,2,1,0:T(8,128)(2,1)S(1)}, bf16[2,1,128,256]{3,2,1,0:T(8,128)(2,1)S(1)}, u32[]{:S(2)}, u32[]{:S(2)}) collective-permute-start(bf16[2,1,128,256]{3,2,1,0:T(8,128)(2,1)S(1)} %collective-permute-done.7.refs_9_), channel_id=1, source_target_pairs={{0,4},{2,6},{4,0},{6,2},{1,5},{3,7},{5,1},{7,3},{8,12},{10,14},{12... | collective-permute-start | bytes 393224 | tf_op jit(solution)/shard_map/ppermute | solution.py:27
  19.1 20.1 %copy-start.8 = (bf16[2,1,128,256]{3,2,1,0:T(8,128)(2,1)}, bf16[2,1,128,256]{3,2,1,0:T(8,128)(2,1)S(1)}, u32[]{:S(2)}) copy-start(bf16[2,1,128,256]{3,2,1,0:T(8,128)(2,1)S(1)} %collective-permute-done.10.refs_12_) | copy-start | bytes 393220
  19.1 4.6 %collective-permute-start.9 = (bf16[2,1,128,256]{3,2,1,0:T(8,128)(2,1)S(1)}, bf16[2,1,128,256]{3,2,1,0:T(8,128)(2,1)S(1)}, u32[]{:S(2)}, u32[]{:S(2)}) collective-permute-start(bf16[2,1,128,256]{3,2,1,0:T(8,128)(2,1)S(1)} %collective-permute-done.7.refs_9_), channel_id=1, source_target_pairs={{0,2},{2,0},{4,6},{6,4},{1,3},{3,1},{5,7},{7,5},{8,10},{10,8},{12,... | collective-permute-start | bytes 393224 | tf_op jit(solution)/shard_map/ppermute | solution.py:27
  19.2 20.1 %copy-start.9 = (bf16[2,1,128,256]{3,2,1,0:T(8,128)(2,1)}, bf16[2,1,128,256]{3,2,1,0:T(8,128)(2,1)S(1)}, u32[]{:S(2)}) copy-start(bf16[2,1,128,256]{3,2,1,0:T(8,128)(2,1)S(1)} %collective-permute-done.8.refs_10_) | copy-start | bytes 393220
  19.2 7.7 %collective-permute-start.22 = (bf16[2,1,128,256]{3,2,1,0:T(8,128)(2,1)S(1)}, bf16[2,1,128,256]{3,2,1,0:T(8,128)(2,1)S(1)}, u32[]{:S(2)}, u32[]{:S(2)}) collective-permute-start(bf16[2,1,128,256]{3,2,1,0:T(8,128)(2,1)S(1)} %collective-permute-done.14.refs_16_), channel_id=1, source_target_pairs={{0,8},{8,16},{16,24},{24,0},{1,9},{9,17},{17,25},{25,1},{2,10},{10... | collective-permute-start | bytes 393224 | tf_op jit(solution)/shard_map/ppermute | solution.py:17
  19.2 20.0 %copy-start.10 = (bf16[2,1,128,256]{3,2,1,0:T(8,128)(2,1)}, bf16[2,1,128,256]{3,2,1,0:T(8,128)(2,1)S(1)}, u32[]{:S(2)}) copy-start(bf16[2,1,128,256]{3,2,1,0:T(8,128)(2,1)S(1)} %collective-permute-done.5.refs_7_) | copy-start | bytes 393220
  19.3 8.5 %collective-permute-start.18 = (bf16[2,1,128,256]{3,2,1,0:T(8,128)(2,1)S(1)}, bf16[2,1,128,256]{3,2,1,0:T(8,128)(2,1)S(1)}, u32[]{:S(2)}, u32[]{:S(2)}) collective-permute-start(bf16[2,1,128,256]{3,2,1,0:T(8,128)(2,1)S(1)} %collective-permute-done.14.refs_16_), channel_id=1, source_target_pairs={{0,4},{2,6},{4,0},{6,2},{1,5},{3,7},{5,1},{7,3},{8,12},{10,14},{12... | collective-permute-start | bytes 393224 | tf_op jit(solution)/shard_map/ppermute | solution.py:27
  22.0 17.3 %copy-start.11 = (bf16[2,1,128,256]{3,2,1,0:T(8,128)(2,1)}, bf16[2,1,128,256]{3,2,1,0:T(8,128)(2,1)S(1)}, u32[]{:S(2)}) copy-start(bf16[2,1,128,256]{3,2,1,0:T(8,128)(2,1)S(1)} %collective-permute-done.15.refs_17_) | copy-start | bytes 393220
  22.0 5.8 %collective-permute-start.16 = (bf16[2,1,128,256]{3,2,1,0:T(8,128)(2,1)S(1)}, bf16[2,1,128,256]{3,2,1,0:T(8,128)(2,1)S(1)}, u32[]{:S(2)}, u32[]{:S(2)}) collective-permute-start(bf16[2,1,128,256]{3,2,1,0:T(8,128)(2,1)S(1)} %collective-permute-done.14.refs_16_), channel_id=1, source_target_pairs={{0,2},{2,0},{4,6},{6,4},{1,3},{3,1},{5,7},{7,5},{8,10},{10,8},{12,... | collective-permute-start | bytes 393224 | tf_op jit(solution)/shard_map/ppermute | solution.py:27
  23.7 15.6 %copy-start.12 = (bf16[2,1,128,256]{3,2,1,0:T(8,128)(2,1)}, bf16[2,1,128,256]{3,2,1,0:T(8,128)(2,1)S(1)}, u32[]{:S(2)}) copy-start(bf16[2,1,128,256]{3,2,1,0:T(8,128)(2,1)S(1)} %collective-permute-done.11.refs_13_) | copy-start | bytes 393220
  23.7 4.6 %collective-permute-start.12 = (bf16[2,1,128,256]{3,2,1,0:T(8,128)(2,1)S(1)}, bf16[2,1,128,256]{3,2,1,0:T(8,128)(2,1)S(1)}, u32[]{:S(2)}, u32[]{:S(2)}) collective-permute-start(bf16[2,1,128,256]{3,2,1,0:T(8,128)(2,1)S(1)} %collective-permute-done.10.refs_12_), channel_id=1, source_target_pairs={{0,2},{2,0},{4,6},{6,4},{1,3},{3,1},{5,7},{7,5},{8,10},{10,8},{12,... | collective-permute-start | bytes 393224 | tf_op jit(solution)/shard_map/ppermute | solution.py:27
  23.7 15.6 %copy-start.13 = (bf16[2,1,128,256]{3,2,1,0:T(8,128)(2,1)}, bf16[2,1,128,256]{3,2,1,0:T(8,128)(2,1)S(1)}, u32[]{:S(2)}) copy-start(bf16[2,1,128,256]{3,2,1,0:T(8,128)(2,1)S(1)} %collective-permute-done.9.refs_11_) | copy-start | bytes 393220
  23.7 7.7 %collective-permute-start.23 = (bf16[2,1,128,256]{3,2,1,0:T(8,128)(2,1)S(1)}, bf16[2,1,128,256]{3,2,1,0:T(8,128)(2,1)S(1)}, u32[]{:S(2)}, u32[]{:S(2)}) collective-permute-start(bf16[2,1,128,256]{3,2,1,0:T(8,128)(2,1)S(1)} %collective-permute-done.15.refs_17_), channel_id=1, source_target_pairs={{0,8},{8,16},{16,24},{24,0},{1,9},{9,17},{17,25},{25,1},{2,10},{10... | collective-permute-start | bytes 393224 | tf_op jit(solution)/shard_map/ppermute | solution.py:17
  26.9 12.5 %copy-start.14 = (bf16[2,1,128,256]{3,2,1,0:T(8,128)(2,1)}, bf16[2,1,128,256]{3,2,1,0:T(8,128)(2,1)S(1)}, u32[]{:S(2)}) copy-start(bf16[2,1,128,256]{3,2,1,0:T(8,128)(2,1)S(1)} %collective-permute-done.22.refs_24_) | copy-start | bytes 393220
  26.9 6.0 %collective-permute-start.19 = (bf16[2,1,128,256]{3,2,1,0:T(8,128)(2,1)S(1)}, bf16[2,1,128,256]{3,2,1,0:T(8,128)(2,1)S(1)}, u32[]{:S(2)}, u32[]{:S(2)}) collective-permute-start(bf16[2,1,128,256]{3,2,1,0:T(8,128)(2,1)S(1)} %collective-permute-done.15.refs_17_), channel_id=1, source_target_pairs={{0,4},{2,6},{4,0},{6,2},{1,5},{3,7},{5,1},{7,3},{8,12},{10,14},{12... | collective-permute-start | bytes 393224 | tf_op jit(solution)/shard_map/ppermute | solution.py:27
  27.8 11.6 %copy-start.15 = (bf16[2,1,128,256]{3,2,1,0:T(8,128)(2,1)}, bf16[2,1,128,256]{3,2,1,0:T(8,128)(2,1)S(1)}, u32[]{:S(2)}) copy-start(bf16[2,1,128,256]{3,2,1,0:T(8,128)(2,1)S(1)} %collective-permute-done.18.refs_20_) | copy-start | bytes 393220
  27.8 5.8 %collective-permute-start.17 = (bf16[2,1,128,256]{3,2,1,0:T(8,128)(2,1)S(1)}, bf16[2,1,128,256]{3,2,1,0:T(8,128)(2,1)S(1)}, u32[]{:S(2)}, u32[]{:S(2)}) collective-permute-start(bf16[2,1,128,256]{3,2,1,0:T(8,128)(2,1)S(1)} %collective-permute-done.15.refs_17_), channel_id=1, source_target_pairs={{0,2},{2,0},{4,6},{6,4},{1,3},{3,1},{5,7},{7,5},{8,10},{10,8},{12,... | collective-permute-start | bytes 393224 | tf_op jit(solution)/shard_map/ppermute | solution.py:27
  27.8 11.5 %copy-start.16 = (bf16[2,1,128,256]{3,2,1,0:T(8,128)(2,1)}, bf16[2,1,128,256]{3,2,1,0:T(8,128)(2,1)S(1)}, u32[]{:S(2)}) copy-start(bf16[2,1,128,256]{3,2,1,0:T(8,128)(2,1)S(1)} %collective-permute-done.16.refs_18_) | copy-start | bytes 393220
  27.8 5.8 %collective-permute-start.13 = (bf16[2,1,128,256]{3,2,1,0:T(8,128)(2,1)S(1)}, bf16[2,1,128,256]{3,2,1,0:T(8,128)(2,1)S(1)}, u32[]{:S(2)}, u32[]{:S(2)}) collective-permute-start(bf16[2,1,128,256]{3,2,1,0:T(8,128)(2,1)S(1)} %collective-permute-done.11.refs_13_), channel_id=1, source_target_pairs={{0,2},{2,0},{4,6},{6,4},{1,3},{3,1},{5,7},{7,5},{8,10},{10,8},{12,... | collective-permute-start | bytes 393224 | tf_op jit(solution)/shard_map/ppermute | solution.py:27
  28.3 11.1 %copy-start.17 = (bf16[2,1,128,256]{3,2,1,0:T(8,128)(2,1)}, bf16[2,1,128,256]{3,2,1,0:T(8,128)(2,1)S(1)}, u32[]{:S(2)}) copy-start(bf16[2,1,128,256]{3,2,1,0:T(8,128)(2,1)S(1)} %collective-permute-done.12.refs_14_) | copy-start | bytes 393220
  28.3 6.5 %collective-permute-start.26 = (bf16[2,1,128,256]{3,2,1,0:T(8,128)(2,1)S(1)}, bf16[2,1,128,256]{3,2,1,0:T(8,128)(2,1)S(1)}, u32[]{:S(2)}, u32[]{:S(2)}) collective-permute-start(bf16[2,1,128,256]{3,2,1,0:T(8,128)(2,1)S(1)} %collective-permute-done.22.refs_24_), channel_id=1, source_target_pairs={{0,4},{2,6},{4,0},{6,2},{1,5},{3,7},{5,1},{7,3},{8,12},{10,14},{12... | collective-permute-start | bytes 393224 | tf_op jit(solution)/shard_map/ppermute | solution.py:27
  31.4 3.5 %collective-permute-start.24 = (bf16[2,1,128,256]{3,2,1,0:T(8,128)(2,1)S(1)}, bf16[2,1,128,256]{3,2,1,0:T(8,128)(2,1)S(1)}, u32[]{:S(2)}, u32[]{:S(2)}) collective-permute-start(bf16[2,1,128,256]{3,2,1,0:T(8,128)(2,1)S(1)} %collective-permute-done.22.refs_24_), channel_id=1, source_target_pairs={{0,2},{2,0},{4,6},{6,4},{1,3},{3,1},{5,7},{7,5},{8,10},{10,8},{12,... | collective-permute-start | bytes 393224 | tf_op jit(solution)/shard_map/ppermute | solution.py:27
  32.9 5.0 %collective-permute-start.27 = (bf16[2,1,128,256]{3,2,1,0:T(8,128)(2,1)S(1)}, bf16[2,1,128,256]{3,2,1,0:T(8,128)(2,1)S(1)}, u32[]{:S(2)}, u32[]{:S(2)}) collective-permute-start(bf16[2,1,128,256]{3,2,1,0:T(8,128)(2,1)S(1)} %collective-permute-done.23.refs_25_), channel_id=1, source_target_pairs={{0,4},{2,6},{4,0},{6,2},{1,5},{3,7},{5,1},{7,3},{8,12},{10,14},{12... | collective-permute-start | bytes 393224 | tf_op jit(solution)/shard_map/ppermute | solution.py:27
  33.6 4.3 %collective-permute-start.25 = (bf16[2,1,128,256]{3,2,1,0:T(8,128)(2,1)S(1)}, bf16[2,1,128,256]{3,2,1,0:T(8,128)(2,1)S(1)}, u32[]{:S(2)}, u32[]{:S(2)}) collective-permute-start(bf16[2,1,128,256]{3,2,1,0:T(8,128)(2,1)S(1)} %collective-permute-done.23.refs_25_), channel_id=1, source_target_pairs={{0,2},{2,0},{4,6},{6,4},{1,3},{3,1},{5,7},{7,5},{8,10},{10,8},{12,... | collective-permute-start | bytes 393224 | tf_op jit(solution)/shard_map/ppermute | solution.py:27
  33.6 4.2 %collective-permute-start.20 = (bf16[2,1,128,256]{3,2,1,0:T(8,128)(2,1)S(1)}, bf16[2,1,128,256]{3,2,1,0:T(8,128)(2,1)S(1)}, u32[]{:S(2)}, u32[]{:S(2)}) collective-permute-start(bf16[2,1,128,256]{3,2,1,0:T(8,128)(2,1)S(1)} %collective-permute-done.18.refs_20_), channel_id=1, source_target_pairs={{0,2},{2,0},{4,6},{6,4},{1,3},{3,1},{5,7},{7,5},{8,10},{10,8},{12,... | collective-permute-start | bytes 393224 | tf_op jit(solution)/shard_map/ppermute | solution.py:27
  34.9 3.0 %collective-permute-start.21 = (bf16[2,1,128,256]{3,2,1,0:T(8,128)(2,1)S(1)}, bf16[2,1,128,256]{3,2,1,0:T(8,128)(2,1)S(1)}, u32[]{:S(2)}, u32[]{:S(2)}) collective-permute-start(bf16[2,1,128,256]{3,2,1,0:T(8,128)(2,1)S(1)} %collective-permute-done.19.refs_21_), channel_id=1, source_target_pairs={{0,2},{2,0},{4,6},{6,4},{1,3},{3,1},{5,7},{7,5},{8,10},{10,8},{12,... | collective-permute-start | bytes 393224 | tf_op jit(solution)/shard_map/ppermute | solution.py:27
  34.9 3.0 %collective-permute-start.28 = (bf16[2,1,128,256]{3,2,1,0:T(8,128)(2,1)S(1)}, bf16[2,1,128,256]{3,2,1,0:T(8,128)(2,1)S(1)}, u32[]{:S(2)}, u32[]{:S(2)}) collective-permute-start(bf16[2,1,128,256]{3,2,1,0:T(8,128)(2,1)S(1)} %collective-permute-done.26.refs_28_), channel_id=1, source_target_pairs={{0,2},{2,0},{4,6},{6,4},{1,3},{3,1},{5,7},{7,5},{8,10},{10,8},{12,... | collective-permute-start | bytes 393224 | tf_op jit(solution)/shard_map/ppermute | solution.py:27
  37.9 1.3 %collective-permute-start.29 = (bf16[2,1,128,256]{3,2,1,0:T(8,128)(2,1)S(1)}, bf16[2,1,128,256]{3,2,1,0:T(8,128)(2,1)S(1)}, u32[]{:S(2)}, u32[]{:S(2)}) collective-permute-start(bf16[2,1,128,256]{3,2,1,0:T(8,128)(2,1)S(1)} %collective-permute-done.27.refs_29_), channel_id=1, source_target_pairs={{0,2},{2,0},{4,6},{6,4},{1,3},{3,1},{5,7},{7,5},{8,10},{10,8},{12,... | collective-permute-start | bytes 393224 | tf_op jit(solution)/shard_map/ppermute | solution.py:27
  (12 other events, 43.5 us)

commit v2 on v0

v2 whole, which is shorter than its diff:
```python
import functools
import math

import jax
import jax.numpy as jnp
from jax import lax
from jax.experimental import pallas as pl
from jax.experimental.pallas import tpu as pltpu
from jax.sharding import PartitionSpec as P

HEAD_DIM = 128
MASKED = -1e30
STAGES = 4


def shift(array, axis, size, step):
    return lax.ppermute(array, axis, [(i, (i + step) % size) for i in range(size)])


def turn(array, size, cores, ring_step, core_step):
    rings = size // cores
    pairs = []
    for ring in range(rings):
        for core in range(cores):
            to = ((ring + ring_step) % rings) * cores + (core + core_step) % cores
            pairs.append((ring * cores + core, to))
    return lax.ppermute(array, "ka", pairs)


def dot(a, b, b_dim):
    return lax.dot_general(a, b, (((1,), (b_dim,)), ((), ())), preferred_element_type=jnp.float32)


def attend_stage(plan, first, last, order_ref, mask_ref, q_ref, *refs):
    pb, ka, cores, places = plan
    count = len(places)
    keys, values = refs[:count], refs[count : 2 * count]
    refs = refs[2 * count :]
    if not first:
        old_refs, refs = refs[:3], refs[3:]
    if last:
        out_ref, refs = refs[0], refs[1:]
    acc, top, total, k_pool, v_pool, bias = refs[:6]
    own_slots, kv_local, rows, _ = acc.shape
    held, _, block_rows, _ = keys[0].shape
    group = rows // block_rows
    rings = ka // cores
    p_at, k_at = lax.axis_index("pb"), lax.axis_index("ka")
    ring_at, core_at = k_at // cores, lax.rem(k_at, cores)
    scale = math.log2(math.e) / math.sqrt(HEAD_DIM)

    blocks = []
    for hops, y, c in places:
        ring = lax.rem(ring_at + (rings - y), rings)
        core = lax.rem(core_at + (cores - c), cores)
        class_local = held // len(hops)
        for z in hops:
            source = lax.rem(p_at + (pb - z), pb)
            for t in range(class_local):
                blocks.append((source * class_local + t) * ka + ring * cores + core)

    if first:
        acc[...] = jnp.zeros(acc.shape, acc.dtype)
        total[...] = jnp.zeros(total.shape, total.dtype)
        top[...] = jnp.full(top.shape, MASKED, top.dtype)
    else:
        for new, old in zip((acc, top, total), old_refs):
            new[...] = old[...]

    row_id = lax.broadcasted_iota(jnp.int32, (block_rows, block_rows), 0)
    col_id = lax.broadcasted_iota(jnp.int32, (block_rows, block_rows), 1)

    def fill(s):
        row = k_at * own_slots + s
        own = order_ref[row]
        listed = [mask_ref[row, block] for block in blocks]
        size = functools.reduce(lambda a, b: a + b, listed)
        done = jnp.int32(0)
        has_own = jnp.int32(0)
        for at, block in enumerate(blocks):
            piece, t = at // held, at % held
            is_own = block == own
            place = jnp.where(is_own, size - 1, done)

            @pl.when(listed[at] == 1)
            def _():
                k_pool[place] = keys[piece][t, 0]
                v_pool[place] = values[piece][t, 0]

            done = done + jnp.where(is_own, 0, listed[at])
            has_own = has_own + jnp.where(is_own, listed[at], 0)

        @pl.when(lax.rem(size, 2) == 1)
        def _():
            k_pool[size] = jnp.zeros(k_pool.shape[1:], k_pool.dtype)
            v_pool[size] = jnp.zeros(v_pool.shape[1:], v_pool.dtype)

        return size, has_own

    def unit(s, size, has_own, u):
        for half in range(2):
            entry = 2 * u + half
            reach = jnp.where(entry >= size, -block_rows, block_rows)
            reach = jnp.where((entry == size - 1) & (has_own == 1), 0, reach)
            bias[:, half * block_rows : (half + 1) * block_rows] = jnp.where(
                col_id <= row_id + reach, 0.0, MASKED
            )
        for g in range(kv_local):
            columns = slice(g * HEAD_DIM, (g + 1) * HEAD_DIM)
            k_pair = jnp.concatenate(
                [k_pool[2 * u, :, columns], k_pool[2 * u + 1, :, columns]], axis=0
            )
            v_pair = jnp.concatenate(
                [v_pool[2 * u, :, columns], v_pool[2 * u + 1, :, columns]], axis=0
            )
            q_rows = jnp.concatenate(
                [
                    q_ref[
                        pl.ds(pl.multiple_of(s * block_rows, block_rows), block_rows),
                        (g * group + x) * HEAD_DIM : (g * group + x + 1) * HEAD_DIM,
                    ]
                    for x in range(group)
                ],
                axis=0,
            )
            scores = dot(q_rows, k_pair, 1)
            weights = []
            shrinks = []
            for x in range(group):
                span = slice(x * block_rows, (x + 1) * block_rows)
                score = scores[span] + bias[...]
                halves = score[:, :block_rows], score[:, block_rows:]
                peak = jnp.max(jnp.maximum(*halves), axis=1, keepdims=True)
                old = top[s, g, span]
                new = jnp.maximum(old, peak)
                top[s, g, span] = new
                shrink = jnp.exp2((old - new) * scale)
                one, two = (jnp.exp2((half - new) * scale) for half in halves)
                total[s, g, span] = total[s, g, span] * shrink + (one + two)
                weights.append(
                    jnp.concatenate([one.astype(jnp.bfloat16), two.astype(jnp.bfloat16)], axis=1)
                )
                shrinks.append(shrink)
            added = dot(jnp.concatenate(weights, axis=0), v_pair, 0)
            for x in range(group):
                span = slice(x * block_rows, (x + 1) * block_rows)
                acc[s, g, span] = acc[s, g, span] * shrinks[x] + added[span]

    for s in range(own_slots):
        size, has_own = fill(s)

        def one_unit(u, carry, s=s, size=size, has_own=has_own):
            unit(s, size, has_own, u)
            return carry

        lax.fori_loop(0, (size + 1) // 2, one_unit, 0)
        if last:
            for g in range(kv_local):
                for x in range(group):
                    span = slice(x * block_rows, (x + 1) * block_rows)
                    under = jnp.sum(total[s, g, span], axis=1, keepdims=True)
                    out_ref[
                        s * block_rows : (s + 1) * block_rows,
                        (g * group + x) * HEAD_DIM : (g * group + x + 1) * HEAD_DIM,
                    ] = (acc[s, g, span] / under).astype(out_ref.dtype)


def on_device(queries, keys, values, q_order, block_mask):
    pb, ka = lax.axis_size("pb"), lax.axis_size("ka")
    cores = 2 if ka % 2 == 0 else 1
    rings = ka // cores
    class_local, _, block_rows, kv_width = keys.shape
    kv_local = kv_width // HEAD_DIM
    width = queries.shape[1]
    group = width // kv_width
    own_slots = queries.shape[0] // block_rows // ka
    own_rows = own_slots * block_rows
    own_queries = lax.dynamic_slice_in_dim(
        queries, lax.axis_index("ka") * own_rows, own_rows, axis=0
    )

    state_shape = jax.ShapeDtypeStruct((own_slots, kv_local, group * block_rows, HEAD_DIM), jnp.float32)
    vmem = pl.BlockSpec(memory_space=pltpu.VMEM)
    smem = pl.BlockSpec(memory_space=pltpu.SMEM)
    stages = min(STAGES, pb)
    sources = pb // stages
    near = (keys, values)
    state = ()
    for stage in range(stages):
        places, pieces, nears = [], [], []
        hops = range(stage * sources, (stage + 1) * sources)
        for z in hops:
            if z:
                near = tuple(shift(array, "pb", pb, 1) for array in near)
            nears.append(near)
        ring = nears[0]
        if sources > 1:
            ring = tuple(jnp.concatenate(arrays, axis=0) for arrays in zip(*nears))
        for y in range(rings):
            if y:
                ring = tuple(turn(array, ka, cores, 1, 0) for array in ring)
            here = ring
            for c in range(cores):
                if c:
                    here = tuple(turn(array, ka, cores, 0, 1) for array in here)
                places.append((hops, y, c))
                pieces.append(here)
        first, last = stage == 0, stage == stages - 1
        held = len(places) * sources * class_local
        held += held % 2
        pools = [pltpu.VMEM((held, block_rows, kv_width), jnp.bfloat16)] * 2
        pools.append(pltpu.VMEM((block_rows, 2 * block_rows), jnp.float32))
        if last:
            outs = jax.ShapeDtypeStruct((own_rows, width), jnp.bfloat16)
            out_specs = vmem
            scratch = [pltpu.VMEM(state_shape.shape, state_shape.dtype)] * 3 + pools
        else:
            outs = (state_shape,) * 3
            out_specs = (vmem,) * 3
            scratch = pools
        state = pl.pallas_call(
            functools.partial(attend_stage, (pb, ka, cores, places), first, last),
            out_shape=outs,
            in_specs=[smem] * 2 + [vmem] * (1 + 2 * len(places) + len(state)),
            out_specs=out_specs,
            scratch_shapes=scratch,
            compiler_params=pltpu.CompilerParams(vmem_limit_bytes=40 * 1024 * 1024),
            cost_estimate=pl.CostEstimate(
                flops=2**30, bytes_accessed=2**22, transcendentals=2**20
            ),
        )(
            q_order,
            block_mask,
            own_queries,
            *[piece[0] for piece in pieces],
            *[piece[1] for piece in pieces],
            *state,
        )
    return state


def solution(mesh):
    in_specs = (
        P("pb", "ha"),
        P("pb", "ka", None, "ha"),
        P("pb", "ka", None, "ha"),
        P("pb"),
        P("pb", None),
    )
    out_specs = P(("pb", "ka"), "ha")
    return jax.shard_map(
        on_device, mesh=mesh, in_specs=in_specs, out_specs=out_specs, check_vma=False
    )
```

time: 311 us -> 61.7 us (0.20)
  the two profiles are of different devices: /device:TPU:27 before, /device:TPU:0 now
where the time goes in v2:
time: 61.7 us; the launch traced here: 61.5 us
  waiting for transfers between devices  21.5 us (35%)
  starting transfers between devices  18.5 us (30%)
  Pallas kernels  17.2 us (28%)
  local copies, waits for them, and re-layouts  4.06 us (7%)
    pallas_call x4, Pallas kernels, on_device(): pl.pallas_call(functools.partial(attend_stage, (pb, ka, cores, places), f...  17.2 us
    ppermute x24, starting transfers between devices, turn(): return lax.ppermute(array, 'ka', pairs)  13.6 us
    ppermute x6, waiting for transfers between devices, shift(): lax.ppermute(array, axis, [(i, (i + step) % size) for i in range(size)])  11.4 us
    ppermute x24, waiting for transfers between devices, turn(): return lax.ppermute(array, 'ka', pairs)  10.1 us
    ppermute x6, starting transfers between devices, shift(): lax.ppermute(array, axis, [(i, (i + step) % size) for i in range(size)])  4.97 us
    unnamed x12, local copies, waits for them, and re-layouts  2.74 us
    dynamic_slice x1, local copies, waits for them, and re-layouts, on_device(): lax.dynamic_slice_in_dim(queries, lax.axis_index('ka') * own_rows, own_ro...  1.32 us
  transfers between devices with their start and end apart: 30, of which 10 were waited for; matrix products, arithmetic and copies ran while one was open for 2% of the time, Pallas kernels for 20%

profile of v2, /device:TPU:0, one launch (start us, length us, event | category | flops | bytes accessed | tf_op | source)
XLA Modules:
  0.0 61.5 jit_solution(13336901800464098174)
XLA Ops:
  0.0 3.0 %collective-permute-start.25 = (bf16[2,1,128,256]{3,2,1,0:T(8,128)(2,1)}, bf16[2,1,128,256]{3,2,1,0:T(8,128)(2,1)S(1)}, u32[]{:S(2)}, u32[]{:S(2)}) collective-permute-start(bf16[2,1,128,256]{3,2,1,0:T(8,128)(2,1)} %refs_0_.1), channel_id=1, source_target_pairs={{0,4},{2,6},{4,0},{6,2},{1,5},{3,7},{5,1},{7,3},{8,12},{10,14},{12... | collective-permute-start | bytes 393224 | tf_op jit(solution)/shard_map/ppermute | solution.py:27
  3.1 0.1 collective-permute-start.28
  3.1 0.0 collective-permute-start.24
  3.1 2.0 %collective-permute-start = (bf16[2,1,128,256]{3,2,1,0:T(8,128)(2,1)}, bf16[2,1,128,256]{3,2,1,0:T(8,128)(2,1)S(1)}, u32[]{:S(2)}, u32[]{:S(2)}) collective-permute-start(bf16[2,1,128,256]{3,2,1,0:T(8,128)(2,1)} %refs_0_.1), channel_id=1, source_target_pairs={{0,8},{8,16},{16,24},{24,0},{1,9},{9,17},{17,25},{25,1},{2,10},{10... | collective-permute-start | bytes 393224 | tf_op jit(solution)/shard_map/ppermute | solution.py:17
  5.1 1.6 %collective-permute-start.6 = (bf16[2,1,128,256]{3,2,1,0:T(8,128)(2,1)}, bf16[2,1,128,256]{3,2,1,0:T(8,128)(2,1)S(1)}, u32[]{:S(2)}, u32[]{:S(2)}) collective-permute-start(bf16[2,1,128,256]{3,2,1,0:T(8,128)(2,1)} %refs_4_.1), channel_id=1, source_target_pairs={{0,8},{8,16},{16,24},{24,0},{1,9},{9,17},{17,25},{25,1},{2,10},{10... | collective-permute-start | bytes 393224 | tf_op jit(solution)/shard_map/ppermute | solution.py:17
  6.7 0.9 %collective-permute-done.25.refs_2_ = bf16[2,1,128,256]{3,2,1,0:T(8,128)(2,1)S(1)} collective-permute-done((bf16[2,1,128,256]{3,2,1,0:T(8,128)(2,1)}, bf16[2,1,128,256]{3,2,1,0:T(8,128)(2,1)S(1)}, u32[]{:S(2)}, u32[]{:S(2)}) %collective-permute-start.25) | collective-permute-done | bytes 131104 | tf_op jit(solution)/shard_map/ppermute | solution.py:27
  7.6 2.0 %collective-permute-done.28.refs_6_ = bf16[2,1,128,256]{3,2,1,0:T(8,128)(2,1)S(1)} collective-permute-done((bf16[2,1,128,256]{3,2,1,0:T(8,128)(2,1)}, bf16[2,1,128,256]{3,2,1,0:T(8,128)(2,1)S(1)}, u32[]{:S(2)}, u32[]{:S(2)}) %collective-permute-start.28) | collective-permute-done | bytes 131104 | tf_op jit(solution)/shard_map/ppermute | solution.py:27
  9.6 0.5 collective-permute-start.29
  10.1 1.6 %collective-permute-done.refs_0_ = bf16[2,1,128,256]{3,2,1,0:T(8,128)(2,1)S(1)} collective-permute-done((bf16[2,1,128,256]{3,2,1,0:T(8,128)(2,1)}, bf16[2,1,128,256]{3,2,1,0:T(8,128)(2,1)S(1)}, u32[]{:S(2)}, u32[]{:S(2)}) %collective-permute-start) | collective-permute-done | bytes 131104 | tf_op jit(solution)/shard_map/ppermute | solution.py:17
  11.7 1.7 %collective-permute-start.19 = (bf16[2,1,128,256]{3,2,1,0:T(8,128)(2,1)S(1)}, bf16[2,1,128,256]{3,2,1,0:T(8,128)(2,1)S(1)}, u32[]{:S(2)}, u32[]{:S(2)}) collective-permute-start(bf16[2,1,128,256]{3,2,1,0:T(8,128)(2,1)S(1)} %collective-permute-done.refs_0_), channel_id=1, source_target_pairs={{0,4},{2,6},{4,0},{6,2},{1,5},{3,7},{5,1},{7,3},{8,12},{10,14},{12... | collective-permute-start | bytes 393224 | tf_op jit(solution)/shard_map/ppermute | solution.py:27
  13.4 1.0 %collective-permute-done.6.refs_4_ = bf16[2,1,128,256]{3,2,1,0:T(8,128)(2,1)S(1)} collective-permute-done((bf16[2,1,128,256]{3,2,1,0:T(8,128)(2,1)}, bf16[2,1,128,256]{3,2,1,0:T(8,128)(2,1)S(1)}, u32[]{:S(2)}, u32[]{:S(2)}) %collective-permute-start.6) | collective-permute-done | bytes 131104 | tf_op jit(solution)/shard_map/ppermute | solution.py:17
  14.3 1.5 %collective-permute-start.22 = (bf16[2,1,128,256]{3,2,1,0:T(8,128)(2,1)S(1)}, bf16[2,1,128,256]{3,2,1,0:T(8,128)(2,1)S(1)}, u32[]{:S(2)}, u32[]{:S(2)}) collective-permute-start(bf16[2,1,128,256]{3,2,1,0:T(8,128)(2,1)S(1)} %collective-permute-done.6.refs_4_), channel_id=1, source_target_pairs={{0,4},{2,6},{4,0},{6,2},{1,5},{3,7},{5,1},{7,3},{8,12},{10,14},{12... | collective-permute-start | bytes 393224 | tf_op jit(solution)/shard_map/ppermute | solution.py:27
  15.9 0.0 collective-permute-done.27.refs_5_
  15.9 0.0 collective-permute-start.18
  15.9 0.0 collective-permute-done.26.refs_3_
  15.9 0.1 collective-permute-start.1
  15.9 0.0 collective-permute-done.29.refs_7_
  16.0 1.3 %collective-permute-start.7 = (bf16[2,1,128,256]{3,2,1,0:T(8,128)(2,1)S(1)}, bf16[2,1,128,256]{3,2,1,0:T(8,128)(2,1)S(1)}, u32[]{:S(2)}, u32[]{:S(2)}) collective-permute-start(bf16[2,1,128,256]{3,2,1,0:T(8,128)(2,1)S(1)} %collective-permute-done.6.refs_4_), channel_id=1, source_target_pairs={{0,8},{8,16},{16,24},{24,0},{1,9},{9,17},{17,25},{25,1},{2,10},{10... | collective-permute-start | bytes 393224 | tf_op jit(solution)/shard_map/ppermute | solution.py:17
  17.2 0.0 collective-permute-done.19.refs_2_
  17.2 0.0 collective-permute-start.21
  17.2 2.4 %collective-permute-done.22.refs_6_ = bf16[2,1,128,256]{3,2,1,0:T(8,128)(2,1)S(1)} collective-permute-done((bf16[2,1,128,256]{3,2,1,0:T(8,128)(2,1)S(1)}, bf16[2,1,128,256]{3,2,1,0:T(8,128)(2,1)S(1)}, u32[]{:S(2)}, u32[]{:S(2)}) %collective-permute-start.22) | collective-permute-done | bytes 131104 | tf_op jit(solution)/shard_map/ppermute | solution.py:27
  19.7 0.0 collective-permute-start.20
  19.7 0.0 collective-permute-done.18.refs_1_
  19.7 0.5 collective-permute-start.23
  20.2 3.8 %collective-permute-done.1.refs_0_ = bf16[2,1,128,256]{3,2,1,0:T(8,128)(2,1)S(1)} collective-permute-done((bf16[2,1,128,256]{3,2,1,0:T(8,128)(2,1)S(1)}, bf16[2,1,128,256]{3,2,1,0:T(8,128)(2,1)S(1)}, u32[]{:S(2)}, u32[]{:S(2)}) %collective-permute-start.1) | collective-permute-done | bytes 131104 | tf_op jit(solution)/shard_map/ppermute | solution.py:17
  24.0 0.5 collective-permute-start.13
  24.5 1.9 %collective-permute-done.7.refs_4_ = bf16[2,1,128,256]{3,2,1,0:T(8,128)(2,1)S(1)} collective-permute-done((bf16[2,1,128,256]{3,2,1,0:T(8,128)(2,1)S(1)}, bf16[2,1,128,256]{3,2,1,0:T(8,128)(2,1)S(1)}, u32[]{:S(2)}, u32[]{:S(2)}) %collective-permute-start.7) | collective-permute-done | bytes 131104 | tf_op jit(solution)/shard_map/ppermute | solution.py:17
  26.4 0.5 collective-permute-start.16
  26.9 0.0 collective-permute-done.20.refs_3_
  26.9 0.1 collective-permute-start.2
  27.0 0.1 collective-permute-start.12
  27.1 2.3 %collective-permute-done.13.refs_2_ = bf16[2,1,128,256]{3,2,1,0:T(8,128)(2,1)S(1)} collective-permute-done((bf16[2,1,128,256]{3,2,1,0:T(8,128)(2,1)S(1)}, bf16[2,1,128,256]{3,2,1,0:T(8,128)(2,1)S(1)}, u32[]{:S(2)}, u32[]{:S(2)}) %collective-permute-start.13) | collective-permute-done | bytes 131104 | tf_op jit(solution)/shard_map/ppermute | solution.py:27
  29.3 2.5 %collective-permute-done.16.refs_6_ = bf16[2,1,128,256]{3,2,1,0:T(8,128)(2,1)S(1)} collective-permute-done((bf16[2,1,128,256]{3,2,1,0:T(8,128)(2,1)S(1)}, bf16[2,1,128,256]{3,2,1,0:T(8,128)(2,1)S(1)}, u32[]{:S(2)}, u32[]{:S(2)}) %collective-permute-start.16) | collective-permute-done | bytes 131104 | tf_op jit(solution)/shard_map/ppermute | solution.py:27
  31.8 3.1 %collective-permute-done.8.refs_4_ = bf16[2,1,128,256]{3,2,1,0:T(8,128)(2,1)S(1)} collective-permute-done((bf16[2,1,128,256]{3,2,1,0:T(8,128)(2,1)S(1)}, bf16[2,1,128,256]{3,2,1,0:T(8,128)(2,1)S(1)}, u32[]{:S(2)}, u32[]{:S(2)}) %collective-permute-start.8) | collective-permute-done | bytes 131104 | tf_op jit(solution)/shard_map/ppermute | solution.py:17
  34.9 1.5 %collective-permute-start.10 = (bf16[2,1,128,256]{3,2,1,0:T(8,128)(2,1)S(1)}, bf16[2,1,128,256]{3,2,1,0:T(8,128)(2,1)S(1)}, u32[]{:S(2)}, u32[]{:S(2)}) collective-permute-start(bf16[2,1,128,256]{3,2,1,0:T(8,128)(2,1)S(1)} %collective-permute-done.8.refs_4_), channel_id=1, source_target_pairs={{0,4},{2,6},{4,0},{6,2},{1,5},{3,7},{5,1},{7,3},{8,12},{10,14},{12... | collective-permute-start | bytes 393224 | tf_op jit(solution)/shard_map/ppermute | solution.py:27
  36.4 1.4 %collective-permute-start.4 = (bf16[2,1,128,256]{3,2,1,0:T(8,128)(2,1)S(1)}, bf16[2,1,128,256]{3,2,1,0:T(8,128)(2,1)S(1)}, u32[]{:S(2)}, u32[]{:S(2)}) collective-permute-start(bf16[2,1,128,256]{3,2,1,0:T(8,128)(2,1)S(1)} %collective-permute-done.2.refs_0_), channel_id=1, source_target_pairs={{0,4},{2,6},{4,0},{6,2},{1,5},{3,7},{5,1},{7,3},{8,12},{10,14},{12... | collective-permute-start | bytes 393224 | tf_op jit(solution)/shard_map/ppermute | solution.py:27
  37.8 1.3 %constant_dynamic-slice_fusion.q_ref = bf16[256,2048]{1,0:T(8,128)(2,1)S(1)} fusion(bf16[1024,2048]{1,0:T(8,128)(2,1)} %param.5, s32[]{:T(128)S(6)} %select_n.3), kind=kLoop, calls=%fused_computation | loop fusion | bytes 2097156 | tf_op jit(solution)/shard_map/dynamic_slice | solution.py:178
  39.2 0.1 collective-permute-start.17
  39.3 3.4 %shard_map.55 = (f32[2,2,1024,128]{3,2,1,0:T(8,128)S(1)}, f32[2,2,1024,128]{3,2,1,0:T(8,128)S(1)}, f32[2,2,1024,128]{3,2,1,0:T(8,128)S(1)}) custom-call(s32[8]{0:T(128)S(1)} %copy-done.3, s32[8,32]{1,0:T(8,128)S(1)} %copy-done.2, bf16[256,2048]{1,0:T(8,128)(2,1)S(1)} %constant_dynamic-slice_fusion.q_ref, bf16[2,1,128,256]{3,2,1,0:T(8,128)(2,1)S(1)} %copy-done.4, ...), custom_call_target="tpu_custom_call" | custom-call | flops 1073741824 | bytes 4194304 | tf_op jit(solution)/shard_map/pallas_call | solution.py:221
  42.7 1.4 %copy-done = f32[2,2,1024,128]{3,2,1,0:T(8,128)} copy-done((f32[2,2,1024,128]{3,2,1,0:T(8,128)}, f32[2,2,1024,128]{3,2,1,0:T(8,128)S(1)}, u32[]{:S(2)}) %copy-start) | copy-done | bytes 2097176
  44.0 1.6 %collective-permute-start.3 = (bf16[2,1,128,256]{3,2,1,0:T(8,128)(2,1)S(1)}, bf16[2,1,128,256]{3,2,1,0:T(8,128)(2,1)S(1)}, u32[]{:S(2)}, u32[]{:S(2)}) collective-permute-start(bf16[2,1,128,256]{3,2,1,0:T(8,128)(2,1)S(1)} %collective-permute-done.2.refs_0_), channel_id=1, source_target_pairs={{0,2},{2,0},{4,6},{6,4},{1,3},{3,1},{5,7},{7,5},{8,10},{10,8},{12,... | collective-permute-start | bytes 393224 | tf_op jit(solution)/shard_map/ppermute | solution.py:27
  45.6 0.1 collective-permute-start.9
  45.7 0.4 collective-permute-start.11
  46.1 0.1 collective-permute-start.5
  46.2 3.3 %shard_map.56 = (f32[2,2,1024,128]{3,2,1,0:T(8,128)S(1)}, f32[2,2,1024,128]{3,2,1,0:T(8,128)S(1)}, f32[2,2,1024,128]{3,2,1,0:T(8,128)S(1)}) custom-call(s32[8]{0:T(128)S(1)} %copy-done.3, s32[8,32]{1,0:T(8,128)S(1)} %copy-done.2, bf16[256,2048]{1,0:T(8,128)(2,1)S(1)} %constant_dynamic-slice_fusion.q_ref, ...), custom_call_target="tpu_custom_call" | custom-call | flops 1073741824 | bytes 4194304 | tf_op jit(solution)/shard_map/pallas_call | solution.py:221
  49.5 1.4 %copy-done.1 = f32[2,2,1024,128]{3,2,1,0:T(8,128)} copy-done((f32[2,2,1024,128]{3,2,1,0:T(8,128)}, f32[2,2,1024,128]{3,2,1,0:T(8,128)S(1)}, u32[]{:S(2)}) %copy-start.1) | copy-done | bytes 2097176
  50.8 5.5 %shard_map.57 = (f32[2,2,1024,128]{3,2,1,0:T(8,128)S(1)}, f32[2,2,1024,128]{3,2,1,0:T(8,128)S(1)}, f32[2,2,1024,128]{3,2,1,0:T(8,128)S(1)}) custom-call(s32[8]{0:T(128)S(1)} %copy-done.3, s32[8,32]{1,0:T(8,128)S(1)} %copy-done.2, bf16[256,2048]{1,0:T(8,128)(2,1)S(1)} %constant_dynamic-slice_fusion.q_ref, ...), custom_call_target="tpu_custom_call" | custom-call | flops 1073741824 | bytes 4194304 | tf_op jit(solution)/shard_map/pallas_call | solution.py:221
  56.4 5.1 %shard_map.58 = bf16[256,2048]{1,0:T(8,128)(2,1)} custom-call(s32[8]{0:T(128)S(1)} %copy-done.3, s32[8,32]{1,0:T(8,128)S(1)} %copy-done.2, bf16[256,2048]{1,0:T(8,128)(2,1)S(1)} %constant_dynamic-slice_fusion.q_ref, bf16[2,1,128,256]{3,2,1,0:T(8,128)(2,1)S(1)} %collective-permute-done.2.refs_0_, bf16[2,1,128,256]{3,2,1,0:T(8,128)(2,1)S(1)} %collective-permute-done.3.refs_1_, ...), custom_call_target="tpu_custom_call" | custom-call | flops 1073741824 | bytes 4194304 | tf_op jit(solution)/shard_map/pallas_call | solution.py:221
  (29 shorter events, 0.1 us)
Async XLA Ops:
  0.0 39.2 %copy-start.4 = (bf16[2,1,128,256]{3,2,1,0:T(8,128)(2,1)S(1)}, bf16[2,1,128,256]{3,2,1,0:T(8,128)(2,1)}, u32[]{:S(2)}) copy-start(bf16[2,1,128,256]{3,2,1,0:T(8,128)(2,1)} %refs_0_.1) | copy-start | bytes 393220
  0.0 39.3 %copy-start.5 = (bf16[2,1,128,256]{3,2,1,0:T(8,128)(2,1)S(1)}, bf16[2,1,128,256]{3,2,1,0:T(8,128)(2,1)}, u32[]{:S(2)}) copy-start(bf16[2,1,128,256]{3,2,1,0:T(8,128)(2,1)} %refs_4_.1) | copy-start | bytes 393220
  0.0 39.3 %copy-start.3 = (s32[8]{0:T(128)S(1)}, s32[8]{0:T(128)}, u32[]{:S(2)}) copy-start(s32[8]{0:T(128)} %order_ref.7) | copy-start | bytes 100
  0.0 39.3 %copy-start.2 = (s32[8,32]{1,0:T(8,128)S(1)}, s32[8,32]{1,0:T(8,128)}, u32[]{:S(2)}) copy-start(s32[8,32]{1,0:T(8,128)} %mask_ref.7) | copy-start | bytes 3076
  0.0 7.6 %collective-permute-start.25 = (bf16[2,1,128,256]{3,2,1,0:T(8,128)(2,1)}, bf16[2,1,128,256]{3,2,1,0:T(8,128)(2,1)S(1)}, u32[]{:S(2)}, u32[]{:S(2)}) collective-permute-start(bf16[2,1,128,256]{3,2,1,0:T(8,128)(2,1)} %refs_0_.1), channel_id=1, source_target_pairs={{0,4},{2,6},{4,0},{6,2},{1,5},{3,7},{5,1},{7,3},{8,12},{10,14},{12... | collective-permute-start | bytes 393224 | tf_op jit(solution)/shard_map/ppermute | solution.py:27
  3.1 6.5 %collective-permute-start.28 = (bf16[2,1,128,256]{3,2,1,0:T(8,128)(2,1)}, bf16[2,1,128,256]{3,2,1,0:T(8,128)(2,1)S(1)}, u32[]{:S(2)}, u32[]{:S(2)}) collective-permute-start(bf16[2,1,128,256]{3,2,1,0:T(8,128)(2,1)} %refs_4_.1), channel_id=1, source_target_pairs={{0,4},{2,6},{4,0},{6,2},{1,5},{3,7},{5,1},{7,3},{8,12},{10,14},{12... | collective-permute-start | bytes 393224 | tf_op jit(solution)/shard_map/ppermute | solution.py:27
  3.1 6.4 %collective-permute-start.24 = (bf16[2,1,128,256]{3,2,1,0:T(8,128)(2,1)}, bf16[2,1,128,256]{3,2,1,0:T(8,128)(2,1)S(1)}, u32[]{:S(2)}, u32[]{:S(2)}) collective-permute-start(bf16[2,1,128,256]{3,2,1,0:T(8,128)(2,1)} %refs_0_.1), channel_id=1, source_target_pairs={{0,2},{2,0},{4,6},{6,4},{1,3},{3,1},{5,7},{7,5},{8,10},{10,8},{12,... | collective-permute-start | bytes 393224 | tf_op jit(solution)/shard_map/ppermute | solution.py:27
  3.1 8.6 %collective-permute-start = (bf16[2,1,128,256]{3,2,1,0:T(8,128)(2,1)}, bf16[2,1,128,256]{3,2,1,0:T(8,128)(2,1)S(1)}, u32[]{:S(2)}, u32[]{:S(2)}) collective-permute-start(bf16[2,1,128,256]{3,2,1,0:T(8,128)(2,1)} %refs_0_.1), channel_id=1, source_target_pairs={{0,8},{8,16},{16,24},{24,0},{1,9},{9,17},{17,25},{25,1},{2,10},{10... | collective-permute-start | bytes 393224 | tf_op jit(solution)/shard_map/ppermute | solution.py:17
  5.1 9.2 %collective-permute-start.6 = (bf16[2,1,128,256]{3,2,1,0:T(8,128)(2,1)}, bf16[2,1,128,256]{3,2,1,0:T(8,128)(2,1)S(1)}, u32[]{:S(2)}, u32[]{:S(2)}) collective-permute-start(bf16[2,1,128,256]{3,2,1,0:T(8,128)(2,1)} %refs_4_.1), channel_id=1, source_target_pairs={{0,8},{8,16},{16,24},{24,0},{1,9},{9,17},{17,25},{25,1},{2,10},{10... | collective-permute-start | bytes 393224 | tf_op jit(solution)/shard_map/ppermute | solution.py:17
  7.6 8.3 %collective-permute-start.27 = (bf16[2,1,128,256]{3,2,1,0:T(8,128)(2,1)}, bf16[2,1,128,256]{3,2,1,0:T(8,128)(2,1)S(1)}, u32[]{:S(2)}, u32[]{:S(2)}) collective-permute-start(bf16[2,1,128,256]{3,2,1,0:T(8,128)(2,1)} %refs_4_.1), channel_id=1, source_target_pairs={{0,2},{2,0},{4,6},{6,4},{1,3},{3,1},{5,7},{7,5},{8,10},{10,8},{12,... | collective-permute-start | bytes 393224 | tf_op jit(solution)/shard_map/ppermute | solution.py:27
  9.6 6.3 %collective-permute-start.26 = (bf16[2,1,128,256]{3,2,1,0:T(8,128)(2,1)S(1)}, bf16[2,1,128,256]{3,2,1,0:T(8,128)(2,1)S(1)}, u32[]{:S(2)}, u32[]{:S(2)}) collective-permute-start(bf16[2,1,128,256]{3,2,1,0:T(8,128)(2,1)S(1)} %collective-permute-done.25.refs_2_), channel_id=1, source_target_pairs={{0,2},{2,0},{4,6},{6,4},{1,3},{3,1},{5,7},{7,5},{8,10},{10,8},{12,... | collective-permute-start | bytes 393224 | tf_op jit(solution)/shard_map/ppermute | solution.py:27
  9.6 6.4 %collective-permute-start.29 = (bf16[2,1,128,256]{3,2,1,0:T(8,128)(2,1)S(1)}, bf16[2,1,128,256]{3,2,1,0:T(8,128)(2,1)S(1)}, u32[]{:S(2)}, u32[]{:S(2)}) collective-permute-start(bf16[2,1,128,256]{3,2,1,0:T(8,128)(2,1)S(1)} %collective-permute-done.28.refs_6_), channel_id=1, source_target_pairs={{0,2},{2,0},{4,6},{6,4},{1,3},{3,1},{5,7},{7,5},{8,10},{10,8},{12,... | collective-permute-start | bytes 393224 | tf_op jit(solution)/shard_map/ppermute | solution.py:27
  11.7 5.5 %collective-permute-start.19 = (bf16[2,1,128,256]{3,2,1,0:T(8,128)(2,1)S(1)}, bf16[2,1,128,256]{3,2,1,0:T(8,128)(2,1)S(1)}, u32[]{:S(2)}, u32[]{:S(2)}) collective-permute-start(bf16[2,1,128,256]{3,2,1,0:T(8,128)(2,1)S(1)} %collective-permute-done.refs_0_), channel_id=1, source_target_pairs={{0,4},{2,6},{4,0},{6,2},{1,5},{3,7},{5,1},{7,3},{8,12},{10,14},{12... | collective-permute-start | bytes 393224 | tf_op jit(solution)/shard_map/ppermute | solution.py:27
  14.3 5.3 %collective-permute-start.22 = (bf16[2,1,128,256]{3,2,1,0:T(8,128)(2,1)S(1)}, bf16[2,1,128,256]{3,2,1,0:T(8,128)(2,1)S(1)}, u32[]{:S(2)}, u32[]{:S(2)}) collective-permute-start(bf16[2,1,128,256]{3,2,1,0:T(8,128)(2,1)S(1)} %collective-permute-done.6.refs_4_), channel_id=1, source_target_pairs={{0,4},{2,6},{4,0},{6,2},{1,5},{3,7},{5,1},{7,3},{8,12},{10,14},{12... | collective-permute-start | bytes 393224 | tf_op jit(solution)/shard_map/ppermute | solution.py:27
  15.9 3.8 %collective-permute-start.18 = (bf16[2,1,128,256]{3,2,1,0:T(8,128)(2,1)S(1)}, bf16[2,1,128,256]{3,2,1,0:T(8,128)(2,1)S(1)}, u32[]{:S(2)}, u32[]{:S(2)}) collective-permute-start(bf16[2,1,128,256]{3,2,1,0:T(8,128)(2,1)S(1)} %collective-permute-done.refs_0_), channel_id=1, source_target_pairs={{0,2},{2,0},{4,6},{6,4},{1,3},{3,1},{5,7},{7,5},{8,10},{10,8},{12,... | collective-permute-start | bytes 393224 | tf_op jit(solution)/shard_map/ppermute | solution.py:27
  15.9 8.2 %collective-permute-start.1 = (bf16[2,1,128,256]{3,2,1,0:T(8,128)(2,1)S(1)}, bf16[2,1,128,256]{3,2,1,0:T(8,128)(2,1)S(1)}, u32[]{:S(2)}, u32[]{:S(2)}) collective-permute-start(bf16[2,1,128,256]{3,2,1,0:T(8,128)(2,1)S(1)} %collective-permute-done.refs_0_), channel_id=1, source_target_pairs={{0,8},{8,16},{16,24},{24,0},{1,9},{9,17},{17,25},{25,1},{2,10},{10... | collective-permute-start | bytes 393224 | tf_op jit(solution)/shard_map/ppermute | solution.py:17
  16.0 10.4 %collective-permute-start.7 = (bf16[2,1,128,256]{3,2,1,0:T(8,128)(2,1)S(1)}, bf16[2,1,128,256]{3,2,1,0:T(8,128)(2,1)S(1)}, u32[]{:S(2)}, u32[]{:S(2)}) collective-permute-start(bf16[2,1,128,256]{3,2,1,0:T(8,128)(2,1)S(1)} %collective-permute-done.6.refs_4_), channel_id=1, source_target_pairs={{0,8},{8,16},{16,24},{24,0},{1,9},{9,17},{17,25},{25,1},{2,10},{10... | collective-permute-start | bytes 393224 | tf_op jit(solution)/shard_map/ppermute | solution.py:17
  17.2 9.7 %collective-permute-start.21 = (bf16[2,1,128,256]{3,2,1,0:T(8,128)(2,1)S(1)}, bf16[2,1,128,256]{3,2,1,0:T(8,128)(2,1)S(1)}, u32[]{:S(2)}, u32[]{:S(2)}) collective-permute-start(bf16[2,1,128,256]{3,2,1,0:T(8,128)(2,1)S(1)} %collective-permute-done.6.refs_4_), channel_id=1, source_target_pairs={{0,2},{2,0},{4,6},{6,4},{1,3},{3,1},{5,7},{7,5},{8,10},{10,8},{12,... | collective-permute-start | bytes 393224 | tf_op jit(solution)/shard_map/ppermute | solution.py:27
  19.7 7.2 %collective-permute-start.20 = (bf16[2,1,128,256]{3,2,1,0:T(8,128)(2,1)S(1)}, bf16[2,1,128,256]{3,2,1,0:T(8,128)(2,1)S(1)}, u32[]{:S(2)}, u32[]{:S(2)}) collective-permute-start(bf16[2,1,128,256]{3,2,1,0:T(8,128)(2,1)S(1)} %collective-permute-done.19.refs_2_), channel_id=1, source_target_pairs={{0,2},{2,0},{4,6},{6,4},{1,3},{3,1},{5,7},{7,5},{8,10},{10,8},{12,... | collective-permute-start | bytes 393224 | tf_op jit(solution)/shard_map/ppermute | solution.py:27
  19.7 7.3 %collective-permute-start.23 = (bf16[2,1,128,256]{3,2,1,0:T(8,128)(2,1)S(1)}, bf16[2,1,128,256]{3,2,1,0:T(8,128)(2,1)S(1)}, u32[]{:S(2)}, u32[]{:S(2)}) collective-permute-start(bf16[2,1,128,256]{3,2,1,0:T(8,128)(2,1)S(1)} %collective-permute-done.22.refs_6_), channel_id=1, source_target_pairs={{0,2},{2,0},{4,6},{6,4},{1,3},{3,1},{5,7},{7,5},{8,10},{10,8},{12,... | collective-permute-start | bytes 393224 | tf_op jit(solution)/shard_map/ppermute | solution.py:27
  24.0 5.3 %collective-permute-start.13 = (bf16[2,1,128,256]{3,2,1,0:T(8,128)(2,1)S(1)}, bf16[2,1,128,256]{3,2,1,0:T(8,128)(2,1)S(1)}, u32[]{:S(2)}, u32[]{:S(2)}) collective-permute-start(bf16[2,1,128,256]{3,2,1,0:T(8,128)(2,1)S(1)} %collective-permute-done.1.refs_0_), channel_id=1, source_target_pairs={{0,4},{2,6},{4,0},{6,2},{1,5},{3,7},{5,1},{7,3},{8,12},{10,14},{12... | collective-permute-start | bytes 393224 | tf_op jit(solution)/shard_map/ppermute | solution.py:27
  26.4 5.4 %collective-permute-start.16 = (bf16[2,1,128,256]{3,2,1,0:T(8,128)(2,1)S(1)}, bf16[2,1,128,256]{3,2,1,0:T(8,128)(2,1)S(1)}, u32[]{:S(2)}, u32[]{:S(2)}) collective-permute-start(bf16[2,1,128,256]{3,2,1,0:T(8,128)(2,1)S(1)} %collective-permute-done.7.refs_4_), channel_id=1, source_target_pairs={{0,4},{2,6},{4,0},{6,2},{1,5},{3,7},{5,1},{7,3},{8,12},{10,14},{12... | collective-permute-start | bytes 393224 | tf_op jit(solution)/shard_map/ppermute | solution.py:27
  26.9 8.0 %collective-permute-start.8 = (bf16[2,1,128,256]{3,2,1,0:T(8,128)(2,1)S(1)}, bf16[2,1,128,256]{3,2,1,0:T(8,128)(2,1)S(1)}, u32[]{:S(2)}, u32[]{:S(2)}) collective-permute-start(bf16[2,1,128,256]{3,2,1,0:T(8,128)(2,1)S(1)} %collective-permute-done.7.refs_4_), channel_id=1, source_target_pairs={{0,8},{8,16},{16,24},{24,0},{1,9},{9,17},{17,25},{25,1},{2,10},{10... | collective-permute-start | bytes 393224 | tf_op jit(solution)/shard_map/ppermute | solution.py:17
  26.9 9.5 %collective-permute-start.2 = (bf16[2,1,128,256]{3,2,1,0:T(8,128)(2,1)S(1)}, bf16[2,1,128,256]{3,2,1,0:T(8,128)(2,1)S(1)}, u32[]{:S(2)}, u32[]{:S(2)}) collective-permute-start(bf16[2,1,128,256]{3,2,1,0:T(8,128)(2,1)S(1)} %collective-permute-done.1.refs_0_), channel_id=1, source_target_pairs={{0,8},{8,16},{16,24},{24,0},{1,9},{9,17},{17,25},{25,1},{2,10},{10... | collective-permute-start | bytes 393224 | tf_op jit(solution)/shard_map/ppermute | solution.py:17
  27.0 12.2 %collective-permute-start.12 = (bf16[2,1,128,256]{3,2,1,0:T(8,128)(2,1)S(1)}, bf16[2,1,128,256]{3,2,1,0:T(8,128)(2,1)S(1)}, u32[]{:S(2)}, u32[]{:S(2)}) collective-permute-start(bf16[2,1,128,256]{3,2,1,0:T(8,128)(2,1)S(1)} %collective-permute-done.1.refs_0_), channel_id=1, source_target_pairs={{0,2},{2,0},{4,6},{6,4},{1,3},{3,1},{5,7},{7,5},{8,10},{10,8},{12,... | collective-permute-start | bytes 393224 | tf_op jit(solution)/shard_map/ppermute | solution.py:27
  29.3 14.7 %collective-permute-start.15 = (bf16[2,1,128,256]{3,2,1,0:T(8,128)(2,1)S(1)}, bf16[2,1,128,256]{3,2,1,0:T(8,128)(2,1)S(1)}, u32[]{:S(2)}, u32[]{:S(2)}) collective-permute-start(bf16[2,1,128,256]{3,2,1,0:T(8,128)(2,1)S(1)} %collective-permute-done.7.refs_4_), channel_id=1, source_target_pairs={{0,2},{2,0},{4,6},{6,4},{1,3},{3,1},{5,7},{7,5},{8,10},{10,8},{12,... | collective-permute-start | bytes 393224 | tf_op jit(solution)/shard_map/ppermute | solution.py:27
  31.8 13.8 %collective-permute-start.14 = (bf16[2,1,128,256]{3,2,1,0:T(8,128)(2,1)S(1)}, bf16[2,1,128,256]{3,2,1,0:T(8,128)(2,1)S(1)}, u32[]{:S(2)}, u32[]{:S(2)}) collective-permute-start(bf16[2,1,128,256]{3,2,1,0:T(8,128)(2,1)S(1)} %collective-permute-done.13.refs_2_), channel_id=1, source_target_pairs={{0,2},{2,0},{4,6},{6,4},{1,3},{3,1},{5,7},{7,5},{8,10},{10,8},{12,... | collective-permute-start | bytes 393224 | tf_op jit(solution)/shard_map/ppermute | solution.py:27
  34.9 10.8 %collective-permute-start.10 = (bf16[2,1,128,256]{3,2,1,0:T(8,128)(2,1)S(1)}, bf16[2,1,128,256]{3,2,1,0:T(8,128)(2,1)S(1)}, u32[]{:S(2)}, u32[]{:S(2)}) collective-permute-start(bf16[2,1,128,256]{3,2,1,0:T(8,128)(2,1)S(1)} %collective-permute-done.8.refs_4_), channel_id=1, source_target_pairs={{0,4},{2,6},{4,0},{6,2},{1,5},{3,7},{5,1},{7,3},{8,12},{10,14},{12... | collective-permute-start | bytes 393224 | tf_op jit(solution)/shard_map/ppermute | solution.py:27
  36.4 9.7 %collective-permute-start.4 = (bf16[2,1,128,256]{3,2,1,0:T(8,128)(2,1)S(1)}, bf16[2,1,128,256]{3,2,1,0:T(8,128)(2,1)S(1)}, u32[]{:S(2)}, u32[]{:S(2)}) collective-permute-start(bf16[2,1,128,256]{3,2,1,0:T(8,128)(2,1)S(1)} %collective-permute-done.2.refs_0_), channel_id=1, source_target_pairs={{0,4},{2,6},{4,0},{6,2},{1,5},{3,7},{5,1},{7,3},{8,12},{10,14},{12... | collective-permute-start | bytes 393224 | tf_op jit(solution)/shard_map/ppermute | solution.py:27
  39.2 11.7 %collective-permute-start.17 = (bf16[2,1,128,256]{3,2,1,0:T(8,128)(2,1)S(1)}, bf16[2,1,128,256]{3,2,1,0:T(8,128)(2,1)S(1)}, u32[]{:S(2)}, u32[]{:S(2)}) collective-permute-start(bf16[2,1,128,256]{3,2,1,0:T(8,128)(2,1)S(1)} %collective-permute-done.16.refs_6_), channel_id=1, source_target_pairs={{0,2},{2,0},{4,6},{6,4},{1,3},{3,1},{5,7},{7,5},{8,10},{10,8},{12,... | collective-permute-start | bytes 393224 | tf_op jit(solution)/shard_map/ppermute | solution.py:27
  42.7 1.4 %copy-start = (f32[2,2,1024,128]{3,2,1,0:T(8,128)}, f32[2,2,1024,128]{3,2,1,0:T(8,128)S(1)}, u32[]{:S(2)}) copy-start(f32[2,2,1024,128]{3,2,1,0:T(8,128)S(1)} %get-tuple-element.16.refs_10_) | copy-start | bytes 6291460
  44.0 12.3 %collective-permute-start.3 = (bf16[2,1,128,256]{3,2,1,0:T(8,128)(2,1)S(1)}, bf16[2,1,128,256]{3,2,1,0:T(8,128)(2,1)S(1)}, u32[]{:S(2)}, u32[]{:S(2)}) collective-permute-start(bf16[2,1,128,256]{3,2,1,0:T(8,128)(2,1)S(1)} %collective-permute-done.2.refs_0_), channel_id=1, source_target_pairs={{0,2},{2,0},{4,6},{6,4},{1,3},{3,1},{5,7},{7,5},{8,10},{10,8},{12,... | collective-permute-start | bytes 393224 | tf_op jit(solution)/shard_map/ppermute | solution.py:27
  45.6 10.7 %collective-permute-start.9 = (bf16[2,1,128,256]{3,2,1,0:T(8,128)(2,1)S(1)}, bf16[2,1,128,256]{3,2,1,0:T(8,128)(2,1)S(1)}, u32[]{:S(2)}, u32[]{:S(2)}) collective-permute-start(bf16[2,1,128,256]{3,2,1,0:T(8,128)(2,1)S(1)} %collective-permute-done.8.refs_4_), channel_id=1, source_target_pairs={{0,2},{2,0},{4,6},{6,4},{1,3},{3,1},{5,7},{7,5},{8,10},{10,8},{12,... | collective-permute-start | bytes 393224 | tf_op jit(solution)/shard_map/ppermute | solution.py:27
  45.7 10.7 %collective-permute-start.11 = (bf16[2,1,128,256]{3,2,1,0:T(8,128)(2,1)S(1)}, bf16[2,1,128,256]{3,2,1,0:T(8,128)(2,1)S(1)}, u32[]{:S(2)}, u32[]{:S(2)}) collective-permute-start(bf16[2,1,128,256]{3,2,1,0:T(8,128)(2,1)S(1)} %collective-permute-done.10.refs_6_), channel_id=1, source_target_pairs={{0,2},{2,0},{4,6},{6,4},{1,3},{3,1},{5,7},{7,5},{8,10},{10,8},{12,... | collective-permute-start | bytes 393224 | tf_op jit(solution)/shard_map/ppermute | solution.py:27
  46.1 10.2 %collective-permute-start.5 = (bf16[2,1,128,256]{3,2,1,0:T(8,128)(2,1)S(1)}, bf16[2,1,128,256]{3,2,1,0:T(8,128)(2,1)S(1)}, u32[]{:S(2)}, u32[]{:S(2)}) collective-permute-start(bf16[2,1,128,256]{3,2,1,0:T(8,128)(2,1)S(1)} %collective-permute-done.4.refs_2_), channel_id=1, source_target_pairs={{0,2},{2,0},{4,6},{6,4},{1,3},{3,1},{5,7},{7,5},{8,10},{10,8},{12,... | collective-permute-start | bytes 393224 | tf_op jit(solution)/shard_map/ppermute | solution.py:27
  49.5 1.4 %copy-start.1 = (f32[2,2,1024,128]{3,2,1,0:T(8,128)}, f32[2,2,1024,128]{3,2,1,0:T(8,128)S(1)}, u32[]{:S(2)}) copy-start(f32[2,2,1024,128]{3,2,1,0:T(8,128)S(1)} %get-tuple-element.19.refs_10_) | copy-start | bytes 6291460

commit v3 on v2

--- a/solution.py
+++ b/solution.py
@@ -11,6 +11,7 @@
 HEAD_DIM = 128
 MASKED = -1e30
 STAGES = 4
+REACH = 3
 
 
 def shift(array, axis, size, step):
@@ -31,18 +32,24 @@
     return lax.dot_general(a, b, (((1,), (b_dim,)), ((), ())), preferred_element_type=jnp.float32)
 
 
-def attend_stage(plan, first, last, order_ref, mask_ref, q_ref, *refs):
+def attend_stage(plan, first, last, order_ref, mask_ref, q_in, *refs):
     pb, ka, cores, places = plan
     count = len(places)
-    keys, values = refs[:count], refs[count : 2 * count]
-    refs = refs[2 * count :]
+    pieces, refs = refs[:count], refs[count:]
     if not first:
         old_refs, refs = refs[:3], refs[3:]
+    if not last:
+        refs = refs[1:]
+    if first:
+        q_ref, refs = refs[0], refs[1:]
+    else:
+        q_ref = q_in
     if last:
         out_ref, refs = refs[0], refs[1:]
     acc, top, total, k_pool, v_pool, bias = refs[:6]
     own_slots, kv_local, rows, _ = acc.shape
-    held, _, block_rows, _ = keys[0].shape
+    held, block_rows, _ = pieces[0].shape
+    held = held // 2
     group = rows // block_rows
     rings = ka // cores
     p_at, k_at = lax.axis_index("pb"), lax.axis_index("ka")
@@ -60,6 +67,11 @@
                 blocks.append((source * class_local + t) * ka + ring * cores + core)
 
     if first:
+        own_rows = own_slots * block_rows
+        q_copy = pltpu.make_async_copy(
+            q_in.at[pl.ds(pl.multiple_of(k_at * own_rows, block_rows), own_rows)], q_ref, refs[6]
+        )
+        q_copy.start()
         acc[...] = jnp.zeros(acc.shape, acc.dtype)
         total[...] = jnp.zeros(total.shape, total.dtype)
         top[...] = jnp.full(top.shape, MASKED, top.dtype)
@@ -67,6 +79,8 @@
         for new, old in zip((acc, top, total), old_refs):
             new[...] = old[...]
 
+    if first:
+        q_copy.wait()
     row_id = lax.broadcasted_iota(jnp.int32, (block_rows, block_rows), 0)
     col_id = lax.broadcasted_iota(jnp.int32, (block_rows, block_rows), 1)
 
@@ -84,8 +98,8 @@
 
             @pl.when(listed[at] == 1)
             def _():
-                k_pool[place] = keys[piece][t, 0]
-                v_pool[place] = values[piece][t, 0]
+                k_pool[place] = pieces[piece][t]
+                v_pool[place] = pieces[piece][held + t]
 
             done = done + jnp.where(is_own, 0, listed[at])
             has_own = has_own + jnp.where(is_own, listed[at], 0)
@@ -175,68 +189,78 @@
     group = width // kv_width
     own_slots = queries.shape[0] // block_rows // ka
     own_rows = own_slots * block_rows
-    own_queries = lax.dynamic_slice_in_dim(
-        queries, lax.axis_index("ka") * own_rows, own_rows, axis=0
-    )
-
     state_shape = jax.ShapeDtypeStruct((own_slots, kv_local, group * block_rows, HEAD_DIM), jnp.float32)
     vmem = pl.BlockSpec(memory_space=pltpu.VMEM)
     smem = pl.BlockSpec(memory_space=pltpu.SMEM)
+    hbm = pl.BlockSpec(memory_space=pltpu.HBM)
     stages = min(STAGES, pb)
     sources = pb // stages
-    near = (keys, values)
-    state = ()
+    q_shape = jax.ShapeDtypeStruct((own_rows, width), queries.dtype)
+    own = jnp.concatenate([keys, values], axis=0)
+    own = own.reshape(own.shape[0], block_rows, kv_width)
+    nears = [own]
+    for z in range(1, pb):
+        hop = (z - 1) % REACH + 1
+        nears.append(shift(nears[z - hop], "pb", pb, hop))
+    rings_of = []
     for stage in range(stages):
-        places, pieces, nears = [], [], []
+        nears_here = nears[stage * sources : (stage + 1) * sources]
+        if sources == 1:
+            rings_of.append(nears_here[0])
+        else:
+            rings_of.append(
+                jnp.concatenate(
+                    [array[:class_local] for array in nears_here]
+                    + [array[class_local:] for array in nears_here],
+                    axis=0,
+                )
+            )
+
+    state, own_queries = (), queries
+    for stage in range(stages):
         hops = range(stage * sources, (stage + 1) * sources)
-        for z in hops:
-            if z:
-                near = tuple(shift(array, "pb", pb, 1) for array in near)
-            nears.append(near)
-        ring = nears[0]
-        if sources > 1:
-            ring = tuple(jnp.concatenate(arrays, axis=0) for arrays in zip(*nears))
+        places, pieces = [], []
+        ring = rings_of[stage]
         for y in range(rings):
             if y:
-                ring = tuple(turn(array, ka, cores, 1, 0) for array in ring)
+                ring = turn(ring, ka, cores, 1, 0)
             here = ring
             for c in range(cores):
                 if c:
-                    here = tuple(turn(array, ka, cores, 0, 1) for array in here)
+                    here = turn(here, ka, cores, 0, 1)
                 places.append((hops, y, c))
                 pieces.append(here)
         first, last = stage == 0, stage == stages - 1
+        ahead = [] if last else [rings_of[stage + 1]]
         held = len(places) * sources * class_local
         held += held % 2
-        pools = [pltpu.VMEM((held, block_rows, kv_width), jnp.bfloat16)] * 2
-        pools.append(pltpu.VMEM((block_rows, 2 * block_rows), jnp.float32))
+        scratch = [pltpu.VMEM((held, block_rows, kv_width), jnp.bfloat16)] * 2
+        scratch.append(pltpu.VMEM((block_rows, 2 * block_rows), jnp.float32))
+        if first:
+            scratch.append(pltpu.SemaphoreType.DMA)
         if last:
-            outs = jax.ShapeDtypeStruct((own_rows, width), jnp.bfloat16)
-            out_specs = vmem
-            scratch = [pltpu.VMEM(state_shape.shape, state_shape.dtype)] * 3 + pools
+            outs = [q_shape]
+            scratch = [pltpu.VMEM(state_shape.shape, state_shape.dtype)] * 3 + scratch
         else:
-            outs = (state_shape,) * 3
-            out_specs = (vmem,) * 3
-            scratch = pools
-        state = pl.pallas_call(
+            outs = [q_shape] * first + [state_shape] * 3
+        results = pl.pallas_call(
             functools.partial(attend_stage, (pb, ka, cores, places), first, last),
             out_shape=outs,
-            in_specs=[smem] * 2 + [vmem] * (1 + 2 * len(places) + len(state)),
-            out_specs=out_specs,
+            in_specs=[smem] * 2
+            + [hbm if first else vmem]
+            + [vmem] * (len(places) + len(state))
+            + [pl.BlockSpec(memory_space=pl.ANY)] * len(ahead),
+            out_specs=[vmem] * len(outs),
             scratch_shapes=scratch,
-            compiler_params=pltpu.CompilerParams(vmem_limit_bytes=40 * 1024 * 1024),
+            compiler_params=pltpu.CompilerParams(vmem_limit_bytes=20 * 1024 * 1024),
             cost_estimate=pl.CostEstimate(
-                flops=2**30, bytes_accessed=2**22, transcendentals=2**20
+                flops=2**31, bytes_accessed=2**22, transcendentals=2**20
             ),
-        )(
-            q_order,
-            block_mask,
-            own_queries,
-            *[piece[0] for piece in pieces],
-            *[piece[1] for piece in pieces],
-            *state,
-        )
-    return state
+        )(q_order, block_mask, own_queries, *pieces, *state, *ahead)
+        if first:
+            own_queries, results = results[0], results[1:]
+        state = results
+    return state[0]
 
 
 def solution(mesh):

time: 61.7 us -> 57.2 us (0.927)
  the two profiles are of different devices: /device:TPU:0 before, /device:TPU:21 now
where the time goes in v3:
time: 57.2 us; the launch traced here: 56.4 us
  starting transfers between devices  31.8 us (56%)
  Pallas kernels  15.4 us (27%)
  waiting for transfers between devices  4.62 us (8%)
  local copies, waits for them, and re-layouts  3.53 us (6%)
  other arithmetic  0.99 us (2%)
    ppermute x12, starting transfers between devices, turn(): return lax.ppermute(array, 'ka', pairs)  29.5 us
    pallas_call x4, Pallas kernels, on_device(): pl.pallas_call(functools.partial(attend_stage, (pb, ka, cores, places), f...  15.4 us
    ppermute x3, waiting for transfers between devices, shift(): lax.ppermute(array, axis, [(i, (i + step) % size) for i in range(size)])  3.95 us
    unnamed x6, local copies, waits for them, and re-layouts  3.53 us
    ppermute x3, starting transfers between devices, shift(): lax.ppermute(array, axis, [(i, (i + step) % size) for i in range(size)])  2.33 us
  transfers between devices with their start and end apart: 15, of which 3 were waited for; matrix products, arithmetic and copies ran while one was open for 0% of the time, Pallas kernels for 22%

profile of v3, /device:TPU:21, one launch (start us, length us, event | category | flops | bytes accessed | tf_op | source)
XLA Modules:
  0.0 56.4 jit_solution(2419353832068079852)
XLA Ops:
  0.0 1.0 %maximum_bitcast_fusion.refs_0_ = bf16[4,128,256]{2,1,0:T(8,128)(2,1)S(1)} fusion(bf16[2,1,128,256]{3,2,0,1:T(8,128)(2,1)} %bitcast.4, bf16[2,1,128,256]{3,2,0,1:T(8,128)(2,1)} %bitcast.5), kind=kLoop, calls=%fused_computation | loop fusion | flops 131072 | bytes 524288 | tf_op jit(solution)/shard_map/reshape | solution.py:200
  1.0 1.3 %collective-permute-start.3 = (bf16[4,128,256]{2,1,0:T(8,128)(2,1)S(1)}, bf16[4,128,256]{2,1,0:T(8,128)(2,1)S(1)}, u32[]{:S(2)}, u32[]{:S(2)}) collective-permute-start(bf16[4,128,256]{2,1,0:T(8,128)(2,1)S(1)} %maximum_bitcast_fusion.refs_0_), channel_id=1, source_target_pairs={{0,8},{8,16},{16,24},{24,0},{1,9},{9,17},{17,25},{25,1},{2,10},{10... | collective-permute-start | bytes 786440 | tf_op jit(solution)/shard_map/ppermute | solution.py:18
  2.3 0.2 collective-permute-start.1
  2.6 0.1 collective-permute-start.8
  2.6 1.5 %collective-permute-start = (bf16[4,128,256]{2,1,0:T(8,128)(2,1)S(1)}, bf16[4,128,256]{2,1,0:T(8,128)(2,1)S(1)}, u32[]{:S(2)}, u32[]{:S(2)}) collective-permute-start(bf16[4,128,256]{2,1,0:T(8,128)(2,1)S(1)} %maximum_bitcast_fusion.refs_0_), channel_id=1, source_target_pairs={{0,2},{2,0},{4,6},{6,4},{1,3},{3,1},{5,7},{7,5},{8,10},{10,8},{12,... | collective-permute-start | bytes 786440 | tf_op jit(solution)/shard_map/ppermute | solution.py:28
  4.1 0.9 %collective-permute-start.4 = (bf16[4,128,256]{2,1,0:T(8,128)(2,1)S(1)}, bf16[4,128,256]{2,1,0:T(8,128)(2,1)S(1)}, u32[]{:S(2)}, u32[]{:S(2)}) collective-permute-start(bf16[4,128,256]{2,1,0:T(8,128)(2,1)S(1)} %maximum_bitcast_fusion.refs_0_), channel_id=1, source_target_pairs={{0,24},{8,0},{16,8},{24,16},{1,25},{9,1},{17,9},{25,17},{2,26},{10... | collective-permute-start | bytes 786440 | tf_op jit(solution)/shard_map/ppermute | solution.py:18
  5.1 3.3 %collective-permute-done.3.refs_4_.refs_0_ = bf16[4,128,256]{2,1,0:T(8,128)(2,1)S(1)} collective-permute-done((bf16[4,128,256]{2,1,0:T(8,128)(2,1)S(1)}, bf16[4,128,256]{2,1,0:T(8,128)(2,1)S(1)}, u32[]{:S(2)}, u32[]{:S(2)}) %collective-permute-start.3) | collective-permute-done | bytes 262176 | tf_op jit(solution)/shard_map/ppermute | solution.py:18
  8.3 0.2 collective-permute-start.13
  8.6 0.6 %collective-permute-done.1.refs_2_ = bf16[4,128,256]{2,1,0:T(8,128)(2,1)S(1)} collective-permute-done((bf16[4,128,256]{2,1,0:T(8,128)(2,1)S(1)}, bf16[4,128,256]{2,1,0:T(8,128)(2,1)S(1)}, u32[]{:S(2)}, u32[]{:S(2)}) %collective-permute-start.1) | collective-permute-done | bytes 262176 | tf_op jit(solution)/shard_map/ppermute | solution.py:28
  9.2 13.5 %collective-permute-start.2 = (bf16[4,128,256]{2,1,0:T(8,128)(2,1)S(1)}, bf16[4,128,256]{2,1,0:T(8,128)(2,1)S(1)}, u32[]{:S(2)}, u32[]{:S(2)}) collective-permute-start(bf16[4,128,256]{2,1,0:T(8,128)(2,1)S(1)} %collective-permute-done.1.refs_2_), channel_id=1, source_target_pairs={{0,2},{2,0},{4,6},{6,4},{1,3},{3,1},{5,7},{7,5},{8,10},{10,8},{12,... | collective-permute-start | bytes 786440 | tf_op jit(solution)/shard_map/ppermute | solution.py:28
  22.7 0.0 collective-permute-done.8.refs_7_.refs_0_
  22.7 1.2 %collective-permute-start.10 = (bf16[4,128,256]{2,1,0:T(8,128)(2,1)S(1)}, bf16[4,128,256]{2,1,0:T(8,128)(2,1)S(1)}, u32[]{:S(2)}, u32[]{:S(2)}) collective-permute-start(bf16[4,128,256]{2,1,0:T(8,128)(2,1)S(1)} %collective-permute-done.8.refs_7_.refs_0_), channel_id=1, source_target_pairs={{0,4},{2,6},{4,0},{6,2},{1,5},{3,7},{5,1},{7,3},{8,12},{10,14},{12... | collective-permute-start | bytes 786440 | tf_op jit(solution)/shard_map/ppermute | solution.py:28
  23.9 0.0 collective-permute-done.refs_1_
  23.9 0.3 collective-permute-start.12
  24.3 0.7 %collective-permute-done.4.refs_7_.refs_0_ = bf16[4,128,256]{2,1,0:T(8,128)(2,1)S(1)} collective-permute-done((bf16[4,128,256]{2,1,0:T(8,128)(2,1)S(1)}, bf16[4,128,256]{2,1,0:T(8,128)(2,1)S(1)}, u32[]{:S(2)}, u32[]{:S(2)}) %collective-permute-start.4) | collective-permute-done | bytes 262176 | tf_op jit(solution)/shard_map/ppermute | solution.py:18
  24.9 0.2 collective-permute-start.6
  25.2 0.0 collective-permute-done.13.refs_2_
  25.2 6.1 %collective-permute-start.14 = (bf16[4,128,256]{2,1,0:T(8,128)(2,1)S(1)}, bf16[4,128,256]{2,1,0:T(8,128)(2,1)S(1)}, u32[]{:S(2)}, u32[]{:S(2)}) collective-permute-start(bf16[4,128,256]{2,1,0:T(8,128)(2,1)S(1)} %collective-permute-done.13.refs_2_), channel_id=1, source_target_pairs={{0,2},{2,0},{4,6},{6,4},{1,3},{3,1},{5,7},{7,5},{8,10},{10,8},{12,... | collective-permute-start | bytes 786440 | tf_op jit(solution)/shard_map/ppermute | solution.py:28
  31.3 0.0 collective-permute-done.2.refs_3_
  31.3 0.0 collective-permute-start.9
  31.3 0.0 collective-permute-done.10.refs_2_
  31.3 5.6 %collective-permute-start.11 = (bf16[4,128,256]{2,1,0:T(8,128)(2,1)S(1)}, bf16[4,128,256]{2,1,0:T(8,128)(2,1)S(1)}, u32[]{:S(2)}, u32[]{:S(2)}) collective-permute-start(bf16[4,128,256]{2,1,0:T(8,128)(2,1)S(1)} %collective-permute-done.10.refs_2_), channel_id=1, source_target_pairs={{0,2},{2,0},{4,6},{6,4},{1,3},{3,1},{5,7},{7,5},{8,10},{10,8},{12,... | collective-permute-start | bytes 786440 | tf_op jit(solution)/shard_map/ppermute | solution.py:28
  36.9 0.0 copy-start
  36.9 0.7 %copy-done = s32[8,32]{1,0:T(8,128)S(1)} copy-done((s32[8,32]{1,0:T(8,128)S(1)}, s32[8,32]{1,0:T(8,128)}, u32[]{:S(2)}) %copy-start) | copy-done | bytes 1048
  37.6 0.0 copy-start.1
  37.6 0.7 %copy-done.1 = s32[8]{0:T(128)S(1)} copy-done((s32[8]{0:T(128)S(1)}, s32[8]{0:T(128)}, u32[]{:S(2)}) %copy-start.1) | copy-done | bytes 56
  38.2 0.0 copy-start.2
  38.2 2.2 %copy-done.2 = bf16[1024,2048]{1,0:T(8,128)(2,1)S(1)} copy-done((bf16[1024,2048]{1,0:T(8,128)(2,1)S(1)}, bf16[1024,2048]{1,0:T(8,128)(2,1)}, u32[]{:S(2)}) %copy-start.2) | copy-done | bytes 4194328
  40.4 2.4 %shard_map.55 = (bf16[256,2048]{1,0:T(8,128)(2,1)S(1)}, f32[2,2,1024,128]{3,2,1,0:T(8,128)S(1)}, f32[2,2,1024,128]{3,2,1,0:T(8,128)S(1)}, f32[2,2,1024,128]{3,2,1,0:T(8,128)S(1)}) custom-call(s32[8]{0:T(128)S(1)} %copy-done.1, s32[8,32]{1,0:T(8,128)S(1)} %copy-done, bf16[1024,2048]{1,0:T(8,128)(2,1)S(1)} %copy-done.2, ...), custom_call_target="tpu_custom_call" | custom-call | flops 2147483648 | bytes 4194304 | tf_op jit(solution)/shard_map/pallas_call | solution.py:246
  42.8 0.0 collective-permute-done.12.refs_1_
  42.9 0.1 collective-permute-start.5
  42.9 0.0 collective-permute-done.6.refs_2_
  42.9 0.5 collective-permute-start.7
  43.4 0.0 collective-permute-done.14.refs_3_
  43.4 4.5 %shard_map.56 = (f32[2,2,1024,128]{3,2,1,0:T(8,128)S(1)}, f32[2,2,1024,128]{3,2,1,0:T(8,128)S(1)}, f32[2,2,1024,128]{3,2,1,0:T(8,128)S(1)}) custom-call(s32[8]{0:T(128)S(1)} %copy-done.1, s32[8,32]{1,0:T(8,128)S(1)} %copy-done, bf16[256,2048]{1,0:T(8,128)(2,1)S(1)} %get-tuple-element.15.q_in, ...), custom_call_target="tpu_custom_call" | custom-call | flops 2147483648 | bytes 4194304 | tf_op jit(solution)/shard_map/pallas_call | solution.py:246
  47.9 0.0 collective-permute-done.9.refs_1_
  47.9 0.0 collective-permute-done.11.refs_3_
  48.0 5.6 %shard_map.57 = (f32[2,2,1024,128]{3,2,1,0:T(8,128)S(1)}, f32[2,2,1024,128]{3,2,1,0:T(8,128)S(1)}, f32[2,2,1024,128]{3,2,1,0:T(8,128)S(1)}) custom-call(s32[8]{0:T(128)S(1)} %copy-done.1, s32[8,32]{1,0:T(8,128)S(1)} %copy-done, bf16[256,2048]{1,0:T(8,128)(2,1)S(1)} %get-tuple-element.15.q_in, ...), custom_call_target="tpu_custom_call" | custom-call | flops 2147483648 | bytes 4194304 | tf_op jit(solution)/shard_map/pallas_call | solution.py:246
  53.6 0.0 collective-permute-done.5.refs_1_
  53.6 0.0 collective-permute-done.7.refs_3_
  53.6 2.8 %shard_map.58 = bf16[256,2048]{1,0:T(8,128)(2,1)} custom-call(s32[8]{0:T(128)S(1)} %copy-done.1, s32[8,32]{1,0:T(8,128)S(1)} %copy-done, bf16[256,2048]{1,0:T(8,128)(2,1)S(1)} %get-tuple-element.15.q_in, bf16[4,128,256]{2,1,0:T(8,128)(2,1)S(1)} %collective-permute-done.4.refs_7_.refs_0_, bf16[4,128,256]{2,1,0:T(8,128)(2,1)S(1)} %collective-permute-done.5.refs_1_, ...), custom_call_target="tpu_custom_call" | custom-call | flops 2147483648 | bytes 4194304 | tf_op jit(solution)/shard_map/pallas_call | solution.py:246
Async XLA Ops:
  1.0 7.3 %collective-permute-start.3 = (bf16[4,128,256]{2,1,0:T(8,128)(2,1)S(1)}, bf16[4,128,256]{2,1,0:T(8,128)(2,1)S(1)}, u32[]{:S(2)}, u32[]{:S(2)}) collective-permute-start(bf16[4,128,256]{2,1,0:T(8,128)(2,1)S(1)} %maximum_bitcast_fusion.refs_0_), channel_id=1, source_target_pairs={{0,8},{8,16},{16,24},{24,0},{1,9},{9,17},{17,25},{25,1},{2,10},{10... | collective-permute-start | bytes 786440 | tf_op jit(solution)/shard_map/ppermute | solution.py:18
  2.3 6.9 %collective-permute-start.1 = (bf16[4,128,256]{2,1,0:T(8,128)(2,1)S(1)}, bf16[4,128,256]{2,1,0:T(8,128)(2,1)S(1)}, u32[]{:S(2)}, u32[]{:S(2)}) collective-permute-start(bf16[4,128,256]{2,1,0:T(8,128)(2,1)S(1)} %maximum_bitcast_fusion.refs_0_), channel_id=1, source_target_pairs={{0,4},{2,6},{4,0},{6,2},{1,5},{3,7},{5,1},{7,3},{8,12},{10,14},{12... | collective-permute-start | bytes 786440 | tf_op jit(solution)/shard_map/ppermute | solution.py:28
  2.6 20.1 %collective-permute-start.8 = (bf16[4,128,256]{2,1,0:T(8,128)(2,1)S(1)}, bf16[4,128,256]{2,1,0:T(8,128)(2,1)S(1)}, u32[]{:S(2)}, u32[]{:S(2)}) collective-permute-start(bf16[4,128,256]{2,1,0:T(8,128)(2,1)S(1)} %maximum_bitcast_fusion.refs_0_), channel_id=1, source_target_pairs={{0,16},{8,24},{16,0},{24,8},{1,17},{9,25},{17,1},{25,9},{2,18},{10... | collective-permute-start | bytes 786440 | tf_op jit(solution)/shard_map/ppermute | solution.py:18
  2.6 21.3 %collective-permute-start = (bf16[4,128,256]{2,1,0:T(8,128)(2,1)S(1)}, bf16[4,128,256]{2,1,0:T(8,128)(2,1)S(1)}, u32[]{:S(2)}, u32[]{:S(2)}) collective-permute-start(bf16[4,128,256]{2,1,0:T(8,128)(2,1)S(1)} %maximum_bitcast_fusion.refs_0_), channel_id=1, source_target_pairs={{0,2},{2,0},{4,6},{6,4},{1,3},{3,1},{5,7},{7,5},{8,10},{10,8},{12,... | collective-permute-start | bytes 786440 | tf_op jit(solution)/shard_map/ppermute | solution.py:28
  4.1 20.8 %collective-permute-start.4 = (bf16[4,128,256]{2,1,0:T(8,128)(2,1)S(1)}, bf16[4,128,256]{2,1,0:T(8,128)(2,1)S(1)}, u32[]{:S(2)}, u32[]{:S(2)}) collective-permute-start(bf16[4,128,256]{2,1,0:T(8,128)(2,1)S(1)} %maximum_bitcast_fusion.refs_0_), channel_id=1, source_target_pairs={{0,24},{8,0},{16,8},{24,16},{1,25},{9,1},{17,9},{25,17},{2,26},{10... | collective-permute-start | bytes 786440 | tf_op jit(solution)/shard_map/ppermute | solution.py:18
  8.3 16.9 %collective-permute-start.13 = (bf16[4,128,256]{2,1,0:T(8,128)(2,1)S(1)}, bf16[4,128,256]{2,1,0:T(8,128)(2,1)S(1)}, u32[]{:S(2)}, u32[]{:S(2)}) collective-permute-start(bf16[4,128,256]{2,1,0:T(8,128)(2,1)S(1)} %collective-permute-done.3.refs_4_.refs_0_), channel_id=1, source_target_pairs={{0,4},{2,6},{4,0},{6,2},{1,5},{3,7},{5,1},{7,3},{8,12},{10,14},{12... | collective-permute-start | bytes 786440 | tf_op jit(solution)/shard_map/ppermute | solution.py:28
  9.2 22.1 %collective-permute-start.2 = (bf16[4,128,256]{2,1,0:T(8,128)(2,1)S(1)}, bf16[4,128,256]{2,1,0:T(8,128)(2,1)S(1)}, u32[]{:S(2)}, u32[]{:S(2)}) collective-permute-start(bf16[4,128,256]{2,1,0:T(8,128)(2,1)S(1)} %collective-permute-done.1.refs_2_), channel_id=1, source_target_pairs={{0,2},{2,0},{4,6},{6,4},{1,3},{3,1},{5,7},{7,5},{8,10},{10,8},{12,... | collective-permute-start | bytes 786440 | tf_op jit(solution)/shard_map/ppermute | solution.py:28
  22.7 8.6 %collective-permute-start.10 = (bf16[4,128,256]{2,1,0:T(8,128)(2,1)S(1)}, bf16[4,128,256]{2,1,0:T(8,128)(2,1)S(1)}, u32[]{:S(2)}, u32[]{:S(2)}) collective-permute-start(bf16[4,128,256]{2,1,0:T(8,128)(2,1)S(1)} %collective-permute-done.8.refs_7_.refs_0_), channel_id=1, source_target_pairs={{0,4},{2,6},{4,0},{6,2},{1,5},{3,7},{5,1},{7,3},{8,12},{10,14},{12... | collective-permute-start | bytes 786440 | tf_op jit(solution)/shard_map/ppermute | solution.py:28
  23.9 18.9 %collective-permute-start.12 = (bf16[4,128,256]{2,1,0:T(8,128)(2,1)S(1)}, bf16[4,128,256]{2,1,0:T(8,128)(2,1)S(1)}, u32[]{:S(2)}, u32[]{:S(2)}) collective-permute-start(bf16[4,128,256]{2,1,0:T(8,128)(2,1)S(1)} %collective-permute-done.3.refs_4_.refs_0_), channel_id=1, source_target_pairs={{0,2},{2,0},{4,6},{6,4},{1,3},{3,1},{5,7},{7,5},{8,10},{10,8},{12,... | collective-permute-start | bytes 786440 | tf_op jit(solution)/shard_map/ppermute | solution.py:28
  24.9 18.0 %collective-permute-start.6 = (bf16[4,128,256]{2,1,0:T(8,128)(2,1)S(1)}, bf16[4,128,256]{2,1,0:T(8,128)(2,1)S(1)}, u32[]{:S(2)}, u32[]{:S(2)}) collective-permute-start(bf16[4,128,256]{2,1,0:T(8,128)(2,1)S(1)} %collective-permute-done.4.refs_7_.refs_0_), channel_id=1, source_target_pairs={{0,4},{2,6},{4,0},{6,2},{1,5},{3,7},{5,1},{7,3},{8,12},{10,14},{12... | collective-permute-start | bytes 786440 | tf_op jit(solution)/shard_map/ppermute | solution.py:28
  25.2 18.3 %collective-permute-start.14 = (bf16[4,128,256]{2,1,0:T(8,128)(2,1)S(1)}, bf16[4,128,256]{2,1,0:T(8,128)(2,1)S(1)}, u32[]{:S(2)}, u32[]{:S(2)}) collective-permute-start(bf16[4,128,256]{2,1,0:T(8,128)(2,1)S(1)} %collective-permute-done.13.refs_2_), channel_id=1, source_target_pairs={{0,2},{2,0},{4,6},{6,4},{1,3},{3,1},{5,7},{7,5},{8,10},{10,8},{12,... | collective-permute-start | bytes 786440 | tf_op jit(solution)/shard_map/ppermute | solution.py:28
  31.3 16.7 %collective-permute-start.9 = (bf16[4,128,256]{2,1,0:T(8,128)(2,1)S(1)}, bf16[4,128,256]{2,1,0:T(8,128)(2,1)S(1)}, u32[]{:S(2)}, u32[]{:S(2)}) collective-permute-start(bf16[4,128,256]{2,1,0:T(8,128)(2,1)S(1)} %collective-permute-done.8.refs_7_.refs_0_), channel_id=1, source_target_pairs={{0,2},{2,0},{4,6},{6,4},{1,3},{3,1},{5,7},{7,5},{8,10},{10,8},{12,... | collective-permute-start | bytes 786440 | tf_op jit(solution)/shard_map/ppermute | solution.py:28
  31.3 16.7 %collective-permute-start.11 = (bf16[4,128,256]{2,1,0:T(8,128)(2,1)S(1)}, bf16[4,128,256]{2,1,0:T(8,128)(2,1)S(1)}, u32[]{:S(2)}, u32[]{:S(2)}) collective-permute-start(bf16[4,128,256]{2,1,0:T(8,128)(2,1)S(1)} %collective-permute-done.10.refs_2_), channel_id=1, source_target_pairs={{0,2},{2,0},{4,6},{6,4},{1,3},{3,1},{5,7},{7,5},{8,10},{10,8},{12,... | collective-permute-start | bytes 786440 | tf_op jit(solution)/shard_map/ppermute | solution.py:28
  36.9 0.7 %copy-start = (s32[8,32]{1,0:T(8,128)S(1)}, s32[8,32]{1,0:T(8,128)}, u32[]{:S(2)}) copy-start(s32[8,32]{1,0:T(8,128)} %mask_ref.7) | copy-start | bytes 3076
  37.6 0.7 %copy-start.1 = (s32[8]{0:T(128)S(1)}, s32[8]{0:T(128)}, u32[]{:S(2)}) copy-start(s32[8]{0:T(128)} %order_ref.7) | copy-start | bytes 100
  38.2 2.2 %copy-start.2 = (bf16[1024,2048]{1,0:T(8,128)(2,1)S(1)}, bf16[1024,2048]{1,0:T(8,128)(2,1)}, u32[]{:S(2)}) copy-start(bf16[1024,2048]{1,0:T(8,128)(2,1)} %q_in.1) | copy-start | bytes 12582916
  42.9 10.7 %collective-permute-start.5 = (bf16[4,128,256]{2,1,0:T(8,128)(2,1)S(1)}, bf16[4,128,256]{2,1,0:T(8,128)(2,1)S(1)}, u32[]{:S(2)}, u32[]{:S(2)}) collective-permute-start(bf16[4,128,256]{2,1,0:T(8,128)(2,1)S(1)} %collective-permute-done.4.refs_7_.refs_0_), channel_id=1, source_target_pairs={{0,2},{2,0},{4,6},{6,4},{1,3},{3,1},{5,7},{7,5},{8,10},{10,8},{12,... | collective-permute-start | bytes 786440 | tf_op jit(solution)/shard_map/ppermute | solution.py:28
  42.9 10.7 %collective-permute-start.7 = (bf16[4,128,256]{2,1,0:T(8,128)(2,1)S(1)}, bf16[4,128,256]{2,1,0:T(8,128)(2,1)S(1)}, u32[]{:S(2)}, u32[]{:S(2)}) collective-permute-start(bf16[4,128,256]{2,1,0:T(8,128)(2,1)S(1)} %collective-permute-done.6.refs_2_), channel_id=1, source_target_pairs={{0,2},{2,0},{4,6},{6,4},{1,3},{3,1},{5,7},{7,5},{8,10},{10,8},{12,... | collective-permute-start | bytes 786440 | tf_op jit(solution)/shard_map/ppermute | solution.py:28

commit v4 on v3

v4 whole, which is shorter than its diff:
```python
import functools
import math

import jax
import jax.numpy as jnp
from jax import lax
from jax.experimental import pallas as pl
from jax.experimental.pallas import tpu as pltpu
from jax.sharding import PartitionSpec as P

HEAD_DIM = 128
MASKED = -1e30
STAGES = 4


def folded(size):
    return list(range(0, size, 2)) + list(range(1, size, 2))[::-1]


def along_ring(array, size):
    ring = folded(size)
    return lax.ppermute(array, "pb", [(ring[i], ring[(i + 1) % size]) for i in range(size)])


def ring_source(at, size, hops):
    place = jnp.where(at % 2 == 0, at // 2, size - 1 - at // 2)
    place = lax.rem(place + (size - hops), size)
    return jnp.where(place < (size + 1) // 2, 2 * place, 2 * (size - 1 - place) + 1)


def turn(array, size, cores, ring_step, core_step):
    rings = size // cores
    pairs = []
    for ring in range(rings):
        for core in range(cores):
            to = ((ring + ring_step) % rings) * cores + (core + core_step) % cores
            pairs.append((ring * cores + core, to))
    return lax.ppermute(array, "ka", pairs)


def dot(a, b, b_dim):
    return lax.dot_general(a, b, (((1,), (b_dim,)), ((), ())), preferred_element_type=jnp.float32)


def attend_stage(plan, first, last, table_ref, q_ref, *refs):
    pb, ka, cores, places, slots, turned = plan
    count = len(places)
    pieces, refs = refs[:count], refs[count:]
    if not first:
        old_refs, refs = refs[:3], refs[3:]
    if not last:
        refs = refs[1:]
    if last:
        out_ref, refs = refs[0], refs[1:]
    acc, top, total, k_pool, v_pool, bias = refs[:6]
    rows = acc.shape[1]
    held, block_rows, _ = pieces[0].shape
    held = held // 2
    group = rows // block_rows
    rings = ka // cores
    own_slots = slots // cores
    p_at, k_at = lax.axis_index("pb"), lax.axis_index("ka")
    ring_at, core_at = k_at // cores, lax.rem(k_at, cores)
    scale = math.log2(math.e) / math.sqrt(HEAD_DIM)

    blocks = []
    for hops, y, c in places:
        ring = lax.rem(ring_at + (rings - y), rings)
        core = lax.rem(core_at + (cores - c), cores)
        class_local = held // len(hops)
        for z in hops:
            source = ring_source(p_at, pb, z)
            for t in range(class_local):
                blocks.append((source * class_local + t) * ka + ring * cores + core)

    if first:
        acc[...] = jnp.zeros(acc.shape, acc.dtype)
        total[...] = jnp.zeros(total.shape, total.dtype)
        top[...] = jnp.full(top.shape, MASKED, top.dtype)

    row_id = lax.broadcasted_iota(jnp.int32, (block_rows, block_rows), 0)
    col_id = lax.broadcasted_iota(jnp.int32, (block_rows, block_rows), 1)

    def fill(row):
        own = table_ref[row, 0]
        listed = [table_ref[row, 1 + block] for block in blocks]
        size = functools.reduce(lambda a, b: a + b, listed)
        done = jnp.int32(0)
        has_own = jnp.int32(0)
        for at, block in enumerate(blocks):
            piece, t = at // held, at % held
            is_own = block == own
            place = jnp.where(is_own, size - 1, done)

            @pl.when(listed[at] == 1)
            def _():
                k_pool[place] = pieces[piece][t]
                v_pool[place] = pieces[piece][held + t]

            done = done + jnp.where(is_own, 0, listed[at])
            has_own = has_own + jnp.where(is_own, listed[at], 0)

        @pl.when(lax.rem(size, 2) == 1)
        def _():
            k_pool[size] = jnp.zeros(k_pool.shape[1:], k_pool.dtype)
            v_pool[size] = jnp.zeros(v_pool.shape[1:], v_pool.dtype)

        return size, has_own

    def unit(s, at, size, has_own, u):
        for half in range(2):
            entry = 2 * u + half
            reach = jnp.where(entry >= size, -block_rows, block_rows)
            reach = jnp.where((entry == size - 1) & (has_own == 1), 0, reach)
            bias[:, half * block_rows : (half + 1) * block_rows] = jnp.where(
                col_id <= row_id + reach, 0.0, MASKED
            )
        k_pair = jnp.concatenate([k_pool[2 * u], k_pool[2 * u + 1]], axis=0)
        v_pair = jnp.concatenate([v_pool[2 * u], v_pool[2 * u + 1]], axis=0)
        q_rows = jnp.concatenate(
            [
                q_ref[
                    pl.ds(pl.multiple_of(s * block_rows, block_rows), block_rows),
                    x * HEAD_DIM : (x + 1) * HEAD_DIM,
                ]
                for x in range(group)
            ],
            axis=0,
        )
        scores = dot(q_rows, k_pair, 1)
        weights = []
        shrinks = []
        for x in range(group):
            span = slice(x * block_rows, (x + 1) * block_rows)
            score = scores[span] + bias[...]
            halves = score[:, :block_rows], score[:, block_rows:]
            peak = jnp.max(jnp.maximum(*halves), axis=1, keepdims=True)
            old = top[at, span]
            new = jnp.maximum(old, peak)
            top[at, span] = new
            shrink = jnp.exp2((old - new) * scale)
            one, two = (jnp.exp2((half - new) * scale) for half in halves)
            total[at, span] = total[at, span] * shrink + (one + two)
            weights.append(
                jnp.concatenate([one.astype(jnp.bfloat16), two.astype(jnp.bfloat16)], axis=1)
            )
            shrinks.append(shrink)
        added = dot(jnp.concatenate(weights, axis=0), v_pair, 0)
        for x in range(group):
            span = slice(x * block_rows, (x + 1) * block_rows)
            acc[at, span] = acc[at, span] * shrinks[x] + added[span]

    for at in range(acc.shape[0]):
        if last:
            s = lax.rem(core_at + turned, cores) * own_slots + at
        else:
            s = at
        if not first:
            for new, old in zip((acc, top, total), old_refs):
                new[at] = old[s]
        size, has_own = fill(ring_at * slots + s)

        def one_unit(u, carry, s=s, at=at, size=size, has_own=has_own):
            unit(s, at, size, has_own, u)
            return carry

        lax.fori_loop(0, (size + 1) // 2, one_unit, 0)
        if last:
            for x in range(group):
                span = slice(x * block_rows, (x + 1) * block_rows)
                under = jnp.sum(total[at, span], axis=1, keepdims=True)
                out_ref[
                    at * block_rows : (at + 1) * block_rows, x * HEAD_DIM : (x + 1) * HEAD_DIM
                ] = (acc[at, span] / under).astype(out_ref.dtype)


def split(cores, keys_ref, values_ref, *refs):
    outs, sems = refs[:cores], refs[cores]
    count = keys_ref.shape[0]
    width = outs[0].shape[2]
    core = lax.rem(lax.axis_index("ka"), cores)
    copies = []
    for i, out in enumerate(outs):
        at = pl.multiple_of(lax.rem(core + i, cores) * width, HEAD_DIM)
        for j, ref in enumerate((keys_ref, values_ref)):
            copy = pltpu.make_async_copy(
                ref.at[:, 0, :, pl.ds(at, width)],
                out.at[pl.ds(j * count, count)],
                sems.at[2 * i + j],
            )
            copy.start()
            copies.append(copy)
    for copy in copies:
        copy.wait()


def fetch(cores, queries_ref, out_ref, sem):
    rows, width = out_ref.shape
    at = lax.axis_index("ka")
    copy = pltpu.make_async_copy(
        queries_ref.at[
            pl.ds(pl.multiple_of(at // cores * rows, HEAD_DIM), rows),
            pl.ds(pl.multiple_of(lax.rem(at, cores) * width, HEAD_DIM), width),
        ],
        out_ref,
        sem,
    )
    copy.start()
    copy.wait()


def join(cores, own_ref, other_ref, out_ref, sems):
    width = own_ref.shape[1]
    core = lax.rem(lax.axis_index("ka"), cores)
    copies = []
    for i, ref in enumerate((own_ref, other_ref)):
        at = lax.rem(core + (cores - i), cores) * width
        copy = pltpu.make_async_copy(
            ref, out_ref.at[:, pl.ds(pl.multiple_of(at, HEAD_DIM), width)], sems.at[i]
        )
        copy.start()
        copies.append(copy)
    for copy in copies:
        copy.wait()


def on_device(queries, keys, values, q_order, block_mask):
    pb, ka = lax.axis_size("pb"), lax.axis_size("ka")
    class_local, _, block_rows, kv_width = keys.shape
    cores = 2 if ka % 2 == 0 and kv_width == 2 * HEAD_DIM else 1
    rings = ka // cores
    head_width = kv_width // cores
    width = queries.shape[1] // cores
    rows = width // head_width * block_rows
    own_slots = queries.shape[0] // block_rows // ka
    slots = own_slots * cores

    vmem = pl.BlockSpec(memory_space=pltpu.VMEM)
    smem = pl.BlockSpec(memory_space=pltpu.SMEM)
    hbm = pl.BlockSpec(memory_space=pltpu.HBM)
    anywhere = pl.BlockSpec(memory_space=pl.ANY)
    stages = min(STAGES, pb)
    sources = pb // stages

    table = jnp.concatenate([q_order[:, None], block_mask], axis=1)
    part = jax.ShapeDtypeStruct((2 * class_local, block_rows, head_width), keys.dtype)
    starts = pl.pallas_call(
        functools.partial(split, cores),
        out_shape=[part] * cores,
        in_specs=[anywhere] * 2,
        out_specs=[vmem] * cores,
        scratch_shapes=[pltpu.SemaphoreType.DMA((2 * cores,))],
        compiler_params=pltpu.CompilerParams(vmem_limit_bytes=60 * 2**20),
    )(keys, values)
    if cores == 2:
        starts = [starts[0], turn(starts[1], ka, cores, 0, 1)]

    near = [starts]
    for z in range(1, pb):
        near.append([along_ring(array, pb) for array in near[-1]])
    staged = []
    for stage in range(stages):
        here = near[stage * sources : (stage + 1) * sources]
        if sources == 1:
            staged.append(here[0])
            continue
        staged.append(
            [
                jnp.concatenate(
                    [array[:class_local] for array in arrays]
                    + [array[class_local:] for array in arrays],
                    axis=0,
                )
                for arrays in zip(*here)
            ]
        )

    def call(stage, first, last, turned, pieces, places, own_queries, state, ahead):
        held = len(places) * sources * class_local
        held += held % 2
        here = own_slots if last else slots
        state_shape = jax.ShapeDtypeStruct((here, rows, HEAD_DIM), jnp.float32)
        scratch = [pltpu.VMEM((held, block_rows, HEAD_DIM), jnp.bfloat16)] * 2
        scratch.append(pltpu.VMEM((block_rows, 2 * block_rows), jnp.float32))
        if last:
            outs = [jax.ShapeDtypeStruct((own_slots * block_rows, width), queries.dtype)]
            scratch = [pltpu.VMEM(state_shape.shape, state_shape.dtype)] * 3 + scratch
        else:
            outs = [state_shape] * 3
        return pl.pallas_call(
            functools.partial(
                attend_stage, (pb, ka, cores, places, slots, turned), first, last
            ),
            out_shape=outs,
            in_specs=[smem]
            + [vmem] * (1 + len(places) + len(state))
            + [anywhere] * len(ahead),
            out_specs=[vmem] * len(outs),
            scratch_shapes=scratch,
            compiler_params=pltpu.CompilerParams(vmem_limit_bytes=20 * 2**20),
            cost_estimate=pl.CostEstimate(
                flops=2**31, bytes_accessed=2**22, transcendentals=2**20
            ),
        )(table, own_queries, *pieces, *state, *ahead)

    own_queries = pl.pallas_call(
        functools.partial(fetch, cores),
        out_shape=jax.ShapeDtypeStruct((slots * block_rows, width), queries.dtype),
        in_specs=[anywhere],
        out_specs=vmem,
        scratch_shapes=[pltpu.SemaphoreType.DMA],
        compiler_params=pltpu.CompilerParams(vmem_limit_bytes=57 * 2**20),
    )(queries)

    state = ()
    for stage in range(stages):
        hops = range(stage * sources, (stage + 1) * sources)
        places, pieces = [], []
        for c in range(cores):
            ring = staged[stage][c]
            for y in range(rings):
                if y:
                    ring = turn(ring, ka, cores, 1, 0)
                places.append((hops, y, c))
                pieces.append(ring)
        first, last = stage == 0, stage == stages - 1
        if not last:
            ahead = [staged[stage + 1][-1]]
            state = call(stage, first, last, 0, pieces, places, own_queries, state, ahead)
            continue
        halves = [
            call(stage, first, last, c, pieces, places, own_queries, state, [])[0]
            for c in range(cores)
        ]
    if cores == 1:
        return halves[0]
    return pl.pallas_call(
        functools.partial(join, cores),
        out_shape=jax.ShapeDtypeStruct((own_slots * block_rows, cores * width), queries.dtype),
        in_specs=[anywhere] * 2,
        out_specs=hbm,
        scratch_shapes=[pltpu.SemaphoreType.DMA((2,))],
    )(halves[0], turn(halves[1], ka, cores, 0, 1))


def solution(mesh):
    in_specs = (
        P("pb", "ha"),
        P("pb", "ka", None, "ha"),
        P("pb", "ka", None, "ha"),
        P("pb"),
        P("pb", None),
    )
    out_specs = P(("pb", "ka"), "ha")
    return jax.shard_map(
        on_device, mesh=mesh, in_specs=in_specs, out_specs=out_specs, check_vma=False
    )
```

time: 57.2 us -> 80.7 us (1.41)
  the two profiles are of different devices: /device:TPU:21 before, /device:TPU:27 now
where the time goes in v4:
time: 80.7 us; the launch traced here: 81.4 us
  Pallas kernels  54.5 us (68%)
  starting transfers between devices  19.6 us (24%)
  waiting for transfers between devices  3.93 us (5%)
  local copies, waits for them, and re-layouts  2.91 us (4%)
    pallas_call x1, Pallas kernels, on_device(): pl.pallas_call(functools.partial(join, cores), out_shape=jax.ShapeDtypeSt...  32.9 us
    pallas_call x5, Pallas kernels, call(): pl.pallas_call(functools.partial(attend_stage, (pb, ka, cores, places, sl...  17.8 us
    ppermute x10, starting transfers between devices, turn(): return lax.ppermute(array, 'ka', pairs)  11.5 us
    ppermute x6, starting transfers between devices, along_ring(): lax.ppermute(array, 'pb', [(ring[i], ring[(i + 1) % size]) for i in range...  8.07 us
    unnamed x12, local copies, waits for them, and re-layouts  2.83 us
    ppermute x6, waiting for transfers between devices, along_ring(): lax.ppermute(array, 'pb', [(ring[i], ring[(i + 1) % size]) for i in range...  2.79 us
    pallas_call x1, Pallas kernels, on_device(): pl.pallas_call(functools.partial(fetch, cores), out_shape=jax.ShapeDtypeS...  2.2 us
    pallas_call x1, Pallas kernels, on_device(): pl.pallas_call(functools.partial(split, cores), out_shape=[part] * cores,...  1.66 us
  transfers between devices with their start and end apart: 16, of which 2 were waited for; matrix products, arithmetic and copies ran while one was open for 0% of the time, Pallas kernels for 21%

profile of v4, /device:TPU:27, one launch (start us, length us, event | category | flops | bytes accessed | tf_op | source)
XLA Modules:
  0.0 81.4 jit_solution(16308163753104085804)
XLA Ops:
  0.0 1.7 %shard_map.56 = (bf16[4,128,128]{2,1,0:T(8,128)(2,1)}, bf16[4,128,128]{2,1,0:T(8,128)(2,1)}) custom-call(bf16[2,1,128,256]{3,2,1,0:T(8,128)(2,1)} %keys_ref.1, bf16[2,1,128,256]{3,2,1,0:T(8,128)(2,1)} %values_ref.1), custom_call_target="tpu_custom_call" | custom-call | tf_op jit(solution)/shard_map/pallas_call | solution.py:247
  1.7 0.7 collective-permute-start.4
  2.4 0.1 collective-permute-start
  2.5 1.1 %collective-permute-done.4.refs_2_ = bf16[4,128,128]{2,1,0:T(8,128)(2,1)S(1)} collective-permute-done((bf16[4,128,128]{2,1,0:T(8,128)(2,1)}, bf16[4,128,128]{2,1,0:T(8,128)(2,1)S(1)}, u32[]{:S(2)}, u32[]{:S(2)}) %collective-permute-start.4) | collective-permute-done | bytes 131104 | tf_op jit(solution)/shard_map/ppermute | solution.py:38
  3.6 0.1 collective-permute-start.5
  3.7 1.2 %collective-permute-start.13 = (bf16[4,128,128]{2,1,0:T(8,128)(2,1)}, bf16[4,128,128]{2,1,0:T(8,128)(2,1)S(1)}, u32[]{:S(2)}, u32[]{:S(2)}) collective-permute-start(bf16[4,128,128]{2,1,0:T(8,128)(2,1)} %get-tuple-element.16.refs_0_), channel_id=1, source_target_pairs={{0,4},{2,6},{4,0},{6,2},{1,5},{3,7},{5,1},{7,3},{8,12},{10,14},{12... | collective-permute-start | bytes 393224 | tf_op jit(solution)/shard_map/ppermute | solution.py:38
  4.9 2.8 %collective-permute-done.refs_0_ = bf16[4,128,128]{2,1,0:T(8,128)(2,1)S(1)} collective-permute-done((bf16[4,128,128]{2,1,0:T(8,128)(2,1)}, bf16[4,128,128]{2,1,0:T(8,128)(2,1)S(1)}, u32[]{:S(2)}, u32[]{:S(2)}) %collective-permute-start) | collective-permute-done | bytes 131104 | tf_op jit(solution)/shard_map/ppermute | solution.py:22
  7.7 1.0 %collective-permute-start.1 = (bf16[4,128,128]{2,1,0:T(8,128)(2,1)S(1)}, bf16[4,128,128]{2,1,0:T(8,128)(2,1)S(1)}, u32[]{:S(2)}, u32[]{:S(2)}) collective-permute-start(bf16[4,128,128]{2,1,0:T(8,128)(2,1)S(1)} %collective-permute-done.refs_0_), channel_id=1, source_target_pairs={{0,16},{16,24},{24,8},{8,0},{1,17},{17,25},{25,9},{9,1},{2,18},{18... | collective-permute-start | bytes 393224 | tf_op jit(solution)/shard_map/ppermute | solution.py:22
  8.7 1.2 %collective-permute-start.14 = (bf16[4,128,128]{2,1,0:T(8,128)(2,1)S(1)}, bf16[4,128,128]{2,1,0:T(8,128)(2,1)S(1)}, u32[]{:S(2)}, u32[]{:S(2)}) collective-permute-start(bf16[4,128,128]{2,1,0:T(8,128)(2,1)S(1)} %collective-permute-done.4.refs_2_), channel_id=1, source_target_pairs={{0,4},{2,6},{4,0},{6,2},{1,5},{3,7},{5,1},{7,3},{8,12},{10,14},{12... | collective-permute-start | bytes 393224 | tf_op jit(solution)/shard_map/ppermute | solution.py:38
  9.9 2.2 %shard_map.55.q_ref = bf16[512,1024]{1,0:T(8,128)(2,1)} custom-call(bf16[1024,2048]{1,0:T(8,128)(2,1)} %queries_ref.1), custom_call_target="tpu_custom_call" | custom-call | tf_op jit(solution)/shard_map/pallas_call | solution.py:306
  12.1 0.0 copy-done.5
  12.1 0.1 copy.6
  12.2 0.0 copy-done.4
  12.2 0.1 pad_add_fusion.table_ref
  12.3 0.2 collective-permute-start.11
  12.5 0.0 collective-permute-done.5.refs_4_.refs_2_
  12.5 0.0 collective-permute-start.6
  12.5 0.0 collective-permute-done.13.refs_1_
  12.5 1.3 %collective-permute-start.12 = (bf16[4,128,128]{2,1,0:T(8,128)(2,1)S(1)}, bf16[4,128,128]{2,1,0:T(8,128)(2,1)S(1)}, u32[]{:S(2)}, u32[]{:S(2)}) collective-permute-start(bf16[4,128,128]{2,1,0:T(8,128)(2,1)S(1)} %collective-permute-done.5.refs_4_.refs_2_), channel_id=1, source_target_pairs={{0,4},{2,6},{4,0},{6,2},{1,5},{3,7},{5,1},{7,3},{8,12},{10,14},{12... | collective-permute-start | bytes 393224 | tf_op jit(solution)/shard_map/ppermute | solution.py:38
  13.8 0.0 collective-permute-done.1.refs_0_
  13.8 0.2 collective-permute-start.9
  14.0 0.0 collective-permute-done.14.refs_3_
  14.0 2.4 %collective-permute-start.2 = (bf16[4,128,128]{2,1,0:T(8,128)(2,1)S(1)}, bf16[4,128,128]{2,1,0:T(8,128)(2,1)S(1)}, u32[]{:S(2)}, u32[]{:S(2)}) collective-permute-start(bf16[4,128,128]{2,1,0:T(8,128)(2,1)S(1)} %collective-permute-done.1.refs_0_), channel_id=1, source_target_pairs={{0,16},{16,24},{24,8},{8,0},{1,17},{17,25},{25,9},{9,1},{2,18},{18... | collective-permute-start | bytes 393224 | tf_op jit(solution)/shard_map/ppermute | solution.py:22
  16.4 0.0 copy-done.2
  16.5 1.2 %copy-done = bf16[512,1024]{1,0:T(8,128)(2,1)S(1)} copy-done((bf16[512,1024]{1,0:T(8,128)(2,1)S(1)}, bf16[512,1024]{1,0:T(8,128)(2,1)}, u32[]{:S(2)}) %copy-start) | copy-done | bytes 1048600
  17.7 2.0 %shard_map.57 = (f32[4,1024,128]{2,1,0:T(8,128)S(1)}, f32[4,1024,128]{2,1,0:T(8,128)S(1)}, f32[4,1024,128]{2,1,0:T(8,128)S(1)}) custom-call(s32[8,33]{1,0:T(8,128)S(1)} %pad_add_fusion.table_ref, bf16[512,1024]{1,0:T(8,128)(2,1)S(1)} %copy-done, bf16[4,128,128]{2,1,0:T(8,128)(2,1)S(1)} %copy-done.2, ...), custom_call_target="tpu_custom_call" | custom-call | flops 2147483648 | bytes 4194304 | tf_op jit(solution)/shard_map/pallas_call | solution.py:290
  19.7 0.0 collective-permute-done.6.refs_7_.refs_2_
  19.7 4.6 %collective-permute-start.7 = (bf16[4,128,128]{2,1,0:T(8,128)(2,1)S(1)}, bf16[4,128,128]{2,1,0:T(8,128)(2,1)S(1)}, u32[]{:S(2)}, u32[]{:S(2)}) collective-permute-start(bf16[4,128,128]{2,1,0:T(8,128)(2,1)S(1)} %collective-permute-done.6.refs_7_.refs_2_), channel_id=1, source_target_pairs={{0,16},{16,24},{24,8},{8,0},{1,17},{17,25},{25,9},{9,1},{2,18},{18... | collective-permute-start | bytes 393224 | tf_op jit(solution)/shard_map/ppermute | solution.py:22
  24.3 0.0 collective-permute-done.11.refs_1_
  24.3 0.0 collective-permute-start.10
  24.3 0.0 collective-permute-done.2.refs_0_
  24.3 1.5 %collective-permute-start.3 = (bf16[4,128,128]{2,1,0:T(8,128)(2,1)S(1)}, bf16[4,128,128]{2,1,0:T(8,128)(2,1)S(1)}, u32[]{:S(2)}, u32[]{:S(2)}) collective-permute-start(bf16[4,128,128]{2,1,0:T(8,128)(2,1)S(1)} %collective-permute-done.2.refs_0_), channel_id=1, source_target_pairs={{0,4},{2,6},{4,0},{6,2},{1,5},{3,7},{5,1},{7,3},{8,12},{10,14},{12... | collective-permute-start | bytes 393224 | tf_op jit(solution)/shard_map/ppermute | solution.py:38
  25.7 0.0 collective-permute-done.12.refs_3_
  25.7 4.8 %shard_map.58 = (f32[4,1024,128]{2,1,0:T(8,128)S(1)}, f32[4,1024,128]{2,1,0:T(8,128)S(1)}, f32[4,1024,128]{2,1,0:T(8,128)S(1)}) custom-call(s32[8,33]{1,0:T(8,128)S(1)} %pad_add_fusion.table_ref, bf16[512,1024]{1,0:T(8,128)(2,1)S(1)} %copy-done, bf16[4,128,128]{2,1,0:T(8,128)(2,1)S(1)} %collective-permute-done.refs_0_, ...), custom_call_target="tpu_custom_call" | custom-call | flops 2147483648 | bytes 4194304 | tf_op jit(solution)/shard_map/pallas_call | solution.py:290
  30.5 0.0 collective-permute-done.7.refs_7_.refs_2_
  30.5 0.1 collective-permute-start.8
  30.6 0.0 collective-permute-done.9.refs_1_
  30.6 0.0 collective-permute-done.10.refs_3_
  30.6 4.8 %shard_map.59 = (f32[4,1024,128]{2,1,0:T(8,128)S(1)}, f32[4,1024,128]{2,1,0:T(8,128)S(1)}, f32[4,1024,128]{2,1,0:T(8,128)S(1)}) custom-call(s32[8,33]{1,0:T(8,128)S(1)} %pad_add_fusion.table_ref, bf16[512,1024]{1,0:T(8,128)(2,1)S(1)} %copy-done, bf16[4,128,128]{2,1,0:T(8,128)(2,1)S(1)} %collective-permute-done.1.refs_0_, ...), custom_call_target="tpu_custom_call" | custom-call | flops 2147483648 | bytes 4194304 | tf_op jit(solution)/shard_map/pallas_call | solution.py:290
  35.4 0.0 collective-permute-done.3.refs_1_
  35.4 0.0 collective-permute-done.8.refs_3_
  35.4 2.9 %shard_map.61 = bf16[256,1024]{1,0:T(8,128)(2,1)S(1)} custom-call(s32[8,33]{1,0:T(8,128)S(1)} %pad_add_fusion.table_ref, bf16[512,1024]{1,0:T(8,128)(2,1)S(1)} %copy-done, bf16[4,128,128]{2,1,0:T(8,128)(2,1)S(1)} %collective-permute-done.2.refs_0_, bf16[4,128,128]{2,1,0:T(8,128)(2,1)S(1)} %collective-permute-done.3.refs_1_, ...), custom_call_target="tpu_custom_call" | custom-call | flops 2147483648 | bytes 4194304 | tf_op jit(solution)/shard_map/pallas_call | solution.py:290
  38.3 5.0 %collective-permute-start.15 = (bf16[256,1024]{1,0:T(8,128)(2,1)S(1)}, bf16[256,1024]{1,0:T(8,128)(2,1)S(1)}, u32[]{:S(2)}, u32[]{:S(2)}) collective-permute-start(bf16[256,1024]{1,0:T(8,128)(2,1)S(1)} %shard_map.61), channel_id=1, source_target_pairs={{0,2},{2,0},{4,6},{6,4},{1,3},{3,1},{5,7},{7,5},{8,10},{10,8},{12,... | collective-permute-start | bytes 1572872 | tf_op jit(solution)/shard_map/ppermute | solution.py:38
  43.3 3.4 %shard_map.60.own_ref = bf16[256,1024]{1,0:T(8,128)(2,1)S(1)} custom-call(s32[8,33]{1,0:T(8,128)S(1)} %pad_add_fusion.table_ref, bf16[512,1024]{1,0:T(8,128)(2,1)S(1)} %copy-done, bf16[4,128,128]{2,1,0:T(8,128)(2,1)S(1)} %collective-permute-done.2.refs_0_, bf16[4,128,128]{2,1,0:T(8,128)(2,1)S(1)} %collective-permute-done.3.refs_1_, ...), custom_call_target="tpu_custom_call" | custom-call | flops 2147483648 | bytes 4194304 | tf_op jit(solution)/shard_map/pallas_call | solution.py:290
  46.7 0.8 copy-done.1
  47.5 0.0 collective-permute-done.15.other_ref
  47.5 0.8 copy-done.3
  48.3 32.9 %shard_map.62 = bf16[256,2048]{1,0:T(8,128)(2,1)} custom-call(bf16[256,1024]{1,0:T(8,128)(2,1)} %copy-done.1, bf16[256,1024]{1,0:T(8,128)(2,1)} %copy-done.3), custom_call_target="tpu_custom_call" | custom-call | tf_op jit(solution)/shard_map/pallas_call | solution.py:337
  (6 shorter events, 0.0 us)
Async XLA Ops:
  1.7 1.9 %collective-permute-start.4 = (bf16[4,128,128]{2,1,0:T(8,128)(2,1)}, bf16[4,128,128]{2,1,0:T(8,128)(2,1)S(1)}, u32[]{:S(2)}, u32[]{:S(2)}) collective-permute-start(bf16[4,128,128]{2,1,0:T(8,128)(2,1)} %get-tuple-element.17), channel_id=1, source_target_pairs={{0,2},{2,0},{4,6},{6,4},{1,3},{3,1},{5,7},{7,5},{8,10},{10,8},{12,... | collective-permute-start | bytes 393224 | tf_op jit(solution)/shard_map/ppermute | solution.py:38
  2.4 9.7 %copy-start.5 = (s32[8]{0:T(128)S(1)}, s32[8]{0:T(128)}, u32[]{:S(2)}) copy-start(s32[8]{0:T(128)} %param.8) | copy-start | bytes 100
  2.4 9.8 %copy-start.4 = (s32[8,32]{1,0:T(8,128)S(1)}, s32[8,32]{1,0:T(8,128)}, u32[]{:S(2)}) copy-start(s32[8,32]{1,0:T(8,128)} %param.9) | copy-start | bytes 3076
  2.4 14.0 %copy-start.2 = (bf16[4,128,128]{2,1,0:T(8,128)(2,1)S(1)}, bf16[4,128,128]{2,1,0:T(8,128)(2,1)}, u32[]{:S(2)}) copy-start(bf16[4,128,128]{2,1,0:T(8,128)(2,1)} %get-tuple-element.16.refs_0_) | copy-start | bytes 393220
  2.4 5.3 %collective-permute-start = (bf16[4,128,128]{2,1,0:T(8,128)(2,1)}, bf16[4,128,128]{2,1,0:T(8,128)(2,1)S(1)}, u32[]{:S(2)}, u32[]{:S(2)}) collective-permute-start(bf16[4,128,128]{2,1,0:T(8,128)(2,1)} %get-tuple-element.16.refs_0_), channel_id=1, source_target_pairs={{0,16},{16,24},{24,8},{8,0},{1,17},{17,25},{25,9},{9,1},{2,18},{18... | collective-permute-start | bytes 393224 | tf_op jit(solution)/shard_map/ppermute | solution.py:22
  3.6 8.9 %collective-permute-start.5 = (bf16[4,128,128]{2,1,0:T(8,128)(2,1)S(1)}, bf16[4,128,128]{2,1,0:T(8,128)(2,1)S(1)}, u32[]{:S(2)}, u32[]{:S(2)}) collective-permute-start(bf16[4,128,128]{2,1,0:T(8,128)(2,1)S(1)} %collective-permute-done.4.refs_2_), channel_id=1, source_target_pairs={{0,16},{16,24},{24,8},{8,0},{1,17},{17,25},{25,9},{9,1},{2,18},{18... | collective-permute-start | bytes 393224 | tf_op jit(solution)/shard_map/ppermute | solution.py:22
  3.7 8.8 %collective-permute-start.13 = (bf16[4,128,128]{2,1,0:T(8,128)(2,1)}, bf16[4,128,128]{2,1,0:T(8,128)(2,1)S(1)}, u32[]{:S(2)}, u32[]{:S(2)}) collective-permute-start(bf16[4,128,128]{2,1,0:T(8,128)(2,1)} %get-tuple-element.16.refs_0_), channel_id=1, source_target_pairs={{0,4},{2,6},{4,0},{6,2},{1,5},{3,7},{5,1},{7,3},{8,12},{10,14},{12... | collective-permute-start | bytes 393224 | tf_op jit(solution)/shard_map/ppermute | solution.py:38
  7.7 6.1 %collective-permute-start.1 = (bf16[4,128,128]{2,1,0:T(8,128)(2,1)S(1)}, bf16[4,128,128]{2,1,0:T(8,128)(2,1)S(1)}, u32[]{:S(2)}, u32[]{:S(2)}) collective-permute-start(bf16[4,128,128]{2,1,0:T(8,128)(2,1)S(1)} %collective-permute-done.refs_0_), channel_id=1, source_target_pairs={{0,16},{16,24},{24,8},{8,0},{1,17},{17,25},{25,9},{9,1},{2,18},{18... | collective-permute-start | bytes 393224 | tf_op jit(solution)/shard_map/ppermute | solution.py:22
  8.7 5.4 %collective-permute-start.14 = (bf16[4,128,128]{2,1,0:T(8,128)(2,1)S(1)}, bf16[4,128,128]{2,1,0:T(8,128)(2,1)S(1)}, u32[]{:S(2)}, u32[]{:S(2)}) collective-permute-start(bf16[4,128,128]{2,1,0:T(8,128)(2,1)S(1)} %collective-permute-done.4.refs_2_), channel_id=1, source_target_pairs={{0,4},{2,6},{4,0},{6,2},{1,5},{3,7},{5,1},{7,3},{8,12},{10,14},{12... | collective-permute-start | bytes 393224 | tf_op jit(solution)/shard_map/ppermute | solution.py:38
  12.3 12.0 %collective-permute-start.11 = (bf16[4,128,128]{2,1,0:T(8,128)(2,1)S(1)}, bf16[4,128,128]{2,1,0:T(8,128)(2,1)S(1)}, u32[]{:S(2)}, u32[]{:S(2)}) collective-permute-start(bf16[4,128,128]{2,1,0:T(8,128)(2,1)S(1)} %collective-permute-done.refs_0_), channel_id=1, source_target_pairs={{0,4},{2,6},{4,0},{6,2},{1,5},{3,7},{5,1},{7,3},{8,12},{10,14},{12... | collective-permute-start | bytes 393224 | tf_op jit(solution)/shard_map/ppermute | solution.py:38
  12.5 7.2 %collective-permute-start.6 = (bf16[4,128,128]{2,1,0:T(8,128)(2,1)S(1)}, bf16[4,128,128]{2,1,0:T(8,128)(2,1)S(1)}, u32[]{:S(2)}, u32[]{:S(2)}) collective-permute-start(bf16[4,128,128]{2,1,0:T(8,128)(2,1)S(1)} %collective-permute-done.5.refs_4_.refs_2_), channel_id=1, source_target_pairs={{0,16},{16,24},{24,8},{8,0},{1,17},{17,25},{25,9},{9,1},{2,18},{18... | collective-permute-start | bytes 393224 | tf_op jit(solution)/shard_map/ppermute | solution.py:22
  12.5 13.2 %collective-permute-start.12 = (bf16[4,128,128]{2,1,0:T(8,128)(2,1)S(1)}, bf16[4,128,128]{2,1,0:T(8,128)(2,1)S(1)}, u32[]{:S(2)}, u32[]{:S(2)}) collective-permute-start(bf16[4,128,128]{2,1,0:T(8,128)(2,1)S(1)} %collective-permute-done.5.refs_4_.refs_2_), channel_id=1, source_target_pairs={{0,4},{2,6},{4,0},{6,2},{1,5},{3,7},{5,1},{7,3},{8,12},{10,14},{12... | collective-permute-start | bytes 393224 | tf_op jit(solution)/shard_map/ppermute | solution.py:38
  13.8 16.8 %collective-permute-start.9 = (bf16[4,128,128]{2,1,0:T(8,128)(2,1)S(1)}, bf16[4,128,128]{2,1,0:T(8,128)(2,1)S(1)}, u32[]{:S(2)}, u32[]{:S(2)}) collective-permute-start(bf16[4,128,128]{2,1,0:T(8,128)(2,1)S(1)} %collective-permute-done.1.refs_0_), channel_id=1, source_target_pairs={{0,4},{2,6},{4,0},{6,2},{1,5},{3,7},{5,1},{7,3},{8,12},{10,14},{12... | collective-permute-start | bytes 393224 | tf_op jit(solution)/shard_map/ppermute | solution.py:38
  14.0 10.2 %collective-permute-start.2 = (bf16[4,128,128]{2,1,0:T(8,128)(2,1)S(1)}, bf16[4,128,128]{2,1,0:T(8,128)(2,1)S(1)}, u32[]{:S(2)}, u32[]{:S(2)}) collective-permute-start(bf16[4,128,128]{2,1,0:T(8,128)(2,1)S(1)} %collective-permute-done.1.refs_0_), channel_id=1, source_target_pairs={{0,16},{16,24},{24,8},{8,0},{1,17},{17,25},{25,9},{9,1},{2,18},{18... | collective-permute-start | bytes 393224 | tf_op jit(solution)/shard_map/ppermute | solution.py:22
  16.4 1.2 %copy-start = (bf16[512,1024]{1,0:T(8,128)(2,1)S(1)}, bf16[512,1024]{1,0:T(8,128)(2,1)}, u32[]{:S(2)}) copy-start(bf16[512,1024]{1,0:T(8,128)(2,1)} %shard_map.55.q_ref) | copy-start | bytes 3145732
  19.7 10.8 %collective-permute-start.7 = (bf16[4,128,128]{2,1,0:T(8,128)(2,1)S(1)}, bf16[4,128,128]{2,1,0:T(8,128)(2,1)S(1)}, u32[]{:S(2)}, u32[]{:S(2)}) collective-permute-start(bf16[4,128,128]{2,1,0:T(8,128)(2,1)S(1)} %collective-permute-done.6.refs_7_.refs_2_), channel_id=1, source_target_pairs={{0,16},{16,24},{24,8},{8,0},{1,17},{17,25},{25,9},{9,1},{2,18},{18... | collective-permute-start | bytes 393224 | tf_op jit(solution)/shard_map/ppermute | solution.py:22
  24.3 6.3 %collective-permute-start.10 = (bf16[4,128,128]{2,1,0:T(8,128)(2,1)S(1)}, bf16[4,128,128]{2,1,0:T(8,128)(2,1)S(1)}, u32[]{:S(2)}, u32[]{:S(2)}) collective-permute-start(bf16[4,128,128]{2,1,0:T(8,128)(2,1)S(1)} %collective-permute-done.6.refs_7_.refs_2_), channel_id=1, source_target_pairs={{0,4},{2,6},{4,0},{6,2},{1,5},{3,7},{5,1},{7,3},{8,12},{10,14},{12... | collective-permute-start | bytes 393224 | tf_op jit(solution)/shard_map/ppermute | solution.py:38
  24.3 11.1 %collective-permute-start.3 = (bf16[4,128,128]{2,1,0:T(8,128)(2,1)S(1)}, bf16[4,128,128]{2,1,0:T(8,128)(2,1)S(1)}, u32[]{:S(2)}, u32[]{:S(2)}) collective-permute-start(bf16[4,128,128]{2,1,0:T(8,128)(2,1)S(1)} %collective-permute-done.2.refs_0_), channel_id=1, source_target_pairs={{0,4},{2,6},{4,0},{6,2},{1,5},{3,7},{5,1},{7,3},{8,12},{10,14},{12... | collective-permute-start | bytes 393224 | tf_op jit(solution)/shard_map/ppermute | solution.py:38
  30.5 4.9 %collective-permute-start.8 = (bf16[4,128,128]{2,1,0:T(8,128)(2,1)S(1)}, bf16[4,128,128]{2,1,0:T(8,128)(2,1)S(1)}, u32[]{:S(2)}, u32[]{:S(2)}) collective-permute-start(bf16[4,128,128]{2,1,0:T(8,128)(2,1)S(1)} %collective-permute-done.7.refs_7_.refs_2_), channel_id=1, source_target_pairs={{0,4},{2,6},{4,0},{6,2},{1,5},{3,7},{5,1},{7,3},{8,12},{10,14},{12... | collective-permute-start | bytes 393224 | tf_op jit(solution)/shard_map/ppermute | solution.py:38
  38.3 9.2 %collective-permute-start.15 = (bf16[256,1024]{1,0:T(8,128)(2,1)S(1)}, bf16[256,1024]{1,0:T(8,128)(2,1)S(1)}, u32[]{:S(2)}, u32[]{:S(2)}) collective-permute-start(bf16[256,1024]{1,0:T(8,128)(2,1)S(1)} %shard_map.61), channel_id=1, source_target_pairs={{0,2},{2,0},{4,6},{6,4},{1,3},{3,1},{5,7},{7,5},{8,10},{10,8},{12,... | collective-permute-start | bytes 1572872 | tf_op jit(solution)/shard_map/ppermute | solution.py:38
  46.7 0.8 copy-start.1
  47.5 0.8 copy-start.3
